TPU v7x, 512 devices: a whole 4x8x8 slice. The times are simulated.
512 devices in a mesh: dp: 32 (over z, x), tensor: 16 (over y, core).
Axes of the slice: x: 4, y: 8, z: 8, core: 2. Of those that a mesh axis runs over, the one named last changes fastest.
Arguments:
- x_in: bfloat16 [8192, 8192], P('dp', 'tensor'), may hold values from -6 to 6
- z_in: bfloat16 [8192, 8192], P('dp', 'tensor'), may hold values from -6 to 6
- bc_in: bfloat16 [8192, 1024], P('dp'), may hold values from -6 to 6
- dt_in: bfloat16 [8192, 128], P('dp', 'tensor'), may hold values from -5 to 5
- lengths: int32 [32, 6], P('dp'), may hold values from 1 to 128, 256 in all within a row
- panel_bin: int32 [512], P('dp'), may hold values from 0 to 31, as said below
- panel_slot: int32 [512], P('dp'), may hold values from 0 to 15, as said below
- conv_x: float32 [4, 8192], P(None, 'tensor'), may hold values from -3 to 3
- conv_bc: float32 [4, 1024], replicated, may hold values from -3 to 3
- dt_bias: float32 [128], P('tensor'), may hold values from -7 to -2
- a_log: float32 [128], P('tensor'), may hold values from 0 to 2.5
- dskip: float32 [128], P('tensor'), may hold values from 0.5 to 1.5
- gain: float32 [8192], P('tensor'), may hold values from 0.5 to 1.5
- w_out: bfloat16 [8192, 4096], P('tensor', 'dp'), may hold values from -0.0625 to 0.0625
- dout: bfloat16 [8192, 4096], P(('dp', 'tensor')), may hold values from -24 to 24
Outputs:
- grad_x: bfloat16 [8192, 8192], P('dp', 'tensor')
- grad_z: bfloat16 [8192, 8192], P('dp', 'tensor')
- grad_bc: bfloat16 [8192, 1024], P('dp', 'tensor')
- grad_dt: bfloat16 [8192, 128], P('dp', 'tensor')
- grad_wout: bfloat16 [8192, 4096], P('tensor', 'dp')
- grad_conv_x: float32 [4, 8192], P(None, 'tensor')
- grad_conv_bc: float32 [4, 1024], P(None, 'tensor')
- grad_gain: float32 [8192], P('tensor')
- grad_heads: float32 [3, 128], P(None, 'tensor')
Inputs may be any that keep to these rules, and one draw needn't show every extreme that they name: `panel_bin`: each device's 16 panels go to bins with exactly 1 of them to each bin they reach, and every bin receives exactly 16 panels. `panel_slot`: the panels dealt to one bin take the positions 0 to 15 once each. Each bin's lengths sum to 256.
All inputs are finite; a program needn't handle non-finite values.
Results may differ from a plain program's by a relative error of at most 0.02.
Values may be sent and summed in bfloat16 or wider, within the bound.
No kernel may reach another device: no remote copies, remote signals or barrier semaphores. Data moves between devices by JAX's collectives and lax.ppermute only.
A program may use at most 128 MiB of HBM per device.

v0:
```python
import math

import jax
import jax.numpy as jnp
from jax import lax
from jax.sharding import PartitionSpec as P

GROUPS = 4
SPAN = 128


highest_precision = lax.Precision.HIGHEST


def partner(block, axis, stride):
    count = lax.axis_size(axis)
    route = []
    for low in range(count):
        high = low | 1 << stride
        if high != low and high < count:
            route += [(low, high), (high, low)]
    return lax.ppermute(block, axis, route)


def segment_ids(lengths_row, total_rows):
    ends = jnp.cumsum(lengths_row)
    positions = jnp.arange(total_rows, dtype=jnp.int32)
    return jnp.sum((positions[:, None] >= ends[None, :]).astype(jnp.int32), axis=1)


def conv_silu(raw, taps, segment):
    width = taps.shape[0]
    total = raw * taps[width - 1][None, :]
    for offset in range(1, width):
        moved = jnp.concatenate(
            [jnp.zeros((offset, raw.shape[1]), raw.dtype), raw[:-offset]], axis=0
        )
        earlier = jnp.concatenate([jnp.full((offset,), -1, jnp.int32), segment[:-offset]], axis=0)
        keep = (earlier == segment).astype(raw.dtype)
        total = total + moved * keep[:, None] * taps[width - 1 - offset][None, :]
    return jax.nn.silu(total)


def ssd_group(values, bmat, cmat, step, rate, skip, segment, block):
    total_rows, heads, head_width = values.shape
    state_width = bmat.shape[1]
    count = total_rows // block
    logdecay = (step * rate[None, :]).reshape(count, block, heads)
    cumulative = jnp.cumsum(logdecay, axis=1)
    seg_blocks = segment.reshape(count, block)
    previous = jnp.concatenate([jnp.full((1,), -1, jnp.int32), seg_blocks[:-1, block - 1]], axis=0)
    lower = jnp.arange(block)[:, None] >= jnp.arange(block)[None, :]

    def advance(state, items):
        xblock, bblock, cblock, sblock, cumblock, segblock, prevseg = items
        same = lower & (segblock[:, None] == segblock[None, :])
        gap = cumblock[:, None, :] - cumblock[None, :, :]
        weights = jnp.where(same[:, :, None], jnp.exp(jnp.minimum(gap, 0.0)), 0.0)
        scores = jnp.dot(cblock, bblock.T, precision=highest_precision)
        mixed = scores[:, :, None] * weights * sblock[None, :, :]
        inner = jnp.einsum("tsh,shp->thp", mixed, xblock, precision=highest_precision)
        carried = (segblock == prevseg).astype(jnp.float32)[:, None] * jnp.exp(cumblock)
        from_state = (
            jnp.einsum("tn,hpn->thp", cblock, state, precision=highest_precision)
            * carried[:, :, None]
        )
        output = inner + from_state + skip[None, :, None] * xblock
        lastseg = segblock[block - 1]
        keep = (segblock == lastseg).astype(jnp.float32)
        toward = jnp.exp(cumblock[block - 1][None, :] - cumblock) * sblock * keep[:, None]
        kept = (lastseg == prevseg).astype(jnp.float32) * jnp.exp(cumblock[block - 1])
        fresh = jnp.einsum("sh,shp,sn->hpn", toward, xblock, bblock, precision=highest_precision)
        return (kept[:, None, None] * state + fresh, output)

    items = (
        values.reshape(count, block, heads, head_width),
        bmat.reshape(count, block, state_width),
        cmat.reshape(count, block, state_width),
        step.reshape(count, block, heads),
        cumulative,
        seg_blocks,
        previous,
    )
    start = jnp.zeros((heads, head_width, state_width), jnp.float32)
    final_state, outputs = lax.scan(advance, start, items)
    return outputs.reshape(total_rows, heads, head_width)


def relay(flat, table):
    return jnp.dot(table, flat, preferred_element_type=jnp.float32).astype(jnp.bfloat16)


def per_device(
    x_in,
    z_in,
    bc_in,
    dt_in,
    lengths,
    panel_bin,
    panel_slot,
    conv_x,
    conv_bc,
    dt_bias,
    a_log,
    dskip,
    gain,
    w_out,
    dout,
):
    dp_size = lax.axis_size("dp")
    tensor_size = lax.axis_size("tensor")
    tensor_index = lax.axis_index("tensor")
    npanels = panel_bin.shape[0]
    total_rows = x_in.shape[0]
    channels = x_in.shape[1]
    heads_here = dt_in.shape[1]
    head_width = channels // heads_here
    bc_width = bc_in.shape[1]
    pair_width = bc_width // GROUPS
    state_width = pair_width // 2
    share_width = bc_width // tensor_size
    devices_per_group = tensor_size // GROUPS
    group_index = tensor_index // devices_per_group
    local_rank = tensor_index % devices_per_group
    bit_count = devices_per_group.bit_length() - 1
    capacity = max(1, npanels // dp_size)
    scale = 1.0 / math.sqrt(total_rows * dp_size)
    segment = segment_ids(lengths[0], total_rows)
    order_index = jnp.arange(npanels, dtype=jnp.int32)
    same_bin = (panel_bin[None, :] == panel_bin[:, None]) & (
        order_index[None, :] < order_index[:, None]
    )
    rank = jnp.sum(same_bin.astype(jnp.int32), axis=1)
    send_slot = panel_bin * capacity + rank
    route = (send_slot[None, :] == jnp.arange(dp_size * capacity, dtype=jnp.int32)[:, None]).astype(
        jnp.bfloat16
    )
    label = jnp.dot(
        route, (panel_slot + 1).astype(jnp.bfloat16)[:, None], preferred_element_type=jnp.float32
    ).astype(jnp.bfloat16)
    dealt = (
        lax.all_to_all(
            relay(x_in.reshape(npanels, -1), route), "dp", split_axis=0, concat_axis=0, tiled=True
        ),
        lax.all_to_all(
            relay(z_in.reshape(npanels, -1), route), "dp", split_axis=0, concat_axis=0, tiled=True
        ),
        lax.all_to_all(
            relay(bc_in.reshape(npanels, -1), route), "dp", split_axis=0, concat_axis=0, tiled=True
        ),
        lax.all_to_all(
            relay(dt_in.reshape(npanels, -1), route), "dp", split_axis=0, concat_axis=0, tiled=True
        ),
        lax.all_to_all(label, "dp", split_axis=0, concat_axis=0, tiled=True),
    )
    placing = (
        dealt[4][:, 0].astype(jnp.float32)[None, :]
        == jnp.arange(1, npanels + 1, dtype=jnp.float32)[:, None]
    ).astype(jnp.bfloat16)
    x_bin = relay(dealt[0], placing).reshape(total_rows, channels)
    z_bin = relay(dealt[1], placing).reshape(total_rows, channels)
    bc_part = relay(dealt[2], placing).reshape(total_rows, -1)
    dt_bin = relay(dealt[3], placing).reshape(total_rows, heads_here)
    raw_share = lax.dynamic_slice_in_dim(bc_part, tensor_index * share_width, share_width, 1)
    own_raw = lax.dynamic_slice_in_dim(bc_part, group_index * pair_width, pair_width, 1).astype(
        jnp.float32
    )
    conv_own = lax.dynamic_slice_in_dim(conv_bc, group_index * pair_width, pair_width, 1)
    bc_active = conv_silu(own_raw, conv_own, segment)

    def local_forward(xraw, active, dtraw, taps, bias, decay_log, skip):
        values = conv_silu(xraw, taps, segment).reshape(total_rows, heads_here, head_width)
        step = jax.nn.softplus(dtraw + bias[None, :])
        output = ssd_group(
            values,
            active[:, :state_width],
            active[:, state_width:],
            step,
            -jnp.exp(decay_log),
            skip,
            segment,
            SPAN,
        )
        return output.reshape(total_rows, channels)

    mixed, pull = jax.vjp(
        local_forward,
        x_bin.astype(jnp.float32),
        bc_active,
        dt_bin.astype(jnp.float32),
        conv_x,
        dt_bias,
        a_log,
        dskip,
    )
    z_float = z_bin.astype(jnp.float32)
    z_sigmoid = jax.nn.sigmoid(z_float)
    z_silu = z_float * z_sigmoid
    gated = mixed * z_silu
    group_size = channels * devices_per_group
    picker = (jnp.arange(GROUPS, dtype=jnp.int32) == group_index).astype(jnp.float32)
    squares = lax.psum(jnp.sum(gated * gated, axis=1)[:, None] * picker[None, :], "tensor")
    inverse = lax.rsqrt(jnp.sum(squares * picker[None, :], axis=1) / group_size + 1e-05)
    normed_b = (gated * inverse[:, None] * gain[None, :]).astype(jnp.bfloat16)
    full_out = lax.all_gather(dout, "tensor", axis=0, tiled=True)
    columns = full_out
    dnormed = lax.dot_general(
        columns,
        lax.all_gather(w_out, "dp", axis=1, tiled=True),
        (((1,), (1,)), ((), ())),
        preferred_element_type=jnp.float32,
    )
    columns = full_out
    weight_share = lax.psum_scatter(
        (
            lax.dot_general(
                columns, normed_b, (((0,), (0,)), ((), ())), preferred_element_type=jnp.float32
            )
            * scale
        ).astype(jnp.bfloat16),
        "dp",
        scatter_dimension=0,
        tiled=True,
    ).astype(jnp.float32)
    grad_gain_part = jnp.sum(dnormed * gated * inverse[:, None], axis=0)
    weighted = dnormed * gain[None, :]
    crossing = lax.psum(jnp.sum(weighted * gated, axis=1)[:, None] * picker[None, :], "tensor")
    cross_sum = jnp.sum(crossing * picker[None, :], axis=1)
    dgated = inverse[:, None] * weighted - gated * (inverse**3 * cross_sum / group_size)[:, None]
    dmixed = dgated * z_silu
    dz_raw = dgated * mixed * z_sigmoid * (1.0 + z_float * (1.0 - z_sigmoid))
    grad_xr, grad_active, grad_dtr, grad_cx, grad_bias, grad_alog, grad_skip = pull(dmixed)
    partial_sum = grad_active
    for bit_number in range(bit_count):
        partial_sum = partial_sum + partner(
            partial_sum.astype(jnp.bfloat16), "tensor", bit_number
        ).astype(partial_sum.dtype)
    dshare = lax.dynamic_slice_in_dim(partial_sum, local_rank * share_width, share_width, 1)
    conv_share = lax.dynamic_slice_in_dim(conv_bc, tensor_index * share_width, share_width, 1)

    def share_act(raw, taps):
        return conv_silu(raw, taps, segment)

    share_out, share_pull = jax.vjp(share_act, raw_share.astype(jnp.float32), conv_share)
    grad_bc_share, grad_cbc_share = share_pull(dshare)
    summed_params = lax.psum(
        (grad_cx, grad_cbc_share, grad_gain_part, jnp.stack([grad_bias, grad_alog, grad_skip])),
        "dp",
    )
    back_table = placing.T
    returned = (
        lax.all_to_all(
            relay(grad_xr.astype(jnp.bfloat16).reshape(npanels, -1), back_table),
            "dp",
            split_axis=0,
            concat_axis=0,
            tiled=True,
        ),
        lax.all_to_all(
            relay(dz_raw.astype(jnp.bfloat16).reshape(npanels, -1), back_table),
            "dp",
            split_axis=0,
            concat_axis=0,
            tiled=True,
        ),
        lax.all_to_all(
            relay(grad_bc_share.astype(jnp.bfloat16).reshape(npanels, -1), back_table),
            "dp",
            split_axis=0,
            concat_axis=0,
            tiled=True,
        ),
        lax.all_to_all(
            relay(grad_dtr.astype(jnp.bfloat16).reshape(npanels, -1), back_table),
            "dp",
            split_axis=0,
            concat_axis=0,
            tiled=True,
        ),
    )
    home_table = route.T
    grad_x = relay(returned[0], home_table).reshape(total_rows, channels)
    grad_z = relay(returned[1], home_table).reshape(total_rows, channels)
    grad_bc = relay(returned[2], home_table).reshape(total_rows, share_width)
    grad_dt = relay(returned[3], home_table).reshape(total_rows, heads_here)
    grad_wout = weight_share.T.astype(jnp.bfloat16)
    return (
        grad_x,
        grad_z,
        grad_bc,
        grad_dt,
        grad_wout,
        summed_params[0] * scale,
        summed_params[1] * scale,
        summed_params[2] * scale,
        summed_params[3] * scale,
    )


def solution(mesh):
    placed = (
        P("dp", "tensor"),
        P("dp", "tensor"),
        P("dp", None),
        P("dp", "tensor"),
        P("dp", None),
        P("dp"),
        P("dp"),
        P(None, "tensor"),
        P(),
        P("tensor"),
        P("tensor"),
        P("tensor"),
        P("tensor"),
        P("tensor", "dp"),
        P(("dp", "tensor"), None),
    )
    return jax.shard_map(
        per_device,
        mesh=mesh,
        in_specs=placed,
        out_specs=(
            P("dp", "tensor"),
            P("dp", "tensor"),
            P("dp", "tensor"),
            P("dp", "tensor"),
            P("tensor", "dp"),
            P(None, "tensor"),
            P(None, "tensor"),
            P("tensor"),
            P(None, "tensor"),
        ),
        check_vma=False,
    )
```

profile of v0, /device:TPU:40, one launch (start us, length us, event | category | flops | bytes accessed | tf_op | source)
XLA Modules:
  0.0 547.1 jit_solution(11335631472859787619)
XLA Ops:
  11.0 13.2 %all-to-all-start = ((bf16[32,1,1]{2,1,0:T(2,128)(2,1)}), bf16[32,1,1]{2,1,0:T(2,128)(2,1)S(1)}, u32[]{:S(2)}, u32[]{:S(2)}) async-start(bf16[32,1,1]{2,1,0:T(2,128)(2,1)} %copy.260), calls=%async_computation | async-start | bytes 32768 | tf_op jit(solution)/shard_map/all_to_all | solution.py:154
  26.9 6.9 %all-to-all-done = bf16[32,1,1]{2,1,0:T(2,128)(2,1)S(1)} async-done(((bf16[32,1,1]{2,1,0:T(2,128)(2,1)}), bf16[32,1,1]{2,1,0:T(2,128)(2,1)S(1)}, u32[]{:S(2)}, u32[]{:S(2)}) %all-to-all-start) | async-done | bytes 96 | tf_op jit(solution)/shard_map/all_to_all | solution.py:154
  33.8 3.8 all-to-all-start.1
  40.7 6.6 %all-to-all-done.1 = bf16[32,1,128]{2,1,0:T(2,128)(2,1)S(1)} async-done(((bf16[32,1,128]{2,1,0:T(2,128)(2,1)}), bf16[32,1,128]{2,1,0:T(2,128)(2,1)S(1)}, u32[]{:S(2)}, u32[]{:S(2)}) %all-to-all-start.1) | async-done | bytes 8224 | tf_op jit(solution)/shard_map/all_to_all | solution.py:151
  47.3 3.9 all-to-all-start.2
  54.8 12.2 %all-to-all-done.2 = bf16[32,2,4096]{2,1,0:T(2,128)(2,1)S(1)} async-done(((bf16[32,2,4096]{2,1,0:T(2,128)(2,1)}), bf16[32,2,4096]{2,1,0:T(2,128)(2,1)S(1)}, u32[]{:S(2)}, u32[]{:S(2)}) %all-to-all-start.2) | async-done | bytes 524320 | tf_op jit(solution)/shard_map/all_to_all | solution.py:142
  67.9 4.2 all-to-all-start.4
  80.9 7.8 %all-to-all-done.4 = bf16[32,2,4096]{2,1,0:T(2,128)(2,1)S(1)} async-done(((bf16[32,2,4096]{2,1,0:T(2,128)(2,1)}), bf16[32,2,4096]{2,1,0:T(2,128)(2,1)S(1)}, u32[]{:S(2)}, u32[]{:S(2)}) %all-to-all-start.4) | async-done | bytes 524320 | tf_op jit(solution)/shard_map/all_to_all | solution.py:145
  88.7 4.7 all-to-all-start.3
  116.9 2.4 copy.275
  119.2 5.8 %reshape.691 = bf16[32,1,16384]{2,1,0:T(2,128)(2,1)} reshape(bf16[32,2,8192]{2,1,0:T(2,128)(2,1)} %all-to-all-done.3) | data formatting | bytes 2097152
  125.0 3.6 convolution_convert_fusion.1
  137.3 51.1 %while.83 = (s32[]{:T(128)}, f32[8,64,128]{2,1,0:T(8,128)S(1)}, f32[2,128,8,64]{1,3,2,0:T(8,128)}, f32[2,128,128,8]{2,3,1,0:T(8,128)}, f32[2,128,128,8]{2,3,1,0:...) while((s32[]{:T(128)}, f32[8,64,128]{2,1,0:T(8,128)S(1)}, ...), condition=%wide.region_5.6_spmd.clone, body=%wide.region_4.5_spmd.clone.sunk | while | flops 329769984 | bytes 11861835 | solution.py:85
  148.1 2.3 fusion.284
  151.6 2.7 fusion.283
  177.2 2.7 fusion.283
  188.4 2.8 copy.318
  194.9 21.6 %psum.42 = f32[256,4]{0,1:T(4,128)S(1)} all-reduce(f32[256,4]{0,1:T(4,128)S(1)} %broadcast_multiply_fusion.4), channel_id=1, replica_groups=mesh['dp'=32,'tensor'=16] {'tensor'}, use_global_device_ids=true, to_apply=%region_7.8 | all-reduce | flops 1024 | bytes 8192 | tf_op jit(solution)/shard_map/psum | solution.py:202
  218.2 5.3 fusion.138
  223.5 6.5 %copy.314 = bf16[4096,512]{1,0:T(8,128)(2,1)} copy(bf16[4096,512]{0,1:T(8,128)(2,1)} %fusion.138) | data formatting | bytes 8388608
  231.2 5.6 %multiply_reduce_fusion.1 = (f32[512]{0:T(512)}, f32[256]{0:T(256)S(1)}, f32[256,512]{1,0:T(8,128)}) fusion(f32[256]{0:T(256)S(1)} %add_rsqrt_fusion, f32[256,512]{1,0:T(8,128)S(1)} %copy-done.18, f32[256,512]{1,0:T(8,128)S(1)} %copy-done.19, f32[512]{0:T(512)S(1)} %copy-done.88, bf16[256,4096]{1,0:T(8,128)(2,1)} %all-gather.3.cloned.1.call-done, ...), kind=kOutput, calls=%fused_computation.258 | convolution fusion | flops 1075182848 | bytes 7870464 | tf_op jit(solution)/shard_map/dot_general | solution.py:207
  236.9 23.5 %psum.43 = f32[256,4]{0,1:T(4,128)S(1)} all-reduce(f32[256,4]{0,1:T(4,128)S(1)} %broadcast_multiply_fusion.3), channel_id=1, replica_groups=mesh['dp'=32,'tensor'=16] {'tensor'}, use_global_device_ids=true, to_apply=%region_10.11 | all-reduce | flops 1024 | bytes 8192 | tf_op jit(solution)/shard_map/psum | solution.py:227
  269.5 41.7 %while.84 = (s32[]{:T(128)}, f32[8]{0:T(128)S(1)}, f32[8,64,128]{2,1,0:T(8,128)S(1)}, f32[2,128,8,64]{1,3,2,0:T(8,128)}, f32[2,128,128]{2,1,0:T(8,128)}, /*index...) while((s32[]{:T(128)}, f32[8]{0:T(128)S(1)}, ...), condition=%wide.region_21.22_spmd.clone, body=%wide.region_12.21_spmd.clone.sunk | while | flops 657091584 | bytes 32515672 | solution.py:85
  320.6 10.1 %all-to-all-start.8 = ((bf16[32,1,128]{2,1,0:T(2,128)(2,1)}), bf16[32,1,128]{2,1,0:T(2,128)(2,1)S(1)}, u32[]{:S(2)}, u32[]{:S(2)}) async-start(bf16[32,1,128]{2,1,0:T(2,128)(2,1)} %copy.301), calls=%async_computation.8 | async-start | bytes 32768 | tf_op jit(solution)/shard_map/all_to_all | solution.py:273
  333.5 5.8 %collective-permute-start.1 = (bf16[256,256]{1,0:T(8,128)(2,1)S(1)}, bf16[256,256]{1,0:T(8,128)(2,1)S(1)}, u32[]{:S(2)}, u32[]{:S(2)}) collective-permute-start(bf16[256,256]{1,0:T(8,128)(2,1)S(1)} %get-tuple-element.1918), channel_id=1, source_target_pairs={{0,2},{2,0},{1,3},{3,1},{4,6},{6,4},{5,7},{7,5},{8,10},{10,8},{9,1... | collective-permute-start | bytes 393224 | tf_op jit(solution)/shard_map/ppermute | solution.py:22
  339.3 3.8 collective-permute-done.1
  346.4 9.5 %all-to-all-start.7 = ((bf16[32,2,512]{2,1,0:T(2,128)(2,1)}), bf16[32,2,512]{2,1,0:T(2,128)(2,1)S(1)}, u32[]{:S(2)}, u32[]{:S(2)}) async-start(bf16[32,2,512]{2,1,0:T(2,128)(2,1)} %reshape.698), calls=%async_computation.7 | async-start | bytes 131072 | tf_op jit(solution)/shard_map/all_to_all | solution.py:266
  359.2 6.7 %all-to-all-done.7 = bf16[32,2,512]{2,1,0:T(2,128)(2,1)S(1)} async-done(((bf16[32,2,512]{2,1,0:T(2,128)(2,1)}), bf16[32,2,512]{2,1,0:T(2,128)(2,1)S(1)}, u32[]{:S(2)}, u32[]{:S(2)}) %all-to-all-start.7) | async-done | bytes 65568 | tf_op jit(solution)/shard_map/all_to_all | solution.py:266
  365.8 3.9 all-to-all-start.5
  373.2 143.1 %all-reduce.29 = (f32[4,512]{1,0:T(4,128)S(1)}, f32[4,64]{1,0:T(4,128)S(1)}, f32[512]{0:T(512)S(1)}, f32[3,8]{1,0:T(4,128)S(1)}) all-reduce(f32[4,512]{1,0:T(4,128)S(1)} %pad_add_fusion.1, f32[4,64]{1,0:T(4,128)S(1)} %pad_add_fusion.2, f32[512]{0:T(512)S(1)} %copy-done.90, ...), channel_id=1, replica_groups=mesh['dp'=32,'tensor'=16] {'dp'}, use_global_device_ids=true, to_apply=%region_28.29 | all-reduce | flops 2840 | bytes 22720 | tf_op jit(solution)/shard_map/psum | solution.py:246
  516.8 6.0 %all-to-all-start.6 = ((bf16[32,2,4096]{2,1,0:T(2,128)(2,1)}), bf16[32,2,4096]{2,1,0:T(2,128)(2,1)S(1)}, u32[]{:S(2)}, u32[]{:S(2)}) async-start(bf16[32,2,4096]{2,1,0:T(2,128)(2,1)} %reshape.696), calls=%async_computation.6 | async-start | bytes 1048576 | tf_op jit(solution)/shard_map/all_to_all | solution.py:259
  527.7 9.0 %all-to-all-done.6 = bf16[32,2,4096]{2,1,0:T(2,128)(2,1)S(1)} async-done(((bf16[32,2,4096]{2,1,0:T(2,128)(2,1)}), bf16[32,2,4096]{2,1,0:T(2,128)(2,1)S(1)}, u32[]{:S(2)}, u32[]{:S(2)}) %all-to-all-start.6) | async-done | bytes 524320 | tf_op jit(solution)/shard_map/all_to_all | solution.py:259
  (555 shorter events, 182.6 us)
Async XLA Ops:
  7.2 211.0 %all-gather.3.cloned.1.call-start = ((), (), s32[]{:S(2)}) async-start(), calls=%async_computation.10 | async-start | bytes 2228224 | tf_op jit(solution)/shard_map/all_gather | solution.py:205
  9.5 62.6 %copy-start.55 = (s32[16]{0:T(128)}, s32[16]{0:T(128)S(1)}, u32[]{:S(2)}) copy-start(s32[16]{0:T(128)S(1)} %add.236) | copy-start | bytes 196
  11.0 22.8 %all-to-all-start = ((bf16[32,1,1]{2,1,0:T(2,128)(2,1)}), bf16[32,1,1]{2,1,0:T(2,128)(2,1)S(1)}, u32[]{:S(2)}, u32[]{:S(2)}) async-start(bf16[32,1,1]{2,1,0:T(2,128)(2,1)} %copy.260), calls=%async_computation | async-start | bytes 32768 | tf_op jit(solution)/shard_map/all_to_all | solution.py:154
  26.3 25.7 %copy-start.25 = (bf16[256,1024]{1,0:T(8,128)(2,1)S(1)}, bf16[256,1024]{1,0:T(8,128)(2,1)}, u32[]{:S(2)}) copy-start(bf16[256,1024]{1,0:T(8,128)(2,1)} %param.21) | copy-start | bytes 1572868
  33.8 13.5 %all-to-all-start.1 = ((bf16[32,1,128]{2,1,0:T(2,128)(2,1)}), bf16[32,1,128]{2,1,0:T(2,128)(2,1)S(1)}, u32[]{:S(2)}, u32[]{:S(2)}) async-start(bf16[32,1,128]{2,1,0:T(2,128)(2,1)} %copy.262), calls=%async_computation.1 | async-start | bytes 32768 | tf_op jit(solution)/shard_map/all_to_all | solution.py:151
  38.5 13.7 %copy-start.32 = (bf16[256,512]{1,0:T(8,128)(2,1)S(1)}, bf16[256,512]{1,0:T(8,128)(2,1)}, u32[]{:S(2)}) copy-start(bf16[256,512]{1,0:T(8,128)(2,1)} %param.20) | copy-start | bytes 786436
  47.3 19.7 %all-to-all-start.2 = ((bf16[32,2,4096]{2,1,0:T(2,128)(2,1)}), bf16[32,2,4096]{2,1,0:T(2,128)(2,1)S(1)}, u32[]{:S(2)}, u32[]{:S(2)}) async-start(bf16[32,2,4096]{2,1,0:T(2,128)(2,1)} %reshape.688), calls=%async_computation.2 | async-start | bytes 1048576 | tf_op jit(solution)/shard_map/all_to_all | solution.py:142
  51.2 178.9 %all-gather.5.cloned.1.call-start = ((), (), s32[]{:S(2)}) async-start(), calls=%async_computation.11 | async-start | bytes 4325376 | tf_op jit(solution)/shard_map/all_gather | solution.py:209
  67.9 20.9 %all-to-all-start.4 = ((bf16[32,2,4096]{2,1,0:T(2,128)(2,1)}), bf16[32,2,4096]{2,1,0:T(2,128)(2,1)S(1)}, u32[]{:S(2)}, u32[]{:S(2)}) async-start(bf16[32,2,4096]{2,1,0:T(2,128)(2,1)} %reshape.692), calls=%async_computation.4 | async-start | bytes 1048576 | tf_op jit(solution)/shard_map/all_to_all | solution.py:145
  74.0 22.0 %copy-start.89 = (f32[8]{0:T(128)S(1)}, f32[8]{0:T(128)}, u32[]{:S(2)}) copy-start(f32[8]{0:T(128)} %param.28) | copy-start | bytes 100
  74.0 25.2 %copy-start.80 = (f32[4,512]{1,0:T(4,128)S(1)}, f32[4,512]{1,0:T(4,128)}, u32[]{:S(2)}) copy-start(f32[4,512]{1,0:T(4,128)} %param.26) | copy-start | bytes 24580
  77.7 47.3 %copy-start.60 = (f32[16]{0:T(128)}, f32[16]{0:T(128)S(1)}, u32[]{:S(2)}) copy-start(f32[16]{0:T(128)S(1)} %iota_add_fusion) | copy-start | bytes 196
  80.0 24.7 %copy-start.82 = (f32[8]{0:T(128)}, f32[8]{0:T(128)S(1)}, u32[]{:S(2)}) copy-start(f32[8]{0:T(128)S(1)} %exponential_negate_fusion) | copy-start | bytes 100
  80.9 50.8 %copy-start.46 = (f32[256]{0:T(256)}, f32[256]{0:T(256)S(1)}, u32[]{:S(2)}) copy-start(f32[256]{0:T(256)S(1)} %get-tuple-element.1960) | copy-start | bytes 3076
  80.9 50.8 %copy-start.48 = (f32[256]{0:T(256)}, f32[256]{0:T(256)S(1)}, u32[]{:S(2)}) copy-start(f32[256]{0:T(256)S(1)} %get-tuple-element.1961) | copy-start | bytes 3076
  80.9 50.8 %copy-start.50 = (f32[256]{0:T(256)}, f32[256]{0:T(256)S(1)}, u32[]{:S(2)}) copy-start(f32[256]{0:T(256)S(1)} %get-tuple-element.1962) | copy-start | bytes 3076
  88.7 30.5 %all-to-all-start.3 = ((bf16[32,2,8192]{2,1,0:T(2,128)(2,1)}), bf16[32,2,8192]{2,1,0:T(2,128)(2,1)}, u32[]{:S(2)}, u32[]{:S(2)}) async-start(bf16[32,2,8192]{2,1,0:T(2,128)(2,1)} %reshape.690), calls=%async_computation.3 | async-start | bytes 2097152 | tf_op jit(solution)/shard_map/all_to_all | solution.py:148
  93.4 445.3 %reduce-scatter.4.cloned.1.call-start = ((), (), s32[]{:S(2)}) async-start(), calls=%async_computation.12 | async-start | bytes 4325376
  99.6 25.4 %copy-start.57 = (f32[32]{0:T(128)}, f32[32]{0:T(128)S(1)}, u32[]{:S(2)}) copy-start(f32[32]{0:T(128)S(1)} %convert_reduce_fusion) | copy-start | bytes 388
  188.4 29.8 %copy-start.88 = (f32[512]{0:T(512)S(1)}, f32[512]{0:T(512)}, u32[]{:S(2)}) copy-start(f32[512]{0:T(512)} %param.31) | copy-start | bytes 6148
  312.1 18.6 %copy-start.20 = (f32[256,512]{1,0:T(8,128)S(1)}, f32[256,512]{1,0:T(8,128)}, u32[]{:S(2)}) copy-start(f32[256,512]{1,0:T(8,128)} %get-tuple-element.1921) | copy-start | bytes 1572868
  312.1 18.6 %copy-start.47 = (f32[256]{0:T(256)S(1)}, f32[256]{0:T(256)}, u32[]{:S(2)}) copy-start(f32[256]{0:T(256)} %copy-done.46) | copy-start | bytes 3076
  312.1 18.6 %copy-start.49 = (f32[256]{0:T(256)S(1)}, f32[256]{0:T(256)}, u32[]{:S(2)}) copy-start(f32[256]{0:T(256)} %copy-done.48) | copy-start | bytes 3076
  312.1 18.6 %copy-start.51 = (f32[256]{0:T(256)S(1)}, f32[256]{0:T(256)}, u32[]{:S(2)}) copy-start(f32[256]{0:T(256)} %copy-done.50) | copy-start | bytes 3076
  313.2 19.2 %collective-permute-start = (bf16[256,256]{1,0:T(8,128)(2,1)S(1)}, bf16[256,256]{1,0:T(8,128)(2,1)}, u32[]{:S(2)}, u32[]{:S(2)}) collective-permute-start(bf16[256,256]{1,0:T(8,128)(2,1)S(1)} %fusion.165), channel_id=1, source_target_pairs={{0,1},{1,0},{2,3},{3,2},{4,5},{5,4},{6,7},{7,6},{8,9},{9,8},{10,11... | collective-permute-start | bytes 393224 | tf_op jit(solution)/shard_map/ppermute | solution.py:22
  320.6 25.8 %all-to-all-start.8 = ((bf16[32,1,128]{2,1,0:T(2,128)(2,1)}), bf16[32,1,128]{2,1,0:T(2,128)(2,1)S(1)}, u32[]{:S(2)}, u32[]{:S(2)}) async-start(bf16[32,1,128]{2,1,0:T(2,128)(2,1)} %copy.301), calls=%async_computation.8 | async-start | bytes 32768 | tf_op jit(solution)/shard_map/all_to_all | solution.py:273
  333.5 9.6 %collective-permute-start.1 = (bf16[256,256]{1,0:T(8,128)(2,1)S(1)}, bf16[256,256]{1,0:T(8,128)(2,1)S(1)}, u32[]{:S(2)}, u32[]{:S(2)}) collective-permute-start(bf16[256,256]{1,0:T(8,128)(2,1)S(1)} %get-tuple-element.1918), channel_id=1, source_target_pairs={{0,2},{2,0},{1,3},{3,1},{4,6},{6,4},{5,7},{7,5},{8,10},{10,8},{9,1... | collective-permute-start | bytes 393224 | tf_op jit(solution)/shard_map/ppermute | solution.py:22
  344.6 14.0 %copy-start.23 = (bf16[256,512]{1,0:T(8,128)(2,1)S(1)}, bf16[256,512]{1,0:T(8,128)(2,1)}, u32[]{:S(2)}) copy-start(bf16[256,512]{1,0:T(8,128)(2,1)} %get-tuple-element.1941) | copy-start | bytes 786436
  346.4 19.4 %all-to-all-start.7 = ((bf16[32,2,512]{2,1,0:T(2,128)(2,1)}), bf16[32,2,512]{2,1,0:T(2,128)(2,1)S(1)}, u32[]{:S(2)}, u32[]{:S(2)}) async-start(bf16[32,2,512]{2,1,0:T(2,128)(2,1)} %reshape.698), calls=%async_computation.7 | async-start | bytes 131072 | tf_op jit(solution)/shard_map/all_to_all | solution.py:266
  358.8 14.4 %copy-start.90 = (f32[512]{0:T(512)S(1)}, f32[512]{0:T(512)}, u32[]{:S(2)}) copy-start(f32[512]{0:T(512)} %get-tuple-element.1758) | copy-start | bytes 6148
  365.8 150.9 %all-to-all-start.5 = ((bf16[32,2,4096]{2,1,0:T(2,128)(2,1)}), bf16[32,2,4096]{2,1,0:T(2,128)(2,1)S(1)}, u32[]{:S(2)}, u32[]{:S(2)}) async-start(bf16[32,2,4096]{2,1,0:T(2,128)(2,1)} %reshape.694), calls=%async_computation.5 | async-start | bytes 1048576 | tf_op jit(solution)/shard_map/all_to_all | solution.py:252
  516.8 19.9 %all-to-all-start.6 = ((bf16[32,2,4096]{2,1,0:T(2,128)(2,1)}), bf16[32,2,4096]{2,1,0:T(2,128)(2,1)S(1)}, u32[]{:S(2)}, u32[]{:S(2)}) async-start(bf16[32,2,4096]{2,1,0:T(2,128)(2,1)} %reshape.696), calls=%async_computation.6 | async-start | bytes 1048576 | tf_op jit(solution)/shard_map/all_to_all | solution.py:259
  (114 other events, 665.2 us)
Sparse Core Ops, SparseCore 0:
  10.1 44.5 all-gather.2
  57.8 99.4 all-gather.4
  230.2 230.6 reduce-scatter.3
where the time goes:
time: 556 us; the launch traced here: 547 us
  blocking collectives  188 us (34%)
  local copies, waits for them, and re-layouts  111 us (20%)
  starting transfers between devices  67.8 us (12%)
  other arithmetic  56.9 us (10%)
  waiting for transfers between devices  54.4 us (10%)
  matrix products  50.3 us (9%)
  between operations  15.3 us (3%)
    psum x1, blocking collectives, per_device(): lax.psum((grad_cx, grad_cbc_share, grad_gain_part, jnp.stack([grad_bias,...  143 us
    unnamed x161, local copies, waits for them, and re-layouts  34.9 us
    psum x1, blocking collectives, per_device(): lax.psum(jnp.sum(weighted * gated, axis=1)[:, None] * picker[None, :], 't...  23.5 us
    psum x1, blocking collectives, per_device(): lax.psum(jnp.sum(gated * gated, axis=1)[:, None] * picker[None, :], 'tens...  21.6 us
    dynamic_update_slice x16, other arithmetic, ssd_group(): final_state, outputs = lax.scan(advance, start, items)  16.2 us
    dynamic_slice x20, local copies, waits for them, and re-layouts, ssd_group(): final_state, outputs = lax.scan(advance, start, items)  14.1 us
    all_to_all x1, starting transfers between devices, per_device(): lax.all_to_all(label, 'dp', split_axis=0, concat_axis=0, tiled=True)  13.2 us
    all_to_all x1, waiting for transfers between devices, per_device(): lax.all_to_all(relay(x_in.reshape(npanels, -1), route), 'dp', split_axis=...  12.2 us
  transfers between devices with their start and end apart: 14, of which 7 were waited for; matrix products, arithmetic and copies ran while one was open for 38% of the time, Pallas kernels for 0%

commit v1 on v0

v1 whole, which is shorter than its diff:
```python
import functools
import math

import jax
import jax.numpy as jnp
from jax import lax
from jax.experimental import pallas as pl
from jax.experimental.pallas import tpu as pltpu
from jax.sharding import PartitionSpec as P

GROUPS = 4
DP_INNER = 4
PANEL = 16
LANES = 128
FAR = -1e30

exact = lax.Precision.HIGHEST
f32 = jnp.float32
bf16 = jnp.bfloat16
smem = pl.BlockSpec(memory_space=pltpu.SMEM)
vmem = pl.BlockSpec(memory_space=pltpu.VMEM)


def call(body, outs, ins, scalars=0, cost=1, scratch=(), name=None):
    size = sum(math.prod(o.shape) * o.dtype.itemsize for o in outs)
    size += sum(math.prod(i.shape) * i.dtype.itemsize for i in ins)
    return pl.pallas_call(
        body,
        out_shape=outs,
        in_specs=[smem] * scalars + [vmem] * (len(ins) - scalars),
        out_specs=[vmem] * len(outs),
        scratch_shapes=list(scratch),
        compiler_params=pltpu.CompilerParams(vmem_limit_bytes=48 << 20),
        cost_estimate=pl.CostEstimate(
            flops=int(cost * 1e6), bytes_accessed=size, transcendentals=0
        ),
        name=name,
    )(*ins)


def shaped(shape, dtype):
    return jax.ShapeDtypeStruct(shape, dtype)


def dot_tn(a, b, precision=None):
    return lax.dot_general(
        a, b, (((0,), (0,)), ((), ())), precision=precision, preferred_element_type=f32
    )


def dot_nt(a, b, precision=None):
    return lax.dot_general(
        a, b, (((1,), (1,)), ((), ())), precision=precision, preferred_element_type=f32
    )


def dot_nn(a, b, precision=None):
    return lax.dot_general(
        a, b, (((1,), (0,)), ((), ())), precision=precision, preferred_element_type=f32
    )


def row_ids(shape):
    return lax.broadcasted_iota(jnp.int32, shape, 0)


def lane_ids(shape):
    return lax.broadcasted_iota(jnp.int32, shape, 1)


def starts_of(len_ref, shape):
    rows = row_ids(shape)
    start = jnp.zeros(shape, jnp.int32)
    end = jnp.int32(0)
    for k in range(len_ref.shape[1]):
        end = end + len_ref[0, k]
        start = jnp.where(rows >= end, end, start)
    return start


def seen_mask(len_ref, rows):
    shape = (rows, rows)
    lanes = lane_ids(shape)
    return (lanes <= row_ids(shape)) & (lanes >= starts_of(len_ref, shape))


def keep_masks(len_ref, rows, taps):
    shape = (rows, LANES)
    place = row_ids(shape) - starts_of(len_ref, shape)
    return [None] + [(place >= o).astype(f32)[:, :1] for o in range(1, taps)]


def conv(raw, taps, keeps):
    width = len(keeps)
    total = raw * taps[width - 1 : width]
    for o in range(1, width):
        total = total + pltpu.roll(raw, o, 0) * keeps[o] * taps[width - 1 - o : width - o]
    return total


def conv_back(dpre, raw, taps, keeps):
    width = len(keeps)
    rows = raw.shape[0]
    draw = dpre * taps[width - 1 : width]
    dtaps = {width - 1: jnp.sum(dpre * raw, axis=0, keepdims=True)}
    for o in range(1, width):
        kept = dpre * keeps[o]
        draw = draw + pltpu.roll(kept, rows - o, 0) * taps[width - 1 - o : width - o]
        dtaps[width - 1 - o] = jnp.sum(kept * pltpu.roll(raw, o, 0), axis=0, keepdims=True)
    return draw, [dtaps[k] for k in range(width)]


def head_table(channels, head_width):
    shape = (channels, LANES)
    return (row_ids(shape) // head_width == lane_ids(shape)).astype(f32)


def head_spread(channels, head_width):
    shape = (LANES, channels)
    return (lane_ids(shape) // head_width == row_ids(shape)).astype(f32)


def pack_dout_body(co_ref, dout_ref, *d_refs):
    inner = len(d_refs)
    outer = dout_ref.shape[1] // (LANES * inner)
    for k in range(inner):
        block = lax.rem(co_ref[1] + k, inner)
        for z in range(outer):
            low = pl.multiple_of((z * inner + block) * LANES, LANES)
            d_refs[k][:, z * LANES : (z + 1) * LANES] = dout_ref[:, pl.ds(low, LANES)]


def pack_body(bin_ref, slot_ref, co_ref, x_ref, z_ref, bc_ref, dt_ref, a_ref, zs_ref):
    npan = bin_ref.shape[0]
    channels = x_ref.shape[1]
    pair = bc_ref.shape[1] // GROUPS
    heads = dt_ref.shape[1]
    a_ref[...] = jnp.zeros_like(a_ref)
    zs_ref[...] = jnp.zeros_like(zs_ref)
    group = pl.multiple_of(co_ref[0] * pair, pair)
    shape = (PANEL, LANES)
    for p in range(npan):
        rows = slice(p * PANEL, (p + 1) * PANEL)
        to = pl.ds(pl.multiple_of(bin_ref[p] * PANEL, PANEL), PANEL)
        a_ref[to, 0:channels] = x_ref[rows, :]
        a_ref[to, channels : channels + pair] = bc_ref[rows, pl.ds(group, pair)]
        label = (slot_ref[p] * PANEL + 1 + row_ids(shape)).astype(f32)
        lanes = lane_ids(shape)
        meta = jnp.where(lanes == LANES - 1, label, dt_ref[rows, :])
        a_ref[to, channels + pair : channels + pair + LANES] = meta.astype(bf16)
        zs_ref[to, :] = z_ref[rows, :]


def forward_body(
    width,
    heads,
    len_ref,
    co_ref,
    recv_ref,
    cx_ref,
    cbc_ref,
    bias_ref,
    alog_ref,
    skip_ref,
    pt_ref,
    xraw_ref,
    xpre_ref,
    mixed_ref,
    share_ref,
    bcact_ref,
    scores_ref,
    step_ref,
    slope_ref,
    cum_ref,
    cumt_ref,
):
    rows, channels = xraw_ref.shape
    pair = bcact_ref.shape[1]
    state = pair // 2
    head_width = channels // heads
    slots = recv_ref.shape[0]
    label = recv_ref[:, channels + pair : channels + pair + LANES].astype(f32)[:, LANES - 1 :]
    place = (label == (lane_ids((slots, rows)) + 1).astype(f32)).astype(bf16)
    pt_ref[...] = place
    raw = dot_tn(place, recv_ref[...])
    keeps = keep_masks(len_ref, rows, width)
    xraw = raw[:, :channels]
    xraw_ref[...] = xraw.astype(bf16)
    xpre = conv(xraw, cx_ref[...], keeps)
    xpre_ref[...] = xpre
    xact = xpre * jax.nn.sigmoid(xpre)
    bcraw = raw[:, channels : channels + pair]
    share = share_ref.shape[2] // 2
    for s in range(share_ref.shape[0]):
        tile = bcraw[:, (s // 2) * LANES : (s // 2 + 1) * LANES]
        if s % 2:
            tile = pltpu.roll(tile, share, 1)
        share_ref[s] = jnp.where(lane_ids(tile.shape) < share, tile, 0.0)
    group = pl.multiple_of(co_ref[0] * pair, pair)
    bcpre = conv(bcraw, cbc_ref[:, pl.ds(group, pair)], keeps)
    bcact = (bcpre * jax.nn.sigmoid(bcpre)).astype(bf16)
    bcact_ref[...] = bcact
    scores = dot_nt(bcact[:, state:], bcact[:, :state])
    scores_ref[...] = scores
    mask = seen_mask(len_ref, rows)
    dt = raw[:, channels + pair : channels + pair + LANES] + bias_ref[...]
    real = lane_ids(dt.shape) < heads
    step = jnp.where(real, jnp.maximum(dt, 0.0) + jnp.log1p(jnp.exp(-jnp.abs(dt))), 0.0)
    step_ref[...] = step
    slope_ref[...] = jnp.where(real, jax.nn.sigmoid(dt), 0.0)
    cum = dot_nn(mask.astype(f32), step * -jnp.exp(alog_ref[...]), exact)
    cum_ref[...] = cum
    cumt = jnp.transpose(cum)[: cumt_ref.shape[0]]
    cumt_ref[...] = cumt
    scaled = (xact * dot_nn(step, head_spread(channels, head_width), exact)).astype(bf16)
    skipped = xact * skip_ref[...]
    low = lane_ids((rows, LANES)) < head_width
    for p in range(channels // LANES):
        tile = scaled[:, p * LANES : (p + 1) * LANES]
        total = skipped[:, p * LANES : (p + 1) * LANES]
        for half in range(2):
            h = 2 * p + half
            gap = jnp.where(mask, cum[:, h : h + 1] - cumt[h : h + 1, :], FAR)
            weights = (scores * jnp.exp(jnp.minimum(gap, 0.0))).astype(bf16)
            part = jnp.where(low if half == 0 else ~low, tile, jnp.zeros_like(tile))
            total = total + dot_nn(weights, part)
        mixed_ref[:, p * LANES : (p + 1) * LANES] = total


def gate_body(recv_ref, pt_ref, mixed_ref, zb_ref, gated_ref, sums_ref):
    z = dot_tn(pt_ref[...], recv_ref[...])
    zb_ref[...] = z.astype(bf16)
    gated = mixed_ref[...] * (z * jax.nn.sigmoid(z))
    gated_ref[...] = gated
    ones = jnp.ones((8, gated.shape[1]), f32)
    sums_ref[...] = dot_nt(ones, gated * gated, exact)


def as_column(parts):
    total = parts[0][...]
    for part in parts[1:]:
        total = total + part[...]
    return dot_tn(total, jnp.full((8, LANES), 0.125, f32), exact)


def norm_body(size, gated_ref, gain_ref, *refs):
    parts, (normed_ref, inv_ref) = refs[:-2], refs[-2:]
    inverse = lax.rsqrt(as_column(parts) / size + 1e-05)
    inv_ref[...] = inverse
    normed = gated_ref[...] * inverse[:, :1] * gain_ref[...]
    normed_ref[...] = normed.astype(bf16)


def rows_of(out_ref, k):
    tensor, _, panel, columns = out_ref.shape
    return out_ref[:, k].reshape(tensor * panel, columns)


def dnormed_body(out_ref, w_ref, *p_refs):
    w = jnp.concatenate([w_ref[z] for z in range(w_ref.shape[0])], axis=1)
    for k, p_ref in enumerate(p_refs):
        p_ref[...] = dot_nt(rows_of(out_ref, k), w).astype(p_ref.dtype)


def term_body(scale, out_ref, *refs):
    normed, term_ref = refs[:-1], refs[-1]
    total = None
    for k, normed_ref in enumerate(normed):
        part = dot_tn(normed_ref[...], rows_of(out_ref, k))
        total = part if total is None else total + part
    total = (total * scale).astype(bf16)
    for z in range(term_ref.shape[0]):
        term_ref[z] = total[:, z * LANES : (z + 1) * LANES]


def cross_body(gated_ref, inv_ref, gain_ref, *refs):
    parts, (weighted_ref, dgain_ref, sums_ref) = refs[:-3], refs[-3:]
    dnormed = parts[0][...].astype(f32)
    for part in parts[1:]:
        dnormed = dnormed + part[...].astype(f32)
    gated = gated_ref[...]
    product = dnormed * gated
    dgain_ref[...] = jnp.sum(product * inv_ref[:, :1], axis=0, keepdims=True)
    weighted = dnormed * gain_ref[...]
    weighted_ref[...] = weighted
    ones = jnp.ones((8, gated.shape[1]), f32)
    sums_ref[...] = dot_nt(ones, product * gain_ref[...], exact)


def dz_body(size, weighted_ref, gated_ref, mixed_ref, zb_ref, inv_ref, pt_ref, *refs):
    parts, (dy_ref, back_ref) = refs[:-2], refs[-2:]
    inverse = inv_ref[...]
    factor = (inverse * inverse * inverse * as_column(parts) / size)[:, :1]
    dgated = inverse[:, :1] * weighted_ref[...] - gated_ref[...] * factor
    z = zb_ref[...].astype(f32)
    sig = jax.nn.sigmoid(z)
    dy_ref[...] = dgated * (z * sig)
    dz = dgated * mixed_ref[...] * sig * (1.0 + z * (1.0 - sig))
    back_ref[...] = dot_nn(pt_ref[...], dz.astype(bf16)).astype(bf16)


def backward_body(
    width,
    heads,
    len_ref,
    co_ref,
    dy_ref,
    xpre_ref,
    xraw_ref,
    mixed_ref,
    step_ref,
    slope_ref,
    cum_ref,
    cumt_ref,
    scores_ref,
    bcact_ref,
    cx_ref,
    alog_ref,
    skip_ref,
    gx_ref,
    dcx_ref,
    ddt_ref,
    dheads_ref,
    pieces_ref,
):
    rows, channels = xraw_ref.shape
    pair = bcact_ref.shape[1]
    state = pair // 2
    head_width = channels // heads
    mask = seen_mask(len_ref, rows)
    keeps = keep_masks(len_ref, rows, width)
    xpre = xpre_ref[...]
    sig = jax.nn.sigmoid(xpre)
    xact = xpre * sig
    step = step_ref[...]
    spread = dot_nn(step, head_spread(channels, head_width), exact)
    scaled = (xact * spread).astype(bf16)
    dy = dy_ref[...]
    dyb = dy.astype(bf16)
    cum = cum_ref[...]
    cumt = cumt_ref[...]
    scores = scores_ref[...]
    low = lane_ids((rows, LANES)) < head_width
    dscores = jnp.zeros((rows, rows), f32)
    pieces = []
    for p in range(channels // LANES):
        tile = scaled[:, p * LANES : (p + 1) * LANES]
        dtile = dyb[:, p * LANES : (p + 1) * LANES]
        total = None
        for half in range(2):
            h = 2 * p + half
            gap = jnp.where(mask, cum[:, h : h + 1] - cumt[h : h + 1, :], FAR)
            decay = jnp.exp(jnp.minimum(gap, 0.0))
            weights = (scores * decay).astype(bf16)
            part = jnp.where(low if half == 0 else ~low, dtile, jnp.zeros_like(dtile))
            dscores = dscores + dot_nt(part, tile) * decay
            term = dot_tn(weights, part)
            total = term if total is None else total + term
        pieces.append(total)
    dscaled = jnp.concatenate(pieces, axis=1)
    skip = skip_ref[...]
    table = head_table(channels, head_width)
    inner = mixed_ref[...] - skip * xact
    rowsum = dyb.astype(f32) * inner
    colsum = scaled.astype(f32) * dscaled
    change = dot_nn(rowsum - colsum, table, exact)
    direct = dot_nn(xact * dscaled, table, exact)
    dlog = dot_tn(mask.astype(f32), change, exact)
    rate = -jnp.exp(alog_ref[...])
    ddt = (dlog * rate + direct) * slope_ref[...]
    ddt_ref[...] = ddt
    dskip = dot_nn(
        jnp.broadcast_to(jnp.sum(dy * xact, axis=0, keepdims=True), (8, channels)), table, exact
    )
    dheads_ref[0:1] = jnp.sum(ddt, axis=0, keepdims=True)
    dheads_ref[1:2] = jnp.sum(dlog * step * rate, axis=0, keepdims=True)
    dheads_ref[2:3] = dskip[0:1]
    dpre = (dscaled * spread + skip * dy) * (sig * (1.0 + xpre * (1.0 - sig)))
    draw, dtaps = conv_back(dpre, xraw_ref[...].astype(f32), cx_ref[...], keeps)
    gx_ref[...] = draw.astype(bf16)
    for k in range(width):
        dcx_ref[k : k + 1] = dtaps[k]
    dsb = dscores.astype(bf16)
    dbc = (
        dot_tn(dsb, bcact_ref[:, state:]),
        dot_nn(dsb, bcact_ref[:, :state]),
    )
    share = pieces_ref.shape[2] // 2
    for s in range(pieces_ref.shape[0]):
        low_lane = (s * share) % state
        tile = dbc[s * share // state][:, low_lane // LANES * LANES : (low_lane // LANES + 1) * LANES]
        if low_lane % LANES:
            tile = pltpu.roll(tile, share, 1)
        tile = jnp.where(lane_ids(tile.shape) < share, tile, 0.0)
        pieces_ref[jnp.bitwise_xor(co_ref[2], s)] = tile.astype(bf16)


def share_body(
    width,
    len_ref,
    co_ref,
    share_ref,
    taps_ref,
    gx_ref,
    ddt_ref,
    pt_ref,
    dcx_ref,
    dgain_ref,
    dheads_ref,
    *refs,
):
    parts, back_ref, small_ref = refs[:-2], refs[-2], refs[-1]
    rows = ddt_ref.shape[0]
    channels = gx_ref.shape[1]
    slots = back_ref.shape[0]
    keeps = keep_masks(len_ref, rows, width)
    raw = share_ref[co_ref[2]]
    taps = taps_ref[...]
    pre = conv(raw, taps, keeps)
    sig = jax.nn.sigmoid(pre)
    dact = parts[0][...].astype(f32)
    for part in parts[1:]:
        dact = dact + part[...].astype(f32)
    draw, dtaps = conv_back(dact * (sig * (1.0 + pre * (1.0 - sig))), raw, taps, keeps)
    share = LANES // 2
    meta = draw + pltpu.roll(ddt_ref[...], share, 1)
    place = pt_ref[...]
    back_ref[:, :channels] = dot_nn(place, gx_ref[...]).astype(bf16)
    back_ref[:, channels : channels + LANES] = dot_nn(place, meta.astype(bf16)).astype(bf16)
    small_ref[...] = jnp.zeros_like(small_ref)
    small_ref[0:width] = dcx_ref[...]
    small_ref[width : width + 1] = dgain_ref[...]
    small_ref[width + 1 : width + 4, 0:LANES] = dheads_ref[...]
    for k in range(width):
        row = width + 1 + k % 3
        lane = LANES * (1 + k // 3)
        small_ref[row : row + 1, lane : lane + LANES] = dtaps[k]
    half = channels // 2
    block = jnp.concatenate([small_ref[:, :half], small_ref[:, half:]], axis=0).astype(bf16)
    for k in range(slots // PANEL):
        back_ref[k * PANEL : (k + 1) * PANEL, channels + LANES :] = block


def home_z_body(bin_ref, ret_ref, gz_ref):
    for p in range(bin_ref.shape[0]):
        at = pl.ds(pl.multiple_of(bin_ref[p] * PANEL, PANEL), PANEL)
        gz_ref[p * PANEL : (p + 1) * PANEL] = ret_ref[at]


def home_body(
    scale, heads, bin_ref, ret_ref, gx_ref, gbc_ref, gdt_ref, dcx_ref, dcbc_ref, dgain_ref, dheads_ref
):
    channels = gx_ref.shape[1]
    width = dcx_ref.shape[0]
    share = gbc_ref.shape[1]
    for p in range(bin_ref.shape[0]):
        rows = slice(p * PANEL, (p + 1) * PANEL)
        at = pl.ds(pl.multiple_of(bin_ref[p] * PANEL, PANEL), PANEL)
        gx_ref[rows] = ret_ref[at, :channels]
        meta = ret_ref[at, channels : channels + LANES].astype(f32)
        gbc_ref[rows] = meta[:, :share].astype(bf16)
        gdt_ref[rows] = pltpu.roll(meta, LANES - share, 1)[:, :heads].astype(bf16)
    total = None
    for k in range(ret_ref.shape[0] // PANEL):
        part = ret_ref[k * PANEL : (k + 1) * PANEL, channels + LANES :].astype(f32)
        total = part if total is None else total + part
    total = total * scale
    small = jnp.concatenate([total[:8], total[8:]], axis=1)
    dcx_ref[...] = small[:width]
    dgain_ref[...] = small[width : width + 1]
    dheads_ref[...] = small[width + 1 : width + 4, :heads]
    for k in range(width):
        row = width + 1 + k % 3
        lane = LANES * (1 + k // 3)
        dcbc_ref[k : k + 1] = small[row : row + 1, lane : lane + share]


def per_device(
    x_in,
    z_in,
    bc_in,
    dt_in,
    lengths,
    panel_bin,
    panel_slot,
    conv_x,
    conv_bc,
    dt_bias,
    a_log,
    dskip,
    gain,
    w_out,
    dout,
):
    dp = lax.axis_size("dp")
    tensor = lax.axis_size("tensor")
    inner = DP_INNER
    outer = dp // inner
    t_index = lax.axis_index("tensor")
    x_index = lax.axis_index("dp") % inner
    rows, channels = x_in.shape
    heads = dt_in.shape[1]
    head_width = channels // heads
    width = conv_x.shape[0]
    bc_width = conv_bc.shape[1]
    pair = bc_width // GROUPS
    share = bc_width // tensor
    members = tensor // GROUPS
    group = t_index // members
    local = t_index % members
    slots = dp * PANEL
    size = channels * members
    scale = 1.0 / math.sqrt(rows * dp)
    columns = outer * LANES

    coords = jnp.stack([group, x_index, local]).astype(jnp.int32)
    over_z = [[z * inner + x for z in range(outer)] for x in range(inner)]

    def along_x(block, shift):
        route = []
        for z in range(outer):
            for x in range(inner):
                route.append((z * inner + x, z * inner + (x + shift) % inner))
        return lax.ppermute(block, "dp", route)

    def partner(block, flip):
        return lax.ppermute(block, "tensor", [(t, t ^ flip) for t in range(tensor)])

    def in_group(block):
        return [block] + [partner(block, flip) for flip in range(1, members)]

    d_parts = call(
        pack_dout_body,
        [shaped((dout.shape[0], columns), bf16)] * inner,
        [coords, dout],
        scalars=1,
        name="pack_dout",
    )
    d_own = [d_parts[0]] + [along_x(d_parts[k], k) for k in range(1, inner)]
    out_rows = lax.all_gather(jnp.concatenate(d_own, axis=0), "tensor", axis=0, tiled=True)
    out_rows = out_rows.reshape(tensor, inner, dout.shape[0], columns)
    w_cols = lax.all_gather(
        w_out, "dp", axis=0, tiled=True, axis_index_groups=over_z
    ).reshape(outer, channels, LANES)

    dt_wide = jnp.pad(dt_in.astype(f32), ((0, 0), (0, LANES - heads)))
    first = channels + pair + LANES
    send_a, send_z = call(
        pack_body,
        [shaped((slots, first), bf16), shaped((slots, channels), bf16)],
        [panel_bin, panel_slot, coords, x_in, z_in, bc_in, dt_wide],
        scalars=3,
        name="pack",
    )
    recv_a = lax.all_to_all(send_a, "dp", split_axis=0, concat_axis=0, tiled=True)
    recv_z = lax.all_to_all(send_z, "dp", split_axis=0, concat_axis=0, tiled=True)

    bias_row = jnp.pad(dt_bias, (0, LANES - heads))[None, :]
    alog_row = jnp.pad(a_log, (0, LANES - heads))[None, :]
    skip_row = jnp.repeat(dskip, head_width)[None, :]
    gain_row = gain[None, :]
    share_taps = jnp.pad(
        lax.dynamic_slice_in_dim(conv_bc, t_index * share, share, 1),
        ((0, 0), (0, LANES - share)),
    )

    place, xraw, xpre, mixed, raw_share, bcact, scores, step, slope, cum, cumt = call(
        functools.partial(forward_body, width, heads),
        [
            shaped((slots, rows), bf16),
            shaped((rows, channels), bf16),
            shaped((rows, channels), f32),
            shaped((rows, channels), f32),
            shaped((members, rows, LANES), f32),
            shaped((rows, pair), bf16),
            shaped((rows, rows), f32),
            shaped((rows, LANES), f32),
            shaped((rows, LANES), f32),
            shaped((rows, LANES), f32),
            shaped((8, rows), f32),
        ],
        [lengths, coords, recv_a, conv_x, conv_bc, bias_row, alog_row, skip_row],
        scalars=2,
        cost=4000,
        name="forward",
    )
    zb, gated, squares = call(
        gate_body,
        [
            shaped((rows, channels), bf16),
            shaped((rows, channels), f32),
            shaped((8, rows), f32),
        ],
        [recv_z, place, mixed],
        cost=1000,
        name="gate",
    )
    normed, inverse = call(
        functools.partial(norm_body, size),
        [shaped((rows, channels), bf16), shaped((rows, LANES), f32)],
        [gated, gain_row] + in_group(squares),
        cost=500,
        name="norm",
    )

    partial = call(
        dnormed_body,
        [shaped((rows, channels), f32)] + [shaped((rows, channels), bf16)] * (inner - 1),
        [out_rows, w_cols],
        cost=1200,
        name="dnormed",
    )
    d_terms = [partial[0]] + [along_x(partial[k], -k) for k in range(1, inner)]
    weighted, dgain, crossing = call(
        cross_body,
        [
            shaped((rows, channels), f32),
            shaped((1, channels), f32),
            shaped((8, rows), f32),
        ],
        [gated, inverse, gain_row] + d_terms,
        cost=500,
        name="cross",
    )
    dy, back_z = call(
        functools.partial(dz_body, size),
        [shaped((rows, channels), f32), shaped((slots, channels), bf16)],
        [weighted, gated, mixed, zb, inverse, place] + in_group(crossing),
        cost=1000,
        name="dz",
    )
    home_z = lax.all_to_all(back_z, "dp", split_axis=0, concat_axis=0, tiled=True)

    normed_all = [normed] + [along_x(normed, k) for k in range(1, inner)]
    (term,) = call(
        functools.partial(term_body, scale),
        [shaped((outer, channels, LANES), bf16)],
        [out_rows] + normed_all,
        cost=1200,
        name="term",
    )
    grad_wout = lax.psum_scatter(
        term.reshape(outer * channels, LANES),
        "dp",
        scatter_dimension=0,
        axis_index_groups=over_z,
        tiled=True,
    )

    gx, dcx, ddt, dheads, pieces = call(
        functools.partial(backward_body, width, heads),
        [
            shaped((rows, channels), bf16),
            shaped((width, channels), f32),
            shaped((rows, LANES), f32),
            shaped((3, LANES), f32),
            shaped((members, rows, LANES), bf16),
        ],
        [
            lengths,
            coords,
            dy,
            xpre,
            xraw,
            mixed,
            step,
            slope,
            cum,
            cumt,
            scores,
            bcact,
            conv_x,
            alog_row,
            skip_row,
        ],
        scalars=2,
        cost=6000,
        name="backward",
    )
    parts = [pieces[0]] + [partner(pieces[flip], flip) for flip in range(1, members)]
    (back_a,) = call(
        functools.partial(share_body, width),
        [shaped((slots, channels + LANES + channels // 2), bf16)],
        [
            lengths,
            coords,
            raw_share,
            share_taps,
            gx,
            ddt,
            place,
            dcx,
            dgain,
            dheads,
        ]
        + parts,
        scalars=2,
        cost=1500,
        scratch=[pltpu.VMEM((8, channels), f32)],
        name="share",
    )
    home_a = lax.all_to_all(back_a, "dp", split_axis=0, concat_axis=0, tiled=True)
    (grad_z,) = call(
        home_z_body,
        [shaped((rows, channels), bf16)],
        [panel_bin, home_z],
        scalars=1,
        name="home_z",
    )
    grad_x, grad_bc, grad_dt, grad_cx, grad_cbc, grad_gain, grad_heads = call(
        functools.partial(home_body, scale, heads),
        [
            shaped((rows, channels), bf16),
            shaped((rows, share), bf16),
            shaped((rows, heads), bf16),
            shaped((width, channels), f32),
            shaped((width, share), f32),
            shaped((1, channels), f32),
            shaped((3, heads), f32),
        ],
        [panel_bin, home_a],
        scalars=1,
        name="home",
    )
    return (
        grad_x,
        grad_z,
        grad_bc,
        grad_dt,
        grad_wout,
        grad_cx,
        grad_cbc,
        grad_gain[0],
        grad_heads,
    )


def solution(mesh):
    placed = (
        P("dp", "tensor"),
        P("dp", "tensor"),
        P("dp", None),
        P("dp", "tensor"),
        P("dp", None),
        P("dp"),
        P("dp"),
        P(None, "tensor"),
        P(),
        P("tensor"),
        P("tensor"),
        P("tensor"),
        P("tensor"),
        P("tensor", "dp"),
        P(("dp", "tensor"), None),
    )
    return jax.shard_map(
        per_device,
        mesh=mesh,
        in_specs=placed,
        out_specs=(
            P("dp", "tensor"),
            P("dp", "tensor"),
            P("dp", "tensor"),
            P("dp", "tensor"),
            P("tensor", "dp"),
            P(None, "tensor"),
            P(None, "tensor"),
            P("tensor"),
            P(None, "tensor"),
        ),
        check_vma=False,
    )
```

time: 556 us -> 248 us (0.45)
  the two profiles are of different devices: /device:TPU:40 before, /device:TPU:2 now
where the time goes in v1:
time: 248 us; the launch traced here: 247 us
  starting transfers between devices  83.6 us (34%)
  waiting for transfers between devices  61.7 us (25%)
  blocking collectives  34.9 us (14%)
  local copies, waits for them, and re-layouts  28.9 us (12%)
  Pallas kernels  22.4 us (9%)
  between operations  14.3 us (6%)
    all_to_all x1, blocking collectives, per_device(): lax.all_to_all(send_a, 'dp', split_axis=0, concat_axis=0, tiled=True)  34.9 us
    ppermute x9, starting transfers between devices, along_x(): return lax.ppermute(block, 'dp', route)  34 us
    unnamed x85, local copies, waits for them, and re-layouts  28.7 us
    all_gather x1, waiting for transfers between devices, per_device(): lax.all_gather(jnp.concatenate(d_own, axis=0), 'tensor', axis=0, tiled=True)  28.4 us
    all_to_all x1, waiting for transfers between devices, per_device(): lax.all_to_all(back_a, 'dp', split_axis=0, concat_axis=0, tiled=True)  24.4 us
    ppermute x9, starting transfers between devices, partner(): return lax.ppermute(block, 'tensor', [(t, t ^ flip) for t in range(tensor)])  22.7 us
    pallas_call x13, Pallas kernels, call(): pl.pallas_call(body, out_shape=outs, in_specs=[smem] * scalars + [vmem] *...  22.4 us
    all_to_all x1, starting transfers between devices, per_device(): lax.all_to_all(back_z, 'dp', split_axis=0, concat_axis=0, tiled=True)  10.3 us
  transfers between devices with their start and end apart: 24, of which 6 were waited for; matrix products, arithmetic and copies ran while one was open for 1% of the time, Pallas kernels for 9%

profile of v1, /device:TPU:2, one launch (start us, length us, event | category | flops | bytes accessed | tf_op | source)
XLA Modules:
  0.0 246.6 jit_solution(4330419474107044952)
XLA Ops:
  9.6 3.4 %collective-permute-start.3 = (bf16[16,1024]{1,0:T(8,128)(2,1)S(1)}, bf16[16,1024]{1,0:T(8,128)(2,1)S(1)}, u32[]{:S(2)}, u32[]{:S(2)}) collective-permute-start(bf16[16,1024]{1,0:T(8,128)(2,1)S(1)} %get-tuple-element.61), channel_id=1, source_target_pairs={{0,16},{16,32},{32,48},{48,0},{64,80},{80,96},{96,112},{112,64},{1... | collective-permute-start | bytes 98312 | tf_op jit(solution)/shard_map/ppermute | solution.py:524
  13.0 8.4 %collective-permute-start.4 = (bf16[16,1024]{1,0:T(8,128)(2,1)S(1)}, bf16[16,1024]{1,0:T(8,128)(2,1)S(1)}, u32[]{:S(2)}, u32[]{:S(2)}) collective-permute-start(bf16[16,1024]{1,0:T(8,128)(2,1)S(1)} %get-tuple-element.62), channel_id=1, source_target_pairs={{0,32},{16,48},{32,0},{48,16},{64,96},{80,112},{96,64},{112,80},{1... | collective-permute-start | bytes 98312 | tf_op jit(solution)/shard_map/ppermute | solution.py:524
  21.4 1.9 collective-permute-start.5
  23.3 3.9 %collective-permute-done.5 = bf16[16,1024]{1,0:T(8,128)(2,1)S(1)} collective-permute-done((bf16[16,1024]{1,0:T(8,128)(2,1)S(1)}, bf16[16,1024]{1,0:T(8,128)(2,1)S(1)}, u32[]{:S(2)}, u32[]{:S(2)}) %collective-permute-start.5) | collective-permute-done | bytes 32800 | tf_op jit(solution)/shard_map/ppermute | solution.py:524
  34.5 34.9 %all_to_all.44 = bf16[32,16,896]{2,1,0:T(8,128)(2,1)S(1)} all-to-all(bf16[32,16,896]{2,1,0:T(8,128)(2,1)S(1)} %bitcast.31), channel_id=1, replica_groups=mesh['dp'=32,'tensor'=16] {'dp'}, dimensions={0} | all-to-all | bytes 1835008 | tf_op jit(solution)/shard_map/all_to_all | solution.py:555
  69.4 7.4 %all-to-all-start.1 = ((bf16[32,16,512]{2,1,0:T(8,128)(2,1)}), bf16[32,16,512]{2,1,0:T(8,128)(2,1)S(1)}, u32[]{:S(2)}, u32[]{:S(2)}) async-start(bf16[32,16,512]{2,1,0:T(8,128)(2,1)} %bitcast.7), calls=%async_computation.1 | async-start | bytes 1048576 | tf_op jit(solution)/shard_map/all_to_all | solution.py:556
  77.1 28.4 %all-gather.3.cloned.1.call-done = bf16[1024,1024]{1,0:T(8,128)(2,1)} async-done(((bf16[64,1024]{1,0:T(8,128)(2,1)}), bf16[1024,1024]{1,0:T(8,128)(2,1)}) %all-gather.3.cloned.1.call-update) | async-done | bytes 2097168 | tf_op jit(solution)/shard_map/all_gather | solution.py:540
  109.5 2.5 %collective-permute-start.6 = (bf16[256,512]{1,0:T(8,128)(2,1)S(1)}, bf16[256,512]{1,0:T(8,128)(2,1)S(1)}, u32[]{:S(2)}, u32[]{:S(2)}) collective-permute-start(bf16[256,512]{1,0:T(8,128)(2,1)S(1)} %get-tuple-element.65), channel_id=1, source_target_pairs={{0,48},{16,0},{32,16},{48,32},{64,112},{80,64},{96,80},{112,96},{1... | collective-permute-start | bytes 786440 | tf_op jit(solution)/shard_map/ppermute | solution.py:524
  112.0 3.1 %forward.1 = (bf16[512,256]{1,0:T(8,128)(2,1)S(1)}, bf16[256,512]{1,0:T(8,128)(2,1)S(1)}, f32[256,512]{1,0:T(8,128)S(1)}, f32[256,512]{1,0:T(8,128)S(1)}, f32[4,...) custom-call(s32[1,6]{1,0:T(1,128)S(1)} %copy-done.13, ...), custom_call_target="tpu_custom_call" | custom-call | flops 4000000000 | bytes 3836964 | tf_op jit(solution)/shard_map/forward/pallas_call | solution.py:27
  125.2 2.5 %collective-permute-start.2 = (f32[8,256]{1,0:T(8,128)S(1)}, f32[8,256]{1,0:T(8,128)S(1)}, u32[]{:S(2)}, u32[]{:S(2)}) collective-permute-start(f32[8,256]{1,0:T(8,128)S(1)} %get-tuple-element.58.refs_0_), channel_id=1, source_target_pairs={{0,3},{1,2},{2,1},{3,0},{4,7},{5,6},{6,5},{7,4},{8,11},{9,10},{10,... | collective-permute-start | bytes 24584 | tf_op jit(solution)/shard_map/ppermute | solution.py:527
  127.7 2.9 %collective-permute-start.1 = (f32[8,256]{1,0:T(8,128)S(1)}, f32[8,256]{1,0:T(8,128)S(1)}, u32[]{:S(2)}, u32[]{:S(2)}) collective-permute-start(f32[8,256]{1,0:T(8,128)S(1)} %get-tuple-element.58.refs_0_), channel_id=1, source_target_pairs={{0,2},{1,3},{2,0},{3,1},{4,6},{5,7},{6,4},{7,5},{8,10},{9,11},{10,... | collective-permute-start | bytes 24584 | tf_op jit(solution)/shard_map/ppermute | solution.py:527
  130.6 2.2 collective-permute-start
  132.8 4.3 %collective-permute-start.7 = (bf16[256,512]{1,0:T(8,128)(2,1)S(1)}, bf16[256,512]{1,0:T(8,128)(2,1)S(1)}, u32[]{:S(2)}, u32[]{:S(2)}) collective-permute-start(bf16[256,512]{1,0:T(8,128)(2,1)S(1)} %get-tuple-element.66), channel_id=1, source_target_pairs={{0,32},{16,48},{32,0},{48,16},{64,96},{80,112},{96,64},{112,80},{1... | collective-permute-start | bytes 786440 | tf_op jit(solution)/shard_map/ppermute | solution.py:524
  137.1 3.5 %collective-permute-start.8 = (bf16[256,512]{1,0:T(8,128)(2,1)S(1)}, bf16[256,512]{1,0:T(8,128)(2,1)S(1)}, u32[]{:S(2)}, u32[]{:S(2)}) collective-permute-start(bf16[256,512]{1,0:T(8,128)(2,1)S(1)} %get-tuple-element.67), channel_id=1, source_target_pairs={{0,16},{16,32},{32,48},{48,0},{64,80},{80,96},{96,112},{112,64},{1... | collective-permute-start | bytes 786440 | tf_op jit(solution)/shard_map/ppermute | solution.py:524
  141.1 2.3 collective-permute-start.17
  143.4 3.1 %collective-permute-start.16 = (bf16[256,512]{1,0:T(8,128)(2,1)S(1)}, bf16[256,512]{1,0:T(8,128)(2,1)}, u32[]{:S(2)}, u32[]{:S(2)}) collective-permute-start(bf16[256,512]{1,0:T(8,128)(2,1)S(1)} %get-tuple-element.90.refs_0_), channel_id=1, source_target_pairs={{0,32},{16,48},{32,0},{48,16},{64,96},{80,112},{96,64},{112,80},{1... | collective-permute-start | bytes 786440 | tf_op jit(solution)/shard_map/ppermute | solution.py:524
  146.6 4.5 %collective-permute-start.15 = (bf16[256,512]{1,0:T(8,128)(2,1)S(1)}, bf16[256,512]{1,0:T(8,128)(2,1)S(1)}, u32[]{:S(2)}, u32[]{:S(2)}) collective-permute-start(bf16[256,512]{1,0:T(8,128)(2,1)S(1)} %get-tuple-element.90.refs_0_), channel_id=1, source_target_pairs={{0,16},{16,32},{32,48},{48,0},{64,80},{80,96},{96,112},{112,64},{1... | collective-permute-start | bytes 786440 | tf_op jit(solution)/shard_map/ppermute | solution.py:524
  151.8 1.9 collective-permute-start.11
  153.7 2.9 %collective-permute-start.10 = (f32[8,256]{1,0:T(8,128)S(1)}, f32[8,256]{1,0:T(8,128)S(1)}, u32[]{:S(2)}, u32[]{:S(2)}) collective-permute-start(f32[8,256]{1,0:T(8,128)S(1)} %get-tuple-element.70.refs_0_), channel_id=1, source_target_pairs={{0,2},{1,3},{2,0},{3,1},{4,6},{5,7},{6,4},{7,5},{8,10},{9,11},{10,... | collective-permute-start | bytes 24584 | tf_op jit(solution)/shard_map/ppermute | solution.py:527
  156.6 2.7 %collective-permute-start.9 = (f32[8,256]{1,0:T(8,128)S(1)}, f32[8,256]{1,0:T(8,128)S(1)}, u32[]{:S(2)}, u32[]{:S(2)}) collective-permute-start(f32[8,256]{1,0:T(8,128)S(1)} %get-tuple-element.70.refs_0_), channel_id=1, source_target_pairs={{0,1},{1,0},{2,3},{3,2},{4,5},{5,4},{6,7},{7,6},{8,9},{9,8},{10,11... | collective-permute-start | bytes 24584 | tf_op jit(solution)/shard_map/ppermute | solution.py:527
  159.4 2.2 collective-permute-done.15.refs_1_
  161.6 1.6 copy-done.10
  163.2 3.2 %term.1 = bf16[8,512,128]{2,1,0:T(8,128)(2,1)} custom-call(bf16[16,4,16,1024]{3,2,1,0:T(8,128)(2,1)S(1)} %bitcast.36, bf16[256,512]{1,0:T(8,128)(2,1)S(1)} %get-tuple-element.90.refs_0_, bf16[256,512]{1,0:T(8,128)(2,1)S(1)} %collective-permute-done.15.refs_1_, bf16[256,512]{1,0:T(8,128)(2,1)} %collective-permute-done.16.refs_2_, ...), custom_call_target="tpu_custom_call" | custom-call | flops 1200000000 | bytes 4194304 | tf_op jit(solution)/shard_map/term/pallas_call | solution.py:27
  169.4 1.8 dz.1
  171.2 10.3 %all-to-all-start.3 = ((bf16[32,16,512]{2,1,0:T(8,128)(2,1)}), bf16[32,16,512]{2,1,0:T(8,128)(2,1)S(1)}, u32[]{:S(2)}, u32[]{:S(2)}) async-start(bf16[32,16,512]{2,1,0:T(8,128)(2,1)} %bitcast.18), calls=%async_computation.3 | async-start | bytes 1048576 | tf_op jit(solution)/shard_map/all_to_all | solution.py:632
  186.3 4.3 %backward.1 = (bf16[256,512]{1,0:T(8,128)(2,1)S(1)}, f32[4,512]{1,0:T(4,128)S(1)}, f32[256,128]{1,0:T(8,128)S(1)}, f32[3,128]{1,0:T(4,128)S(1)}, bf16[4,256,128]{2,1,0:T(8,128)(2,1)S(1)}) custom-call(s32[1,6]{1,0:T(1,128)S(1)} %copy-done.13, s32[3]{0:T(128)S(1)} %pad_add_fusion.co_ref, f32[256,512]{1,0:T(8,128)S(1)} %get-tuple-element.71.dy_ref, ...), custom_call_target="tpu_custom_call" | custom-call | flops 6000000000 | bytes 3305508 | tf_op jit(solution)/shard_map/backward/pallas_call | solution.py:27
  190.6 2.3 collective-permute-start.14
  192.9 2.9 %collective-permute-start.13 = (bf16[256,128]{1,0:T(8,128)(2,1)S(1)}, bf16[256,128]{1,0:T(8,128)(2,1)S(1)}, u32[]{:S(2)}, u32[]{:S(2)}) collective-permute-start(bf16[256,128]{1,0:T(8,128)(2,1)S(1)} %get-tuple-element.105), channel_id=1, source_target_pairs={{0,2},{1,3},{2,0},{3,1},{4,6},{5,7},{6,4},{7,5},{8,10},{9,11},{10,... | collective-permute-start | bytes 196616 | tf_op jit(solution)/shard_map/ppermute | solution.py:527
  195.8 2.4 collective-permute-start.12
  199.7 2.1 share.1
  202.6 9.1 %all-to-all-start.2 = ((bf16[32,16,896]{2,1,0:T(8,128)(2,1)}), bf16[32,16,896]{2,1,0:T(8,128)(2,1)S(1)}, u32[]{:S(2)}, u32[]{:S(2)}) async-start(bf16[32,16,896]{2,1,0:T(8,128)(2,1)} %bitcast.16), calls=%async_computation.2 | async-start | bytes 1835008 | tf_op jit(solution)/shard_map/all_to_all | solution.py:702
  212.9 24.4 %all-to-all-done.2 = bf16[32,16,896]{2,1,0:T(8,128)(2,1)S(1)} async-done(((bf16[32,16,896]{2,1,0:T(8,128)(2,1)}), bf16[32,16,896]{2,1,0:T(8,128)(2,1)S(1)}, u32[]{:S(2)}, u32[]{:S(2)}) %all-to-all-start.2) | async-done | bytes 917536 | tf_op jit(solution)/shard_map/all_to_all | solution.py:702
  (127 shorter events, 38.9 us)
Async XLA Ops:
  7.2 69.9 %all-gather.5.cloned.1.call-start = ((), (), s32[]{:S(2)}) async-start(), calls=%async_computation.6 | async-start | bytes 1179648 | tf_op jit(solution)/shard_map/all_gather | solution.py:542
  7.9 97.5 %all-gather.3.cloned.1.call-start = ((), (), s32[]{:S(2)}) async-start(), calls=%async_computation.5 | async-start | bytes 2228224 | tf_op jit(solution)/shard_map/all_gather | solution.py:540
  9.6 13.7 %collective-permute-start.3 = (bf16[16,1024]{1,0:T(8,128)(2,1)S(1)}, bf16[16,1024]{1,0:T(8,128)(2,1)S(1)}, u32[]{:S(2)}, u32[]{:S(2)}) collective-permute-start(bf16[16,1024]{1,0:T(8,128)(2,1)S(1)} %get-tuple-element.61), channel_id=1, source_target_pairs={{0,16},{16,32},{32,48},{48,0},{64,80},{80,96},{96,112},{112,64},{1... | collective-permute-start | bytes 98312 | tf_op jit(solution)/shard_map/ppermute | solution.py:524
  13.0 10.3 %collective-permute-start.4 = (bf16[16,1024]{1,0:T(8,128)(2,1)S(1)}, bf16[16,1024]{1,0:T(8,128)(2,1)S(1)}, u32[]{:S(2)}, u32[]{:S(2)}) collective-permute-start(bf16[16,1024]{1,0:T(8,128)(2,1)S(1)} %get-tuple-element.62), channel_id=1, source_target_pairs={{0,32},{16,48},{32,0},{48,16},{64,96},{80,112},{96,64},{112,80},{1... | collective-permute-start | bytes 98312 | tf_op jit(solution)/shard_map/ppermute | solution.py:524
  21.4 5.8 %collective-permute-start.5 = (bf16[16,1024]{1,0:T(8,128)(2,1)S(1)}, bf16[16,1024]{1,0:T(8,128)(2,1)S(1)}, u32[]{:S(2)}, u32[]{:S(2)}) collective-permute-start(bf16[16,1024]{1,0:T(8,128)(2,1)S(1)} %get-tuple-element.63), channel_id=1, source_target_pairs={{0,48},{16,0},{32,16},{48,32},{64,112},{80,64},{96,80},{112,96},{1... | collective-permute-start | bytes 98312 | tf_op jit(solution)/shard_map/ppermute | solution.py:524
  28.7 48.2 %copy-start.38 = (f32[8]{0:T(128)S(1)}, f32[8]{0:T(128)}, u32[]{:S(2)}) copy-start(f32[8]{0:T(128)} %param.26) | copy-start | bytes 100
  28.7 48.3 %copy-start.39 = (f32[8]{0:T(128)S(1)}, f32[8]{0:T(128)}, u32[]{:S(2)}) copy-start(f32[8]{0:T(128)} %param.25) | copy-start | bytes 100
  28.7 48.3 %copy-start.40 = (f32[8]{0:T(128)S(1)}, f32[8]{0:T(128)}, u32[]{:S(2)}) copy-start(f32[8]{0:T(128)} %param.24) | copy-start | bytes 100
  69.4 52.2 %all-to-all-start.1 = ((bf16[32,16,512]{2,1,0:T(8,128)(2,1)}), bf16[32,16,512]{2,1,0:T(8,128)(2,1)S(1)}, u32[]{:S(2)}, u32[]{:S(2)}) async-start(bf16[32,16,512]{2,1,0:T(8,128)(2,1)} %bitcast.7), calls=%async_computation.1 | async-start | bytes 1048576 | tf_op jit(solution)/shard_map/all_to_all | solution.py:556
  76.8 163.2 %reduce-scatter.2.cloned.1.call-start = ((), (), s32[]{:S(2)}) async-start(), calls=%async_computation.7 | async-start | bytes 1179648 | tf_op jit(solution)/shard_map/reduce_scatter | solution.py:642
  109.5 37.0 %collective-permute-start.6 = (bf16[256,512]{1,0:T(8,128)(2,1)S(1)}, bf16[256,512]{1,0:T(8,128)(2,1)S(1)}, u32[]{:S(2)}, u32[]{:S(2)}) collective-permute-start(bf16[256,512]{1,0:T(8,128)(2,1)S(1)} %get-tuple-element.65), channel_id=1, source_target_pairs={{0,48},{16,0},{32,16},{48,32},{64,112},{80,64},{96,80},{112,96},{1... | collective-permute-start | bytes 786440 | tf_op jit(solution)/shard_map/ppermute | solution.py:524
  121.6 19.0 %copy-start.6 = (f32[512]{0:T(512)S(1)}, f32[512]{0:T(512)}, u32[]{:S(2)}) copy-start(f32[512]{0:T(512)} %param.27) | copy-start | bytes 6148
  125.2 11.9 %collective-permute-start.2 = (f32[8,256]{1,0:T(8,128)S(1)}, f32[8,256]{1,0:T(8,128)S(1)}, u32[]{:S(2)}, u32[]{:S(2)}) collective-permute-start(f32[8,256]{1,0:T(8,128)S(1)} %get-tuple-element.58.refs_0_), channel_id=1, source_target_pairs={{0,3},{1,2},{2,1},{3,0},{4,7},{5,6},{6,5},{7,4},{8,11},{9,10},{10,... | collective-permute-start | bytes 24584 | tf_op jit(solution)/shard_map/ppermute | solution.py:527
  127.7 12.9 %collective-permute-start.1 = (f32[8,256]{1,0:T(8,128)S(1)}, f32[8,256]{1,0:T(8,128)S(1)}, u32[]{:S(2)}, u32[]{:S(2)}) collective-permute-start(f32[8,256]{1,0:T(8,128)S(1)} %get-tuple-element.58.refs_0_), channel_id=1, source_target_pairs={{0,2},{1,3},{2,0},{3,1},{4,6},{5,7},{6,4},{7,5},{8,10},{9,11},{10,... | collective-permute-start | bytes 24584 | tf_op jit(solution)/shard_map/ppermute | solution.py:527
  130.6 10.0 %collective-permute-start = (f32[8,256]{1,0:T(8,128)S(1)}, f32[8,256]{1,0:T(8,128)S(1)}, u32[]{:S(2)}, u32[]{:S(2)}) collective-permute-start(f32[8,256]{1,0:T(8,128)S(1)} %get-tuple-element.58.refs_0_), channel_id=1, source_target_pairs={{0,1},{1,0},{2,3},{3,2},{4,5},{5,4},{6,7},{7,6},{8,9},{9,8},{10,11... | collective-permute-start | bytes 24584 | tf_op jit(solution)/shard_map/ppermute | solution.py:527
  132.8 18.3 %collective-permute-start.7 = (bf16[256,512]{1,0:T(8,128)(2,1)S(1)}, bf16[256,512]{1,0:T(8,128)(2,1)S(1)}, u32[]{:S(2)}, u32[]{:S(2)}) collective-permute-start(bf16[256,512]{1,0:T(8,128)(2,1)S(1)} %get-tuple-element.66), channel_id=1, source_target_pairs={{0,32},{16,48},{32,0},{48,16},{64,96},{80,112},{96,64},{112,80},{1... | collective-permute-start | bytes 786440 | tf_op jit(solution)/shard_map/ppermute | solution.py:524
  137.1 14.0 %collective-permute-start.8 = (bf16[256,512]{1,0:T(8,128)(2,1)S(1)}, bf16[256,512]{1,0:T(8,128)(2,1)S(1)}, u32[]{:S(2)}, u32[]{:S(2)}) collective-permute-start(bf16[256,512]{1,0:T(8,128)(2,1)S(1)} %get-tuple-element.67), channel_id=1, source_target_pairs={{0,16},{16,32},{32,48},{48,0},{64,80},{80,96},{96,112},{112,64},{1... | collective-permute-start | bytes 786440 | tf_op jit(solution)/shard_map/ppermute | solution.py:524
  141.1 15.5 %collective-permute-start.17 = (bf16[256,512]{1,0:T(8,128)(2,1)S(1)}, bf16[256,512]{1,0:T(8,128)(2,1)S(1)}, u32[]{:S(2)}, u32[]{:S(2)}) collective-permute-start(bf16[256,512]{1,0:T(8,128)(2,1)S(1)} %get-tuple-element.90.refs_0_), channel_id=1, source_target_pairs={{0,48},{16,0},{32,16},{48,32},{64,112},{80,64},{96,80},{112,96},{1... | collective-permute-start | bytes 786440 | tf_op jit(solution)/shard_map/ppermute | solution.py:524
  143.4 16.0 %collective-permute-start.16 = (bf16[256,512]{1,0:T(8,128)(2,1)S(1)}, bf16[256,512]{1,0:T(8,128)(2,1)}, u32[]{:S(2)}, u32[]{:S(2)}) collective-permute-start(bf16[256,512]{1,0:T(8,128)(2,1)S(1)} %get-tuple-element.90.refs_0_), channel_id=1, source_target_pairs={{0,32},{16,48},{32,0},{48,16},{64,96},{80,112},{96,64},{112,80},{1... | collective-permute-start | bytes 786440 | tf_op jit(solution)/shard_map/ppermute | solution.py:524
  146.6 15.0 %collective-permute-start.15 = (bf16[256,512]{1,0:T(8,128)(2,1)S(1)}, bf16[256,512]{1,0:T(8,128)(2,1)S(1)}, u32[]{:S(2)}, u32[]{:S(2)}) collective-permute-start(bf16[256,512]{1,0:T(8,128)(2,1)S(1)} %get-tuple-element.90.refs_0_), channel_id=1, source_target_pairs={{0,16},{16,32},{32,48},{48,0},{64,80},{80,96},{96,112},{112,64},{1... | collective-permute-start | bytes 786440 | tf_op jit(solution)/shard_map/ppermute | solution.py:524
  151.8 14.6 %collective-permute-start.11 = (f32[8,256]{1,0:T(8,128)S(1)}, f32[8,256]{1,0:T(8,128)S(1)}, u32[]{:S(2)}, u32[]{:S(2)}) collective-permute-start(f32[8,256]{1,0:T(8,128)S(1)} %get-tuple-element.70.refs_0_), channel_id=1, source_target_pairs={{0,3},{1,2},{2,1},{3,0},{4,7},{5,6},{6,5},{7,4},{8,11},{9,10},{10,... | collective-permute-start | bytes 24584 | tf_op jit(solution)/shard_map/ppermute | solution.py:527
  153.7 12.7 %collective-permute-start.10 = (f32[8,256]{1,0:T(8,128)S(1)}, f32[8,256]{1,0:T(8,128)S(1)}, u32[]{:S(2)}, u32[]{:S(2)}) collective-permute-start(f32[8,256]{1,0:T(8,128)S(1)} %get-tuple-element.70.refs_0_), channel_id=1, source_target_pairs={{0,2},{1,3},{2,0},{3,1},{4,6},{5,7},{6,4},{7,5},{8,10},{9,11},{10,... | collective-permute-start | bytes 24584 | tf_op jit(solution)/shard_map/ppermute | solution.py:527
  156.6 9.8 %collective-permute-start.9 = (f32[8,256]{1,0:T(8,128)S(1)}, f32[8,256]{1,0:T(8,128)S(1)}, u32[]{:S(2)}, u32[]{:S(2)}) collective-permute-start(f32[8,256]{1,0:T(8,128)S(1)} %get-tuple-element.70.refs_0_), channel_id=1, source_target_pairs={{0,1},{1,0},{2,3},{3,2},{4,5},{5,4},{6,7},{7,6},{8,9},{9,8},{10,11... | collective-permute-start | bytes 24584 | tf_op jit(solution)/shard_map/ppermute | solution.py:527
  169.4 12.1 %copy-start.17 = (f32[256,512]{1,0:T(8,128)S(1)}, f32[256,512]{1,0:T(8,128)}, u32[]{:S(2)}) copy-start(f32[256,512]{1,0:T(8,128)} %copy-done.14) | copy-start | bytes 1572868
  169.4 12.1 %copy-start.33 = (f32[256,128]{1,0:T(8,128)S(1)}, f32[256,128]{1,0:T(8,128)}, u32[]{:S(2)}) copy-start(f32[256,128]{1,0:T(8,128)} %copy-done.32) | copy-start | bytes 393220
  171.2 31.4 %all-to-all-start.3 = ((bf16[32,16,512]{2,1,0:T(8,128)(2,1)}), bf16[32,16,512]{2,1,0:T(8,128)(2,1)S(1)}, u32[]{:S(2)}, u32[]{:S(2)}) async-start(bf16[32,16,512]{2,1,0:T(8,128)(2,1)} %bitcast.18), calls=%async_computation.3 | async-start | bytes 1048576 | tf_op jit(solution)/shard_map/all_to_all | solution.py:632
  186.3 13.4 %copy-start.21 = (bf16[512,256]{1,0:T(8,128)(2,1)S(1)}, bf16[512,256]{1,0:T(8,128)(2,1)}, u32[]{:S(2)}) copy-start(bf16[512,256]{1,0:T(8,128)(2,1)} %copy-done.18) | copy-start | bytes 786436
  186.3 13.4 %copy-start.25 = (f32[4,256,128]{2,1,0:T(8,128)S(1)}, f32[4,256,128]{2,1,0:T(8,128)}, u32[]{:S(2)}) copy-start(f32[4,256,128]{2,1,0:T(8,128)} %copy-done.24) | copy-start | bytes 1572868
  190.6 7.7 %collective-permute-start.14 = (bf16[256,128]{1,0:T(8,128)(2,1)S(1)}, bf16[256,128]{1,0:T(8,128)(2,1)S(1)}, u32[]{:S(2)}, u32[]{:S(2)}) collective-permute-start(bf16[256,128]{1,0:T(8,128)(2,1)S(1)} %get-tuple-element.104), channel_id=1, source_target_pairs={{0,3},{1,2},{2,1},{3,0},{4,7},{5,6},{6,5},{7,4},{8,11},{9,10},{10,... | collective-permute-start | bytes 196616 | tf_op jit(solution)/shard_map/ppermute | solution.py:527
  192.9 6.8 %collective-permute-start.13 = (bf16[256,128]{1,0:T(8,128)(2,1)S(1)}, bf16[256,128]{1,0:T(8,128)(2,1)S(1)}, u32[]{:S(2)}, u32[]{:S(2)}) collective-permute-start(bf16[256,128]{1,0:T(8,128)(2,1)S(1)} %get-tuple-element.105), channel_id=1, source_target_pairs={{0,2},{1,3},{2,0},{3,1},{4,6},{5,7},{6,4},{7,5},{8,10},{9,11},{10,... | collective-permute-start | bytes 196616 | tf_op jit(solution)/shard_map/ppermute | solution.py:527
  195.8 3.9 %collective-permute-start.12 = (bf16[256,128]{1,0:T(8,128)(2,1)S(1)}, bf16[256,128]{1,0:T(8,128)(2,1)S(1)}, u32[]{:S(2)}, u32[]{:S(2)}) collective-permute-start(bf16[256,128]{1,0:T(8,128)(2,1)S(1)} %get-tuple-element.106), channel_id=1, source_target_pairs={{0,1},{1,0},{2,3},{3,2},{4,5},{5,4},{6,7},{7,6},{8,9},{9,8},{10,11... | collective-permute-start | bytes 196616 | tf_op jit(solution)/shard_map/ppermute | solution.py:527
  202.6 34.8 %all-to-all-start.2 = ((bf16[32,16,896]{2,1,0:T(8,128)(2,1)}), bf16[32,16,896]{2,1,0:T(8,128)(2,1)S(1)}, u32[]{:S(2)}, u32[]{:S(2)}) async-start(bf16[32,16,896]{2,1,0:T(8,128)(2,1)} %bitcast.16), calls=%async_computation.2 | async-start | bytes 1835008 | tf_op jit(solution)/shard_map/all_to_all | solution.py:702
  (33 other events, 49.7 us)
Sparse Core Ops, SparseCore 0:
  10.1 51.9 all-gather.4
  64.7 40.6 all-gather.2
  166.5 45.9 reduce-scatter.1

commit v2 on v1

--- a/solution.py
+++ b/solution.py
@@ -10,6 +10,7 @@
 
 GROUPS = 4
 DP_INNER = 4
+CORES = 2
 PANEL = 16
 LANES = 128
 FAR = -1e30
@@ -30,7 +31,7 @@
         in_specs=[smem] * scalars + [vmem] * (len(ins) - scalars),
         out_specs=[vmem] * len(outs),
         scratch_shapes=list(scratch),
-        compiler_params=pltpu.CompilerParams(vmem_limit_bytes=48 << 20),
+        compiler_params=pltpu.CompilerParams(vmem_limit_bytes=16 << 20),
         cost_estimate=pl.CostEstimate(
             flops=int(cost * 1e6), bytes_accessed=size, transcendentals=0
         ),
@@ -120,7 +121,25 @@
     return (lane_ids(shape) // head_width == row_ids(shape)).astype(f32)
 
 
-def pack_dout_body(co_ref, dout_ref, *d_refs):
+def pack_body(
+    bin_ref, slot_ref, co_ref, x_ref, z_ref, bc_ref, dt_ref, dout_ref, a_ref, *d_refs
+):
+    npan = bin_ref.shape[0]
+    channels = x_ref.shape[1]
+    pair = bc_ref.shape[1] // GROUPS
+    a_ref[...] = jnp.zeros_like(a_ref)
+    group = pl.multiple_of(co_ref[0] * pair, pair)
+    shape = (PANEL, LANES)
+    low, high = 2 * channels, 2 * channels + pair
+    for p in range(npan):
+        rows = slice(p * PANEL, (p + 1) * PANEL)
+        to = pl.ds(pl.multiple_of(bin_ref[p] * PANEL, PANEL), PANEL)
+        a_ref[to, 0:channels] = x_ref[rows, :]
+        a_ref[to, channels:low] = z_ref[rows, :]
+        a_ref[to, low:high] = bc_ref[rows, pl.ds(group, pair)]
+        label = (slot_ref[p] * PANEL + 1 + row_ids(shape)).astype(f32)
+        meta = jnp.where(lane_ids(shape) == LANES - 1, label, dt_ref[rows, :])
+        a_ref[to, high : high + LANES] = meta.astype(bf16)
     inner = len(d_refs)
     outer = dout_ref.shape[1] // (LANES * inner)
     for k in range(inner):
@@ -128,27 +147,6 @@
         for z in range(outer):
             low = pl.multiple_of((z * inner + block) * LANES, LANES)
             d_refs[k][:, z * LANES : (z + 1) * LANES] = dout_ref[:, pl.ds(low, LANES)]
-
-
-def pack_body(bin_ref, slot_ref, co_ref, x_ref, z_ref, bc_ref, dt_ref, a_ref, zs_ref):
-    npan = bin_ref.shape[0]
-    channels = x_ref.shape[1]
-    pair = bc_ref.shape[1] // GROUPS
-    heads = dt_ref.shape[1]
-    a_ref[...] = jnp.zeros_like(a_ref)
-    zs_ref[...] = jnp.zeros_like(zs_ref)
-    group = pl.multiple_of(co_ref[0] * pair, pair)
-    shape = (PANEL, LANES)
-    for p in range(npan):
-        rows = slice(p * PANEL, (p + 1) * PANEL)
-        to = pl.ds(pl.multiple_of(bin_ref[p] * PANEL, PANEL), PANEL)
-        a_ref[to, 0:channels] = x_ref[rows, :]
-        a_ref[to, channels : channels + pair] = bc_ref[rows, pl.ds(group, pair)]
-        label = (slot_ref[p] * PANEL + 1 + row_ids(shape)).astype(f32)
-        lanes = lane_ids(shape)
-        meta = jnp.where(lanes == LANES - 1, label, dt_ref[rows, :])
-        a_ref[to, channels + pair : channels + pair + LANES] = meta.astype(bf16)
-        zs_ref[to, :] = z_ref[rows, :]
 
 
 def forward_body(
@@ -173,13 +171,16 @@
     slope_ref,
     cum_ref,
     cumt_ref,
+    zb_ref,
+    gated_ref,
 ):
     rows, channels = xraw_ref.shape
     pair = bcact_ref.shape[1]
     state = pair // 2
     head_width = channels // heads
+    base = 2 * channels
     slots = recv_ref.shape[0]
-    label = recv_ref[:, channels + pair : channels + pair + LANES].astype(f32)[:, LANES - 1 :]
+    label = recv_ref[:, base + pair : base + pair + LANES].astype(f32)[:, LANES - 1 :]
     place = (label == (lane_ids((slots, rows)) + 1).astype(f32)).astype(bf16)
     pt_ref[...] = place
     raw = dot_tn(place, recv_ref[...])
@@ -189,7 +190,7 @@
     xpre = conv(xraw, cx_ref[...], keeps)
     xpre_ref[...] = xpre
     xact = xpre * jax.nn.sigmoid(xpre)
-    bcraw = raw[:, channels : channels + pair]
+    bcraw = raw[:, base : base + pair]
     share = share_ref.shape[2] // 2
     for s in range(share_ref.shape[0]):
         tile = bcraw[:, (s // 2) * LANES : (s // 2 + 1) * LANES]
@@ -203,7 +204,7 @@
     scores = dot_nt(bcact[:, state:], bcact[:, :state])
     scores_ref[...] = scores
     mask = seen_mask(len_ref, rows)
-    dt = raw[:, channels + pair : channels + pair + LANES] + bias_ref[...]
+    dt = raw[:, base + pair : base + pair + LANES] + bias_ref[...]
     real = lane_ids(dt.shape) < heads
     step = jnp.where(real, jnp.maximum(dt, 0.0) + jnp.log1p(jnp.exp(-jnp.abs(dt))), 0.0)
     step_ref[...] = step
@@ -225,73 +226,82 @@
             part = jnp.where(low if half == 0 else ~low, tile, jnp.zeros_like(tile))
             total = total + dot_nn(weights, part)
         mixed_ref[:, p * LANES : (p + 1) * LANES] = total
-
-
-def gate_body(recv_ref, pt_ref, mixed_ref, zb_ref, gated_ref, sums_ref):
-    z = dot_tn(pt_ref[...], recv_ref[...])
+    z = raw[:, channels:base]
     zb_ref[...] = z.astype(bf16)
-    gated = mixed_ref[...] * (z * jax.nn.sigmoid(z))
-    gated_ref[...] = gated
-    ones = jnp.ones((8, gated.shape[1]), f32)
-    sums_ref[...] = dot_nt(ones, gated * gated, exact)
+    gated_ref[...] = mixed_ref[...] * (z * jax.nn.sigmoid(z))
 
 
 def as_column(parts):
     total = parts[0][...]
     for part in parts[1:]:
         total = total + part[...]
-    return dot_tn(total, jnp.full((8, LANES), 0.125, f32), exact)
-
-
-def norm_body(size, gated_ref, gain_ref, *refs):
-    parts, (normed_ref, inv_ref) = refs[:-2], refs[-2:]
-    inverse = lax.rsqrt(as_column(parts) / size + 1e-05)
-    inv_ref[...] = inverse
-    normed = gated_ref[...] * inverse[:, :1] * gain_ref[...]
-    normed_ref[...] = normed.astype(bf16)
-
-
-def rows_of(out_ref, k):
-    tensor, _, panel, columns = out_ref.shape
-    return out_ref[:, k].reshape(tensor * panel, columns)
-
-
-def dnormed_body(out_ref, w_ref, *p_refs):
+    eighth = jnp.full((8, LANES), 0.125, f32)
+    return dot_tn(total[:8], eighth, exact), dot_tn(total[8:], eighth, exact)
+
+
+def collect_body(co_ref, *refs):
+    blocks, half_ref = refs[:-1], refs[-1]
+    count = len(blocks)
+    for k, block in enumerate(blocks):
+        half_ref[lax.rem(co_ref[3] + count - k, count)] = block[...]
+
+
+def rows_of(co_ref, mine_ref, other_ref, k):
+    mine, other = mine_ref[:, k], other_ref[:, k]
+    first = co_ref[4] == 0
+    both = jnp.stack([jnp.where(first, mine, other), jnp.where(first, other, mine)], axis=1)
+    return both.reshape(-1, both.shape[3])
+
+
+def dnormed_body(co_ref, mine_ref, other_ref, w_ref, *refs):
+    p_refs, rows_ref = refs[:-1], refs[-1]
     w = jnp.concatenate([w_ref[z] for z in range(w_ref.shape[0])], axis=1)
     for k, p_ref in enumerate(p_refs):
-        p_ref[...] = dot_nt(rows_of(out_ref, k), w).astype(p_ref.dtype)
-
-
-def term_body(scale, out_ref, *refs):
-    normed, term_ref = refs[:-1], refs[-1]
+        rows = rows_of(co_ref, mine_ref, other_ref, k)
+        rows_ref[k] = rows
+        p_ref[...] = dot_nt(rows, w).astype(p_ref.dtype)
+
+
+def term_body(scale, co_ref, rows_ref, *refs):
+    count = rows_ref.shape[0]
+    normed, terms, total_ref = refs[:count], refs[count:-1], refs[-1]
     total = None
     for k, normed_ref in enumerate(normed):
-        part = dot_tn(normed_ref[...], rows_of(out_ref, k))
+        part = dot_tn(normed_ref[...], rows_ref[k])
         total = part if total is None else total + part
-    total = (total * scale).astype(bf16)
-    for z in range(term_ref.shape[0]):
-        term_ref[z] = total[:, z * LANES : (z + 1) * LANES]
-
-
-def cross_body(gated_ref, inv_ref, gain_ref, *refs):
-    parts, (weighted_ref, dgain_ref, sums_ref) = refs[:-3], refs[-3:]
+    total_ref[...] = total * scale
+    outer = len(terms)
+    for k, term_ref in enumerate(terms):
+        block = lax.rem(co_ref[5] + outer - k, outer)
+        low = pl.multiple_of(block * LANES, LANES)
+        term_ref[...] = total_ref[:, pl.ds(low, LANES)].astype(bf16)
+
+
+def cross_body(gated_ref, gain_ref, *refs):
+    parts, (dnormed_ref, sums_ref) = refs[:-2], refs[-2:]
     dnormed = parts[0][...].astype(f32)
     for part in parts[1:]:
         dnormed = dnormed + part[...].astype(f32)
+    dnormed_ref[...] = dnormed
     gated = gated_ref[...]
-    product = dnormed * gated
-    dgain_ref[...] = jnp.sum(product * inv_ref[:, :1], axis=0, keepdims=True)
-    weighted = dnormed * gain_ref[...]
-    weighted_ref[...] = weighted
     ones = jnp.ones((8, gated.shape[1]), f32)
-    sums_ref[...] = dot_nt(ones, product * gain_ref[...], exact)
-
-
-def dz_body(size, weighted_ref, gated_ref, mixed_ref, zb_ref, inv_ref, pt_ref, *refs):
-    parts, (dy_ref, back_ref) = refs[:-2], refs[-2:]
-    inverse = inv_ref[...]
-    factor = (inverse * inverse * inverse * as_column(parts) / size)[:, :1]
-    dgated = inverse[:, :1] * weighted_ref[...] - gated_ref[...] * factor
+    sums_ref[:8] = dot_nt(ones, gated * gated, exact)
+    sums_ref[8:] = dot_nt(ones, dnormed * gated * gain_ref[...], exact)
+
+
+def dz_body(size, dnormed_ref, gain_ref, gated_ref, mixed_ref, zb_ref, pt_ref, *refs):
+    parts, (normed_ref, dgain_ref, dy_ref, back_ref) = refs[:-4], refs[-4:]
+    squares, crossing = as_column(parts)
+    inverse = lax.rsqrt(squares / size + 1e-05)
+    factor = (inverse * inverse * inverse * crossing / size)[:, :1]
+    inverse = inverse[:, :1]
+    gain = gain_ref[...]
+    gated = gated_ref[...]
+    dnormed = dnormed_ref[...]
+    scaled = gated * inverse
+    normed_ref[...] = (scaled * gain).astype(bf16)
+    dgain_ref[...] = jnp.sum(dnormed * scaled, axis=0, keepdims=True)
+    dgated = inverse * (dnormed * gain) - gated * factor
     z = zb_ref[...].astype(f32)
     sig = jax.nn.sigmoid(z)
     dy_ref[...] = dgated * (z * sig)
@@ -513,7 +523,10 @@
     scale = 1.0 / math.sqrt(rows * dp)
     columns = outer * LANES
 
-    coords = jnp.stack([group, x_index, local]).astype(jnp.int32)
+    z_index = lax.axis_index("dp") // inner
+    coords = jnp.stack(
+        [group, x_index, local, t_index // CORES, t_index % CORES, z_index]
+    ).astype(jnp.int32)
     over_z = [[z * inner + x for z in range(outer)] for x in range(inner)]
 
     def along_x(block, shift):
@@ -523,37 +536,51 @@
                 route.append((z * inner + x, z * inner + (x + shift) % inner))
         return lax.ppermute(block, "dp", route)
 
+    def along_z(block, shift):
+        route = [(d, (d + shift * inner) % dp) for d in range(dp)]
+        return lax.ppermute(block, "dp", route)
+
+    def along_y(block, shift):
+        route = [(t, (t + shift * CORES) % tensor) for t in range(tensor)]
+        return lax.ppermute(block, "tensor", route)
+
     def partner(block, flip):
         return lax.ppermute(block, "tensor", [(t, t ^ flip) for t in range(tensor)])
 
     def in_group(block):
         return [block] + [partner(block, flip) for flip in range(1, members)]
 
-    d_parts = call(
-        pack_dout_body,
-        [shaped((dout.shape[0], columns), bf16)] * inner,
-        [coords, dout],
-        scalars=1,
-        name="pack_dout",
-    )
-    d_own = [d_parts[0]] + [along_x(d_parts[k], k) for k in range(1, inner)]
-    out_rows = lax.all_gather(jnp.concatenate(d_own, axis=0), "tensor", axis=0, tiled=True)
-    out_rows = out_rows.reshape(tensor, inner, dout.shape[0], columns)
     w_cols = lax.all_gather(
         w_out, "dp", axis=0, tiled=True, axis_index_groups=over_z
     ).reshape(outer, channels, LANES)
 
     dt_wide = jnp.pad(dt_in.astype(f32), ((0, 0), (0, LANES - heads)))
-    first = channels + pair + LANES
-    send_a, send_z = call(
+    packed = call(
         pack_body,
-        [shaped((slots, first), bf16), shaped((slots, channels), bf16)],
-        [panel_bin, panel_slot, coords, x_in, z_in, bc_in, dt_wide],
+        [shaped((slots, 2 * channels + pair + LANES), bf16)]
+        + [shaped((dout.shape[0], columns), bf16)] * inner,
+        [panel_bin, panel_slot, coords, x_in, z_in, bc_in, dt_wide, dout],
         scalars=3,
         name="pack",
     )
-    recv_a = lax.all_to_all(send_a, "dp", split_axis=0, concat_axis=0, tiled=True)
-    recv_z = lax.all_to_all(send_z, "dp", split_axis=0, concat_axis=0, tiled=True)
+    send, d_parts = packed[0], packed[1:]
+    recv = lax.all_to_all(send, "dp", split_axis=0, concat_axis=0, tiled=True)
+
+    d_own = jnp.stack([d_parts[0]] + [along_x(d_parts[k], k) for k in range(1, inner)])
+    ring_y = tensor // CORES
+    ups, downs = [d_own], []
+    for step in range(1, ring_y // 2 + 1):
+        ups.append(along_y(ups[-1], 1))
+        if step < ring_y - ring_y // 2:
+            downs.append(along_y(downs[-1] if downs else d_own, -1))
+    (mine,) = call(
+        collect_body,
+        [shaped((ring_y,) + d_own.shape, bf16)],
+        [coords] + ups + downs[::-1],
+        scalars=1,
+        name="collect",
+    )
+    other = partner(mine, 1)
 
     bias_row = jnp.pad(dt_bias, (0, LANES - heads))[None, :]
     alog_row = jnp.pad(a_log, (0, LANES - heads))[None, :]
@@ -564,7 +591,21 @@
         ((0, 0), (0, LANES - share)),
     )
 
-    place, xraw, xpre, mixed, raw_share, bcact, scores, step, slope, cum, cumt = call(
+    (
+        place,
+        xraw,
+        xpre,
+        mixed,
+        raw_share,
+        bcact,
+        scores,
+        step,
+        slope,
+        cum,
+        cumt,
+        zb,
+        gated,
+    ) = call(
         functools.partial(forward_body, width, heads),
         [
             shaped((slots, rows), bf16),
@@ -578,74 +619,71 @@
             shaped((rows, LANES), f32),
             shaped((rows, LANES), f32),
             shaped((8, rows), f32),
+            shaped((rows, channels), bf16),
+            shaped((rows, channels), f32),
         ],
-        [lengths, coords, recv_a, conv_x, conv_bc, bias_row, alog_row, skip_row],
+        [lengths, coords, recv, conv_x, conv_bc, bias_row, alog_row, skip_row],
         scalars=2,
         cost=4000,
         name="forward",
     )
-    zb, gated, squares = call(
-        gate_body,
+
+    partial = call(
+        dnormed_body,
+        [shaped((rows, channels), f32)]
+        + [shaped((rows, channels), bf16)] * (inner - 1)
+        + [shaped((inner, rows, columns), bf16)],
+        [coords, mine, other, w_cols],
+        scalars=1,
+        cost=1200,
+        name="dnormed",
+    )
+    partial, out_rows = partial[:-1], partial[-1]
+    d_terms = [partial[0]] + [along_x(partial[k], -k) for k in range(1, inner)]
+    dnormed, sums = call(
+        cross_body,
+        [shaped((rows, channels), f32), shaped((16, rows), f32)],
+        [gated, gain_row] + d_terms,
+        cost=500,
+        name="cross",
+    )
+    normed, dgain, dy, back_z = call(
+        functools.partial(dz_body, size),
         [
             shaped((rows, channels), bf16),
+            shaped((1, channels), f32),
             shaped((rows, channels), f32),
-            shaped((8, rows), f32),
+            shaped((slots, channels), bf16),
         ],
-        [recv_z, place, mixed],
-        cost=1000,
-        name="gate",
-    )
-    normed, inverse = call(
-        functools.partial(norm_body, size),
-        [shaped((rows, channels), bf16), shaped((rows, LANES), f32)],
-        [gated, gain_row] + in_group(squares),
-        cost=500,
-        name="norm",
-    )
-
-    partial = call(
-        dnormed_body,
-        [shaped((rows, channels), f32)] + [shaped((rows, channels), bf16)] * (inner - 1),
-        [out_rows, w_cols],
-        cost=1200,
-        name="dnormed",
-    )
-    d_terms = [partial[0]] + [along_x(partial[k], -k) for k in range(1, inner)]
-    weighted, dgain, crossing = call(
-        cross_body,
-        [
-            shaped((rows, channels), f32),
-            shaped((1, channels), f32),
-            shaped((8, rows), f32),
-        ],
-        [gated, inverse, gain_row] + d_terms,
-        cost=500,
-        name="cross",
-    )
-    dy, back_z = call(
-        functools.partial(dz_body, size),
-        [shaped((rows, channels), f32), shaped((slots, channels), bf16)],
-        [weighted, gated, mixed, zb, inverse, place] + in_group(crossing),
+        [dnormed, gain_row, gated, mixed, zb, place] + in_group(sums),
         cost=1000,
         name="dz",
     )
     home_z = lax.all_to_all(back_z, "dp", split_axis=0, concat_axis=0, tiled=True)
 
     normed_all = [normed] + [along_x(normed, k) for k in range(1, inner)]
-    (term,) = call(
+    terms = call(
         functools.partial(term_body, scale),
-        [shaped((outer, channels, LANES), bf16)],
-        [out_rows] + normed_all,
+        [shaped((channels, LANES), bf16)] * outer,
+        [coords, out_rows] + normed_all,
+        scalars=1,
         cost=1200,
+        scratch=[pltpu.VMEM((channels, columns), f32)],
         name="term",
     )
-    grad_wout = lax.psum_scatter(
-        term.reshape(outer * channels, LANES),
-        "dp",
-        scatter_dimension=0,
-        axis_index_groups=over_z,
-        tiled=True,
-    )
+
+    def add(moved, term):
+        return (moved.astype(f32) + term.astype(f32)).astype(bf16)
+
+    far = outer // 2
+    down, up = terms[far], terms[far + 1]
+    for k in range(far - 1, 0, -1):
+        down = add(along_z(down, -1), terms[k])
+    for k in range(far + 2, outer):
+        up = add(along_z(up, 1), terms[k])
+    grad_wout = (
+        along_z(down, -1).astype(f32) + along_z(up, 1).astype(f32) + terms[0].astype(f32)
+    ).astype(bf16)
 
     gx, dcx, ddt, dheads, pieces = call(
         functools.partial(backward_body, width, heads),

time: 248 us -> 233 us (0.940)
  the two profiles are of different devices: /device:TPU:2 before, /device:TPU:238 now
where the time goes in v2:
time: 233 us; the launch traced here: 232 us
  starting transfers between devices  119 us (51%)
  waiting for transfers between devices  52.7 us (23%)
  local copies, waits for them, and re-layouts  23 us (10%)
  Pallas kernels  21.5 us (9%)
  between operations  14.8 us (6%)
    ppermute x9, starting transfers between devices, along_x(): return lax.ppermute(block, 'dp', route)  26.3 us
    ppermute x7, waiting for transfers between devices, along_z(): return lax.ppermute(block, 'dp', route)  23.5 us
    ppermute x7, starting transfers between devices, along_z(): return lax.ppermute(block, 'dp', route)  23.1 us
    unnamed x77, local copies, waits for them, and re-layouts  22 us
    pallas_call x11, Pallas kernels, call(): pl.pallas_call(body, out_shape=outs, in_specs=[smem] * scalars + [vmem] *...  21.5 us
    ppermute x7, starting transfers between devices, along_y(): return lax.ppermute(block, 'tensor', route)  21.2 us
    ppermute x7, starting transfers between devices, partner(): return lax.ppermute(block, 'tensor', [(t, t ^ flip) for t in range(tensor)])  18.1 us
    ppermute x9, waiting for transfers between devices, along_x(): return lax.ppermute(block, 'dp', route)  11.8 us
  transfers between devices with their start and end apart: 34, of which 16 were waited for; matrix products, arithmetic and copies ran while one was open for 1% of the time, Pallas kernels for 7%

profile of v2, /device:TPU:238, one launch (start us, length us, event | category | flops | bytes accessed | tf_op | source)
XLA Modules:
  0.0 231.8 jit_solution(773049491848511205)
XLA Ops:
  15.2 10.7 %all-to-all-start = ((bf16[32,16,1408]{2,1,0:T(8,128)(2,1)}), bf16[32,16,1408]{2,1,0:T(8,128)(2,1)S(1)}, u32[]{:S(2)}, u32[]{:S(2)}) async-start(bf16[32,16,1408]{2,1,0:T(8,128)(2,1)} %bitcast.6), calls=%async_computation | async-start | bytes 2883584 | tf_op jit(solution)/shard_map/all_to_all | solution.py:567
  26.7 2.5 %collective-permute-start = (bf16[16,1024]{1,0:T(8,128)(2,1)S(1)}, bf16[16,1024]{1,0:T(8,128)(2,1)S(1)}, u32[]{:S(2)}, u32[]{:S(2)}) collective-permute-start(bf16[16,1024]{1,0:T(8,128)(2,1)S(1)} %get-tuple-element.62), channel_id=1, source_target_pairs={{0,16},{16,32},{32,48},{48,0},{64,80},{80,96},{96,112},{112,64},{1... | collective-permute-start | bytes 98312 | tf_op jit(solution)/shard_map/ppermute | solution.py:537
  29.1 4.3 %collective-permute-start.1 = (bf16[16,1024]{1,0:T(8,128)(2,1)S(1)}, bf16[16,1024]{1,0:T(8,128)(2,1)S(1)}, u32[]{:S(2)}, u32[]{:S(2)}) collective-permute-start(bf16[16,1024]{1,0:T(8,128)(2,1)S(1)} %get-tuple-element.63), channel_id=1, source_target_pairs={{0,32},{16,48},{32,0},{48,16},{64,96},{80,112},{96,64},{112,80},{1... | collective-permute-start | bytes 98312 | tf_op jit(solution)/shard_map/ppermute | solution.py:537
  36.6 4.0 %collective-permute-done.2 = bf16[16,1024]{1,0:T(8,128)(2,1)S(1)} collective-permute-done((bf16[16,1024]{1,0:T(8,128)(2,1)S(1)}, bf16[16,1024]{1,0:T(8,128)(2,1)S(1)}, u32[]{:S(2)}, u32[]{:S(2)}) %collective-permute-start.2) | collective-permute-done | bytes 32800 | tf_op jit(solution)/shard_map/ppermute | solution.py:537
  40.7 2.6 %collective-permute-start.3 = (bf16[4,16,1024]{2,1,0:T(8,128)(2,1)S(1)}, bf16[4,16,1024]{2,1,0:T(8,128)(2,1)S(1)}, u32[]{:S(2)}, u32[]{:S(2)}) collective-permute-start(bf16[4,16,1024]{2,1,0:T(8,128)(2,1)S(1)} %pad_maximum_fusion.refs_0_), channel_id=1, source_target_pairs={{0,2},{1,3},{2,4},{3,5},{4,6},{5,7},{6,8},{7,9},{8,10},{9,11},{10,... | collective-permute-start | bytes 393224 | tf_op jit(solution)/shard_map/ppermute | solution.py:545
  43.3 3.3 %collective-permute-start.7 = (bf16[4,16,1024]{2,1,0:T(8,128)(2,1)S(1)}, bf16[4,16,1024]{2,1,0:T(8,128)(2,1)S(1)}, u32[]{:S(2)}, u32[]{:S(2)}) collective-permute-start(bf16[4,16,1024]{2,1,0:T(8,128)(2,1)S(1)} %pad_maximum_fusion.refs_0_), channel_id=1, source_target_pairs={{0,14},{1,15},{2,0},{3,1},{4,2},{5,3},{6,4},{7,5},{8,6},{9,7},{10,... | collective-permute-start | bytes 393224 | tf_op jit(solution)/shard_map/ppermute | solution.py:545
  47.6 2.6 %collective-permute-start.4 = (bf16[4,16,1024]{2,1,0:T(8,128)(2,1)S(1)}, bf16[4,16,1024]{2,1,0:T(8,128)(2,1)S(1)}, u32[]{:S(2)}, u32[]{:S(2)}) collective-permute-start(bf16[4,16,1024]{2,1,0:T(8,128)(2,1)S(1)} %collective-permute-done.3.refs_1_), channel_id=1, source_target_pairs={{0,2},{1,3},{2,4},{3,5},{4,6},{5,7},{6,8},{7,9},{8,10},{9,11},{10,... | collective-permute-start | bytes 393224 | tf_op jit(solution)/shard_map/ppermute | solution.py:545
  50.2 3.8 %collective-permute-start.8 = (bf16[4,16,1024]{2,1,0:T(8,128)(2,1)S(1)}, bf16[4,16,1024]{2,1,0:T(8,128)(2,1)S(1)}, u32[]{:S(2)}, u32[]{:S(2)}) collective-permute-start(bf16[4,16,1024]{2,1,0:T(8,128)(2,1)S(1)} %collective-permute-done.7.refs_7_), channel_id=1, source_target_pairs={{0,14},{1,15},{2,0},{3,1},{4,2},{5,3},{6,4},{7,5},{8,6},{9,7},{10,... | collective-permute-start | bytes 393224 | tf_op jit(solution)/shard_map/ppermute | solution.py:545
  57.0 5.0 %collective-permute-start.9 = (bf16[4,16,1024]{2,1,0:T(8,128)(2,1)S(1)}, bf16[4,16,1024]{2,1,0:T(8,128)(2,1)S(1)}, u32[]{:S(2)}, u32[]{:S(2)}) collective-permute-start(bf16[4,16,1024]{2,1,0:T(8,128)(2,1)S(1)} %collective-permute-done.8.refs_6_), channel_id=1, source_target_pairs={{0,14},{1,15},{2,0},{3,1},{4,2},{5,3},{6,4},{7,5},{8,6},{9,7},{10,... | collective-permute-start | bytes 393224 | tf_op jit(solution)/shard_map/ppermute | solution.py:545
  64.9 6.1 %collective-permute-done.6.refs_4_ = bf16[4,16,1024]{2,1,0:T(8,128)(2,1)S(1)} collective-permute-done((bf16[4,16,1024]{2,1,0:T(8,128)(2,1)S(1)}, bf16[4,16,1024]{2,1,0:T(8,128)(2,1)S(1)}, u32[]{:S(2)}, u32[]{:S(2)}) %collective-permute-start.6) | collective-permute-done | bytes 131104 | tf_op jit(solution)/shard_map/ppermute | solution.py:545
  85.6 3.7 %collective-permute-start.12 = (bf16[256,512]{1,0:T(8,128)(2,1)S(1)}, bf16[256,512]{1,0:T(8,128)(2,1)S(1)}, u32[]{:S(2)}, u32[]{:S(2)}) collective-permute-start(bf16[256,512]{1,0:T(8,128)(2,1)S(1)} %get-tuple-element.67), channel_id=1, source_target_pairs={{0,32},{16,48},{32,0},{48,16},{64,96},{80,112},{96,64},{112,80},{1... | collective-permute-start | bytes 786440 | tf_op jit(solution)/shard_map/ppermute | solution.py:537
  89.3 3.4 %collective-permute-start.13 = (bf16[256,512]{1,0:T(8,128)(2,1)S(1)}, bf16[256,512]{1,0:T(8,128)(2,1)S(1)}, u32[]{:S(2)}, u32[]{:S(2)}) collective-permute-start(bf16[256,512]{1,0:T(8,128)(2,1)S(1)} %get-tuple-element.68), channel_id=1, source_target_pairs={{0,16},{16,32},{32,48},{48,0},{64,80},{80,96},{96,112},{112,64},{1... | collective-permute-start | bytes 786440 | tf_op jit(solution)/shard_map/ppermute | solution.py:537
  92.7 3.2 %forward.1 = (bf16[512,256]{1,0:T(8,128)(2,1)S(1)}, bf16[256,512]{1,0:T(8,128)(2,1)S(1)}, f32[256,512]{1,0:T(8,128)S(1)}, f32[256,512]{1,0:T(8,128)S(1)}, f32[4,...) custom-call(s32[1,6]{1,0:T(1,128)S(1)} %copy-done.13, ...), custom_call_target="tpu_custom_call" | custom-call | flops 4000000000 | bytes 5147696 | tf_op jit(solution)/shard_map/forward/pallas_call | solution.py:28
  96.8 4.0 %collective-permute-done.11.refs_1_ = bf16[256,512]{1,0:T(8,128)(2,1)S(1)} collective-permute-done((bf16[256,512]{1,0:T(8,128)(2,1)S(1)}, bf16[256,512]{1,0:T(8,128)(2,1)S(1)}, u32[]{:S(2)}, u32[]{:S(2)}) %collective-permute-start.11) | collective-permute-done | bytes 262176 | tf_op jit(solution)/shard_map/ppermute | solution.py:537
  100.7 2.5 %collective-permute-done.13.refs_3_ = bf16[256,512]{1,0:T(8,128)(2,1)S(1)} collective-permute-done((bf16[256,512]{1,0:T(8,128)(2,1)S(1)}, bf16[256,512]{1,0:T(8,128)(2,1)S(1)}, u32[]{:S(2)}, u32[]{:S(2)}) %collective-permute-start.13) | collective-permute-done | bytes 262176 | tf_op jit(solution)/shard_map/ppermute | solution.py:537
  106.2 5.1 %collective-permute-start.15 = (f32[16,256]{1,0:T(8,128)S(1)}, f32[16,256]{1,0:T(8,128)S(1)}, u32[]{:S(2)}, u32[]{:S(2)}) collective-permute-start(f32[16,256]{1,0:T(8,128)S(1)} %get-tuple-element.73.refs_0_), channel_id=1, source_target_pairs={{0,2},{1,3},{2,0},{3,1},{4,6},{5,7},{6,4},{7,5},{8,10},{9,11},{10,... | collective-permute-start | bytes 49160 | tf_op jit(solution)/shard_map/ppermute | solution.py:548
  113.4 3.0 %collective-permute-done.16.refs_3_ = f32[16,256]{1,0:T(8,128)S(1)} collective-permute-done((f32[16,256]{1,0:T(8,128)S(1)}, f32[16,256]{1,0:T(8,128)S(1)}, u32[]{:S(2)}, u32[]{:S(2)}) %collective-permute-start.16) | collective-permute-done | bytes 16416 | tf_op jit(solution)/shard_map/ppermute | solution.py:548
  118.3 9.5 %all-to-all-start.2 = ((bf16[32,16,512]{2,1,0:T(8,128)(2,1)}), bf16[32,16,512]{2,1,0:T(8,128)(2,1)S(1)}, u32[]{:S(2)}, u32[]{:S(2)}) async-start(bf16[32,16,512]{2,1,0:T(8,128)(2,1)} %bitcast.22), calls=%async_computation.2 | async-start | bytes 1048576 | tf_op jit(solution)/shard_map/all_to_all | solution.py:662
  134.5 4.3 %backward.1 = (bf16[256,512]{1,0:T(8,128)(2,1)S(1)}, f32[4,512]{1,0:T(4,128)S(1)}, f32[256,128]{1,0:T(8,128)S(1)}, f32[3,128]{1,0:T(4,128)S(1)}, bf16[4,256,128]{2,1,0:T(8,128)(2,1)S(1)}) custom-call(s32[1,6]{1,0:T(1,128)S(1)} %copy-done.13, s32[6]{0:T(128)S(1)} %stack.42.co_ref, f32[256,512]{1,0:T(8,128)S(1)} %get-tuple-element.74.dy_ref, ...), custom_call_target="tpu_custom_call" | custom-call | flops 6000000000 | bytes 3305520 | tf_op jit(solution)/shard_map/backward/pallas_call | solution.py:28
  140.8 2.5 %collective-permute-start.20 = (bf16[256,512]{1,0:T(8,128)(2,1)S(1)}, bf16[256,512]{1,0:T(8,128)(2,1)S(1)}, u32[]{:S(2)}, u32[]{:S(2)}) collective-permute-start(bf16[256,512]{1,0:T(8,128)(2,1)S(1)} %get-tuple-element.94.refs_0_), channel_id=1, source_target_pairs={{0,16},{16,32},{32,48},{48,0},{64,80},{80,96},{96,112},{112,64},{1... | collective-permute-start | bytes 786440 | tf_op jit(solution)/shard_map/ppermute | solution.py:537
  143.3 4.3 %collective-permute-start.21 = (bf16[256,512]{1,0:T(8,128)(2,1)S(1)}, bf16[256,512]{1,0:T(8,128)(2,1)S(1)}, u32[]{:S(2)}, u32[]{:S(2)}) collective-permute-start(bf16[256,512]{1,0:T(8,128)(2,1)S(1)} %get-tuple-element.94.refs_0_), channel_id=1, source_target_pairs={{0,32},{16,48},{32,0},{48,16},{64,96},{80,112},{96,64},{112,80},{1... | collective-permute-start | bytes 786440 | tf_op jit(solution)/shard_map/ppermute | solution.py:537
  149.5 2.1 collective-permute-start.18
  151.6 3.0 %collective-permute-start.19 = (bf16[256,128]{1,0:T(8,128)(2,1)S(1)}, bf16[256,128]{1,0:T(8,128)(2,1)S(1)}, u32[]{:S(2)}, u32[]{:S(2)}) collective-permute-start(bf16[256,128]{1,0:T(8,128)(2,1)S(1)} %get-tuple-element.116), channel_id=1, source_target_pairs={{0,3},{1,2},{2,1},{3,0},{4,7},{5,6},{6,5},{7,4},{8,11},{9,10},{10,... | collective-permute-start | bytes 196616 | tf_op jit(solution)/shard_map/ppermute | solution.py:548
  157.5 2.2 share.1
  159.7 10.0 %all-to-all-start.1 = ((bf16[32,16,896]{2,1,0:T(8,128)(2,1)}), bf16[32,16,896]{2,1,0:T(8,128)(2,1)S(1)}, u32[]{:S(2)}, u32[]{:S(2)}) async-start(bf16[32,16,896]{2,1,0:T(8,128)(2,1)} %bitcast.20), calls=%async_computation.1 | async-start | bytes 1835008 | tf_op jit(solution)/shard_map/all_to_all | solution.py:740
  171.3 2.1 term.1
  173.4 2.5 %collective-permute-start.23 = (bf16[512,128]{1,0:T(8,128)(2,1)S(1)}, bf16[512,128]{1,0:T(8,128)(2,1)S(1)}, u32[]{:S(2)}, u32[]{:S(2)}) collective-permute-start(bf16[512,128]{1,0:T(8,128)(2,1)S(1)} %get-tuple-element.95), channel_id=1, source_target_pairs={{0,448},{16,464},{32,480},{48,496},{64,0},{80,16},{96,32},{112,48}... | collective-permute-start | bytes 393224 | tf_op jit(solution)/shard_map/ppermute | solution.py:541
  175.9 4.6 %collective-permute-start.27 = (bf16[512,128]{1,0:T(8,128)(2,1)S(1)}, bf16[512,128]{1,0:T(8,128)(2,1)S(1)}, u32[]{:S(2)}, u32[]{:S(2)}) collective-permute-start(bf16[512,128]{1,0:T(8,128)(2,1)S(1)} %get-tuple-element.99), channel_id=1, source_target_pairs={{0,64},{16,80},{32,96},{48,112},{64,128},{80,144},{96,160},{112,17... | collective-permute-start | bytes 393224 | tf_op jit(solution)/shard_map/ppermute | solution.py:541
  180.5 15.2 %collective-permute-done.23 = bf16[512,128]{1,0:T(8,128)(2,1)S(1)} collective-permute-done((bf16[512,128]{1,0:T(8,128)(2,1)S(1)}, bf16[512,128]{1,0:T(8,128)(2,1)S(1)}, u32[]{:S(2)}, u32[]{:S(2)}) %collective-permute-start.23) | collective-permute-done | bytes 131104 | tf_op jit(solution)/shard_map/ppermute | solution.py:541
  197.7 5.1 %collective-permute-start.28 = (bf16[512,128]{1,0:T(8,128)(2,1)S(1)}, bf16[512,128]{1,0:T(8,128)(2,1)S(1)}, u32[]{:S(2)}, u32[]{:S(2)}) collective-permute-start(bf16[512,128]{1,0:T(8,128)(2,1)S(1)} %add_convert_fusion.2), channel_id=1, source_target_pairs={{0,64},{16,80},{32,96},{48,112},{64,128},{80,144},{96,160},{112,17... | collective-permute-start | bytes 393224 | tf_op jit(solution)/shard_map/ppermute | solution.py:541
  206.1 5.1 %collective-permute-start.29 = (bf16[512,128]{1,0:T(8,128)(2,1)S(1)}, bf16[512,128]{1,0:T(8,128)(2,1)S(1)}, u32[]{:S(2)}, u32[]{:S(2)}) collective-permute-start(bf16[512,128]{1,0:T(8,128)(2,1)S(1)} %add_convert_fusion.1), channel_id=1, source_target_pairs={{0,64},{16,80},{32,96},{48,112},{64,128},{80,144},{96,160},{112,17... | collective-permute-start | bytes 393224 | tf_op jit(solution)/shard_map/ppermute | solution.py:541
  214.1 6.1 %collective-permute-done.26 = bf16[512,128]{1,0:T(8,128)(2,1)S(1)} collective-permute-done((bf16[512,128]{1,0:T(8,128)(2,1)S(1)}, bf16[512,128]{1,0:T(8,128)(2,1)S(1)}, u32[]{:S(2)}, u32[]{:S(2)}) %collective-permute-start.26) | collective-permute-done | bytes 131104 | tf_op jit(solution)/shard_map/ppermute | solution.py:541
  (140 shorter events, 68.8 us)
Async XLA Ops:
  15.2 77.4 %all-to-all-start = ((bf16[32,16,1408]{2,1,0:T(8,128)(2,1)}), bf16[32,16,1408]{2,1,0:T(8,128)(2,1)S(1)}, u32[]{:S(2)}, u32[]{:S(2)}) async-start(bf16[32,16,1408]{2,1,0:T(8,128)(2,1)} %bitcast.6), calls=%async_computation | async-start | bytes 2883584 | tf_op jit(solution)/shard_map/all_to_all | solution.py:567
  25.9 51.3 %all-gather.2.cloned.1.call-start = ((), (), s32[]{:S(2)}) async-start(), calls=%async_computation.3 | async-start | bytes 1179648 | tf_op jit(solution)/shard_map/all_gather | solution.py:553
  26.7 8.7 %collective-permute-start = (bf16[16,1024]{1,0:T(8,128)(2,1)S(1)}, bf16[16,1024]{1,0:T(8,128)(2,1)S(1)}, u32[]{:S(2)}, u32[]{:S(2)}) collective-permute-start(bf16[16,1024]{1,0:T(8,128)(2,1)S(1)} %get-tuple-element.62), channel_id=1, source_target_pairs={{0,16},{16,32},{32,48},{48,0},{64,80},{80,96},{96,112},{112,64},{1... | collective-permute-start | bytes 98312 | tf_op jit(solution)/shard_map/ppermute | solution.py:537
  29.1 7.5 %collective-permute-start.1 = (bf16[16,1024]{1,0:T(8,128)(2,1)S(1)}, bf16[16,1024]{1,0:T(8,128)(2,1)S(1)}, u32[]{:S(2)}, u32[]{:S(2)}) collective-permute-start(bf16[16,1024]{1,0:T(8,128)(2,1)S(1)} %get-tuple-element.63), channel_id=1, source_target_pairs={{0,32},{16,48},{32,0},{48,16},{64,96},{80,112},{96,64},{112,80},{1... | collective-permute-start | bytes 98312 | tf_op jit(solution)/shard_map/ppermute | solution.py:537
  33.4 7.3 %collective-permute-start.2 = (bf16[16,1024]{1,0:T(8,128)(2,1)S(1)}, bf16[16,1024]{1,0:T(8,128)(2,1)S(1)}, u32[]{:S(2)}, u32[]{:S(2)}) collective-permute-start(bf16[16,1024]{1,0:T(8,128)(2,1)S(1)} %get-tuple-element.64), channel_id=1, source_target_pairs={{0,48},{16,0},{32,16},{48,32},{64,112},{80,64},{96,80},{112,96},{1... | collective-permute-start | bytes 98312 | tf_op jit(solution)/shard_map/ppermute | solution.py:537
  40.7 6.9 %collective-permute-start.3 = (bf16[4,16,1024]{2,1,0:T(8,128)(2,1)S(1)}, bf16[4,16,1024]{2,1,0:T(8,128)(2,1)S(1)}, u32[]{:S(2)}, u32[]{:S(2)}) collective-permute-start(bf16[4,16,1024]{2,1,0:T(8,128)(2,1)S(1)} %pad_maximum_fusion.refs_0_), channel_id=1, source_target_pairs={{0,2},{1,3},{2,4},{3,5},{4,6},{5,7},{6,8},{7,9},{8,10},{9,11},{10,... | collective-permute-start | bytes 393224 | tf_op jit(solution)/shard_map/ppermute | solution.py:545
  43.3 6.9 %collective-permute-start.7 = (bf16[4,16,1024]{2,1,0:T(8,128)(2,1)S(1)}, bf16[4,16,1024]{2,1,0:T(8,128)(2,1)S(1)}, u32[]{:S(2)}, u32[]{:S(2)}) collective-permute-start(bf16[4,16,1024]{2,1,0:T(8,128)(2,1)S(1)} %pad_maximum_fusion.refs_0_), channel_id=1, source_target_pairs={{0,14},{1,15},{2,0},{3,1},{4,2},{5,3},{6,4},{7,5},{8,6},{9,7},{10,... | collective-permute-start | bytes 393224 | tf_op jit(solution)/shard_map/ppermute | solution.py:545
  47.6 7.4 %collective-permute-start.4 = (bf16[4,16,1024]{2,1,0:T(8,128)(2,1)S(1)}, bf16[4,16,1024]{2,1,0:T(8,128)(2,1)S(1)}, u32[]{:S(2)}, u32[]{:S(2)}) collective-permute-start(bf16[4,16,1024]{2,1,0:T(8,128)(2,1)S(1)} %collective-permute-done.3.refs_1_), channel_id=1, source_target_pairs={{0,2},{1,3},{2,4},{3,5},{4,6},{5,7},{6,8},{7,9},{8,10},{9,11},{10,... | collective-permute-start | bytes 393224 | tf_op jit(solution)/shard_map/ppermute | solution.py:545
  50.2 6.9 %collective-permute-start.8 = (bf16[4,16,1024]{2,1,0:T(8,128)(2,1)S(1)}, bf16[4,16,1024]{2,1,0:T(8,128)(2,1)S(1)}, u32[]{:S(2)}, u32[]{:S(2)}) collective-permute-start(bf16[4,16,1024]{2,1,0:T(8,128)(2,1)S(1)} %collective-permute-done.7.refs_7_), channel_id=1, source_target_pairs={{0,14},{1,15},{2,0},{3,1},{4,2},{5,3},{6,4},{7,5},{8,6},{9,7},{10,... | collective-permute-start | bytes 393224 | tf_op jit(solution)/shard_map/ppermute | solution.py:545
  55.0 8.1 %collective-permute-start.5 = (bf16[4,16,1024]{2,1,0:T(8,128)(2,1)S(1)}, bf16[4,16,1024]{2,1,0:T(8,128)(2,1)S(1)}, u32[]{:S(2)}, u32[]{:S(2)}) collective-permute-start(bf16[4,16,1024]{2,1,0:T(8,128)(2,1)S(1)} %collective-permute-done.4.refs_2_), channel_id=1, source_target_pairs={{0,2},{1,3},{2,4},{3,5},{4,6},{5,7},{6,8},{7,9},{8,10},{9,11},{10,... | collective-permute-start | bytes 393224 | tf_op jit(solution)/shard_map/ppermute | solution.py:545
  57.0 7.9 %collective-permute-start.9 = (bf16[4,16,1024]{2,1,0:T(8,128)(2,1)S(1)}, bf16[4,16,1024]{2,1,0:T(8,128)(2,1)S(1)}, u32[]{:S(2)}, u32[]{:S(2)}) collective-permute-start(bf16[4,16,1024]{2,1,0:T(8,128)(2,1)S(1)} %collective-permute-done.8.refs_6_), channel_id=1, source_target_pairs={{0,14},{1,15},{2,0},{3,1},{4,2},{5,3},{6,4},{7,5},{8,6},{9,7},{10,... | collective-permute-start | bytes 393224 | tf_op jit(solution)/shard_map/ppermute | solution.py:545
  63.0 8.1 %collective-permute-start.6 = (bf16[4,16,1024]{2,1,0:T(8,128)(2,1)S(1)}, bf16[4,16,1024]{2,1,0:T(8,128)(2,1)S(1)}, u32[]{:S(2)}, u32[]{:S(2)}) collective-permute-start(bf16[4,16,1024]{2,1,0:T(8,128)(2,1)S(1)} %collective-permute-done.5.refs_3_), channel_id=1, source_target_pairs={{0,2},{1,3},{2,4},{3,5},{4,6},{5,7},{6,8},{7,9},{8,10},{9,11},{10,... | collective-permute-start | bytes 393224 | tf_op jit(solution)/shard_map/ppermute | solution.py:545
  83.7 17.1 %collective-permute-start.11 = (bf16[256,512]{1,0:T(8,128)(2,1)S(1)}, bf16[256,512]{1,0:T(8,128)(2,1)S(1)}, u32[]{:S(2)}, u32[]{:S(2)}) collective-permute-start(bf16[256,512]{1,0:T(8,128)(2,1)S(1)} %get-tuple-element.66), channel_id=1, source_target_pairs={{0,48},{16,0},{32,16},{48,32},{64,112},{80,64},{96,80},{112,96},{1... | collective-permute-start | bytes 786440 | tf_op jit(solution)/shard_map/ppermute | solution.py:537
  85.6 15.1 %collective-permute-start.12 = (bf16[256,512]{1,0:T(8,128)(2,1)S(1)}, bf16[256,512]{1,0:T(8,128)(2,1)S(1)}, u32[]{:S(2)}, u32[]{:S(2)}) collective-permute-start(bf16[256,512]{1,0:T(8,128)(2,1)S(1)} %get-tuple-element.67), channel_id=1, source_target_pairs={{0,32},{16,48},{32,0},{48,16},{64,96},{80,112},{96,64},{112,80},{1... | collective-permute-start | bytes 786440 | tf_op jit(solution)/shard_map/ppermute | solution.py:537
  89.3 14.0 %collective-permute-start.13 = (bf16[256,512]{1,0:T(8,128)(2,1)S(1)}, bf16[256,512]{1,0:T(8,128)(2,1)S(1)}, u32[]{:S(2)}, u32[]{:S(2)}) collective-permute-start(bf16[256,512]{1,0:T(8,128)(2,1)S(1)} %get-tuple-element.68), channel_id=1, source_target_pairs={{0,16},{16,32},{32,48},{48,0},{64,80},{80,96},{96,112},{112,64},{1... | collective-permute-start | bytes 786440 | tf_op jit(solution)/shard_map/ppermute | solution.py:537
  104.2 9.1 %collective-permute-start.14 = (f32[16,256]{1,0:T(8,128)S(1)}, f32[16,256]{1,0:T(8,128)S(1)}, u32[]{:S(2)}, u32[]{:S(2)}) collective-permute-start(f32[16,256]{1,0:T(8,128)S(1)} %get-tuple-element.73.refs_0_), channel_id=1, source_target_pairs={{0,1},{1,0},{2,3},{3,2},{4,5},{5,4},{6,7},{7,6},{8,9},{9,8},{10,11... | collective-permute-start | bytes 49160 | tf_op jit(solution)/shard_map/ppermute | solution.py:548
  106.2 7.2 %collective-permute-start.15 = (f32[16,256]{1,0:T(8,128)S(1)}, f32[16,256]{1,0:T(8,128)S(1)}, u32[]{:S(2)}, u32[]{:S(2)}) collective-permute-start(f32[16,256]{1,0:T(8,128)S(1)} %get-tuple-element.73.refs_0_), channel_id=1, source_target_pairs={{0,2},{1,3},{2,0},{3,1},{4,6},{5,7},{6,4},{7,5},{8,10},{9,11},{10,... | collective-permute-start | bytes 49160 | tf_op jit(solution)/shard_map/ppermute | solution.py:548
  118.3 41.3 %all-to-all-start.2 = ((bf16[32,16,512]{2,1,0:T(8,128)(2,1)}), bf16[32,16,512]{2,1,0:T(8,128)(2,1)S(1)}, u32[]{:S(2)}, u32[]{:S(2)}) async-start(bf16[32,16,512]{2,1,0:T(8,128)(2,1)} %bitcast.22), calls=%async_computation.2 | async-start | bytes 1048576 | tf_op jit(solution)/shard_map/all_to_all | solution.py:662
  138.9 12.7 %collective-permute-start.17 = (bf16[256,128]{1,0:T(8,128)(2,1)S(1)}, bf16[256,128]{1,0:T(8,128)(2,1)S(1)}, u32[]{:S(2)}, u32[]{:S(2)}) collective-permute-start(bf16[256,128]{1,0:T(8,128)(2,1)S(1)} %get-tuple-element.118), channel_id=1, source_target_pairs={{0,1},{1,0},{2,3},{3,2},{4,5},{5,4},{6,7},{7,6},{8,9},{9,8},{10,11... | collective-permute-start | bytes 196616 | tf_op jit(solution)/shard_map/ppermute | solution.py:548
  140.8 28.9 %collective-permute-start.20 = (bf16[256,512]{1,0:T(8,128)(2,1)S(1)}, bf16[256,512]{1,0:T(8,128)(2,1)S(1)}, u32[]{:S(2)}, u32[]{:S(2)}) collective-permute-start(bf16[256,512]{1,0:T(8,128)(2,1)S(1)} %get-tuple-element.94.refs_0_), channel_id=1, source_target_pairs={{0,16},{16,32},{32,48},{48,0},{64,80},{80,96},{96,112},{112,64},{1... | collective-permute-start | bytes 786440 | tf_op jit(solution)/shard_map/ppermute | solution.py:537
  143.3 26.4 %collective-permute-start.21 = (bf16[256,512]{1,0:T(8,128)(2,1)S(1)}, bf16[256,512]{1,0:T(8,128)(2,1)S(1)}, u32[]{:S(2)}, u32[]{:S(2)}) collective-permute-start(bf16[256,512]{1,0:T(8,128)(2,1)S(1)} %get-tuple-element.94.refs_0_), channel_id=1, source_target_pairs={{0,32},{16,48},{32,0},{48,16},{64,96},{80,112},{96,64},{112,80},{1... | collective-permute-start | bytes 786440 | tf_op jit(solution)/shard_map/ppermute | solution.py:537
  147.6 22.2 %collective-permute-start.22 = (bf16[256,512]{1,0:T(8,128)(2,1)S(1)}, bf16[256,512]{1,0:T(8,128)(2,1)S(1)}, u32[]{:S(2)}, u32[]{:S(2)}) collective-permute-start(bf16[256,512]{1,0:T(8,128)(2,1)S(1)} %get-tuple-element.94.refs_0_), channel_id=1, source_target_pairs={{0,48},{16,0},{32,16},{48,32},{64,112},{80,64},{96,80},{112,96},{1... | collective-permute-start | bytes 786440 | tf_op jit(solution)/shard_map/ppermute | solution.py:537
  149.5 6.2 %collective-permute-start.18 = (bf16[256,128]{1,0:T(8,128)(2,1)S(1)}, bf16[256,128]{1,0:T(8,128)(2,1)S(1)}, u32[]{:S(2)}, u32[]{:S(2)}) collective-permute-start(bf16[256,128]{1,0:T(8,128)(2,1)S(1)} %get-tuple-element.117), channel_id=1, source_target_pairs={{0,2},{1,3},{2,0},{3,1},{4,6},{5,7},{6,4},{7,5},{8,10},{9,11},{10,... | collective-permute-start | bytes 196616 | tf_op jit(solution)/shard_map/ppermute | solution.py:548
  151.6 5.9 %collective-permute-start.19 = (bf16[256,128]{1,0:T(8,128)(2,1)S(1)}, bf16[256,128]{1,0:T(8,128)(2,1)S(1)}, u32[]{:S(2)}, u32[]{:S(2)}) collective-permute-start(bf16[256,128]{1,0:T(8,128)(2,1)S(1)} %get-tuple-element.116), channel_id=1, source_target_pairs={{0,3},{1,2},{2,1},{3,0},{4,7},{5,6},{6,5},{7,4},{8,11},{9,10},{10,... | collective-permute-start | bytes 196616 | tf_op jit(solution)/shard_map/ppermute | solution.py:548
  159.7 62.6 %all-to-all-start.1 = ((bf16[32,16,896]{2,1,0:T(8,128)(2,1)}), bf16[32,16,896]{2,1,0:T(8,128)(2,1)S(1)}, u32[]{:S(2)}, u32[]{:S(2)}) async-start(bf16[32,16,896]{2,1,0:T(8,128)(2,1)} %bitcast.20), calls=%async_computation.1 | async-start | bytes 1835008 | tf_op jit(solution)/shard_map/all_to_all | solution.py:740
  173.4 22.3 %collective-permute-start.23 = (bf16[512,128]{1,0:T(8,128)(2,1)S(1)}, bf16[512,128]{1,0:T(8,128)(2,1)S(1)}, u32[]{:S(2)}, u32[]{:S(2)}) collective-permute-start(bf16[512,128]{1,0:T(8,128)(2,1)S(1)} %get-tuple-element.95), channel_id=1, source_target_pairs={{0,448},{16,464},{32,480},{48,496},{64,0},{80,16},{96,32},{112,48}... | collective-permute-start | bytes 393224 | tf_op jit(solution)/shard_map/ppermute | solution.py:541
  175.9 21.8 %collective-permute-start.27 = (bf16[512,128]{1,0:T(8,128)(2,1)S(1)}, bf16[512,128]{1,0:T(8,128)(2,1)S(1)}, u32[]{:S(2)}, u32[]{:S(2)}) collective-permute-start(bf16[512,128]{1,0:T(8,128)(2,1)S(1)} %get-tuple-element.99), channel_id=1, source_target_pairs={{0,64},{16,80},{32,96},{48,112},{64,128},{80,144},{96,160},{112,17... | collective-permute-start | bytes 393224 | tf_op jit(solution)/shard_map/ppermute | solution.py:541
  195.7 8.3 %collective-permute-start.24 = (bf16[512,128]{1,0:T(8,128)(2,1)S(1)}, bf16[512,128]{1,0:T(8,128)(2,1)S(1)}, u32[]{:S(2)}, u32[]{:S(2)}) collective-permute-start(bf16[512,128]{1,0:T(8,128)(2,1)S(1)} %add_convert_fusion.5), channel_id=1, source_target_pairs={{0,448},{16,464},{32,480},{48,496},{64,0},{80,16},{96,32},{112,48}... | collective-permute-start | bytes 393224 | tf_op jit(solution)/shard_map/ppermute | solution.py:541
  197.7 8.3 %collective-permute-start.28 = (bf16[512,128]{1,0:T(8,128)(2,1)S(1)}, bf16[512,128]{1,0:T(8,128)(2,1)S(1)}, u32[]{:S(2)}, u32[]{:S(2)}) collective-permute-start(bf16[512,128]{1,0:T(8,128)(2,1)S(1)} %add_convert_fusion.2), channel_id=1, source_target_pairs={{0,64},{16,80},{32,96},{48,112},{64,128},{80,144},{96,160},{112,17... | collective-permute-start | bytes 393224 | tf_op jit(solution)/shard_map/ppermute | solution.py:541
  204.1 8.1 %collective-permute-start.25 = (bf16[512,128]{1,0:T(8,128)(2,1)S(1)}, bf16[512,128]{1,0:T(8,128)(2,1)S(1)}, u32[]{:S(2)}, u32[]{:S(2)}) collective-permute-start(bf16[512,128]{1,0:T(8,128)(2,1)S(1)} %add_convert_fusion.4), channel_id=1, source_target_pairs={{0,448},{16,464},{32,480},{48,496},{64,0},{80,16},{96,32},{112,48}... | collective-permute-start | bytes 393224 | tf_op jit(solution)/shard_map/ppermute | solution.py:541
  206.1 8.1 %collective-permute-start.29 = (bf16[512,128]{1,0:T(8,128)(2,1)S(1)}, bf16[512,128]{1,0:T(8,128)(2,1)S(1)}, u32[]{:S(2)}, u32[]{:S(2)}) collective-permute-start(bf16[512,128]{1,0:T(8,128)(2,1)S(1)} %add_convert_fusion.1), channel_id=1, source_target_pairs={{0,64},{16,80},{32,96},{48,112},{64,128},{80,144},{96,160},{112,17... | collective-permute-start | bytes 393224 | tf_op jit(solution)/shard_map/ppermute | solution.py:541
  212.2 8.1 %collective-permute-start.26 = (bf16[512,128]{1,0:T(8,128)(2,1)S(1)}, bf16[512,128]{1,0:T(8,128)(2,1)S(1)}, u32[]{:S(2)}, u32[]{:S(2)}) collective-permute-start(bf16[512,128]{1,0:T(8,128)(2,1)S(1)} %add_convert_fusion.3), channel_id=1, source_target_pairs={{0,448},{16,464},{32,480},{48,496},{64,0},{80,16},{96,32},{112,48}... | collective-permute-start | bytes 393224 | tf_op jit(solution)/shard_map/ppermute | solution.py:541
  (39 other events, 403.5 us)
Sparse Core Ops, SparseCore 0:
  28.8 46.4 all-gather.1

commit v3 on v1

--- a/solution.py
+++ b/solution.py
@@ -19,18 +19,40 @@
 bf16 = jnp.bfloat16
 smem = pl.BlockSpec(memory_space=pltpu.SMEM)
 vmem = pl.BlockSpec(memory_space=pltpu.VMEM)
-
-
-def call(body, outs, ins, scalars=0, cost=1, scratch=(), name=None):
+anywhere = pl.BlockSpec(memory_space=pl.ANY)
+
+
+def call(body, outs, ins, scalars=0, fetch=(), cost=1, scratch=(), name=None):
     size = sum(math.prod(o.shape) * o.dtype.itemsize for o in outs)
     size += sum(math.prod(i.shape) * i.dtype.itemsize for i in ins)
+    specs = [smem] * scalars + [vmem] * (len(ins) - scalars)
+    for k in fetch:
+        specs[k] = anywhere
+    kept = len(ins) + len(outs) + len(scratch)
+
+    def fetching(*refs):
+        args, held, sems = list(refs[:kept]), refs[kept:-1], refs[-1]
+        copies = []
+        for n, k in enumerate(fetch):
+            copies.append(pltpu.make_async_copy(args[k], held[n], sems.at[n]))
+            args[k] = held[n]
+        for copy in copies:
+            copy.start()
+        for copy in copies:
+            copy.wait()
+        body(*args)
+
+    extra = []
+    if fetch:
+        extra = [pltpu.VMEM(ins[k].shape, ins[k].dtype) for k in fetch]
+        extra.append(pltpu.SemaphoreType.DMA((len(fetch),)))
     return pl.pallas_call(
-        body,
+        fetching if fetch else body,
         out_shape=outs,
-        in_specs=[smem] * scalars + [vmem] * (len(ins) - scalars),
+        in_specs=specs,
         out_specs=[vmem] * len(outs),
-        scratch_shapes=list(scratch),
-        compiler_params=pltpu.CompilerParams(vmem_limit_bytes=48 << 20),
+        scratch_shapes=list(scratch) + extra,
+        compiler_params=pltpu.CompilerParams(vmem_limit_bytes=16 << 20),
         cost_estimate=pl.CostEstimate(
             flops=int(cost * 1e6), bytes_accessed=size, transcendentals=0
         ),
@@ -120,35 +142,38 @@
     return (lane_ids(shape) // head_width == row_ids(shape)).astype(f32)
 
 
-def pack_dout_body(co_ref, dout_ref, *d_refs):
-    inner = len(d_refs)
+def pack_dout_body(inner, co_ref, dout_ref, d_ref):
+    rows = dout_ref.shape[0]
     outer = dout_ref.shape[1] // (LANES * inner)
-    for k in range(inner):
-        block = lax.rem(co_ref[1] + k, inner)
-        for z in range(outer):
-            low = pl.multiple_of((z * inner + block) * LANES, LANES)
-            d_refs[k][:, z * LANES : (z + 1) * LANES] = dout_ref[:, pl.ds(low, LANES)]
-
-
-def pack_body(bin_ref, slot_ref, co_ref, x_ref, z_ref, bc_ref, dt_ref, a_ref, zs_ref):
+    for z in range(outer):
+        block = lax.rem(co_ref[3] + outer - z, outer) * inner * LANES
+        low = pl.multiple_of(block, LANES)
+        for x in range(inner):
+            d_ref[x * rows : (x + 1) * rows, z * LANES : (z + 1) * LANES] = dout_ref[
+                :, pl.ds(low + x * LANES, LANES)
+            ]
+
+
+def pack_body(bin_ref, slot_ref, co_ref, x_ref, z_ref, bc_ref, dt_ref, a_ref):
     npan = bin_ref.shape[0]
     channels = x_ref.shape[1]
+    heads = dt_ref.shape[1]
     pair = bc_ref.shape[1] // GROUPS
-    heads = dt_ref.shape[1]
     a_ref[...] = jnp.zeros_like(a_ref)
-    zs_ref[...] = jnp.zeros_like(zs_ref)
     group = pl.multiple_of(co_ref[0] * pair, pair)
     shape = (PANEL, LANES)
+    low, high = 2 * channels, 2 * channels + pair
+    widen = (row_ids((heads, LANES)) == lane_ids((heads, LANES))).astype(bf16)
+    wide = dot_nn(dt_ref[...], widen)
     for p in range(npan):
         rows = slice(p * PANEL, (p + 1) * PANEL)
         to = pl.ds(pl.multiple_of(bin_ref[p] * PANEL, PANEL), PANEL)
         a_ref[to, 0:channels] = x_ref[rows, :]
-        a_ref[to, channels : channels + pair] = bc_ref[rows, pl.ds(group, pair)]
+        a_ref[to, channels:low] = z_ref[rows, :]
+        a_ref[to, low:high] = bc_ref[rows, pl.ds(group, pair)]
         label = (slot_ref[p] * PANEL + 1 + row_ids(shape)).astype(f32)
-        lanes = lane_ids(shape)
-        meta = jnp.where(lanes == LANES - 1, label, dt_ref[rows, :])
-        a_ref[to, channels + pair : channels + pair + LANES] = meta.astype(bf16)
-        zs_ref[to, :] = z_ref[rows, :]
+        meta = jnp.where(lane_ids(shape) == LANES - 1, label, wide[rows, :])
+        a_ref[to, high : high + LANES] = meta.astype(bf16)
 
 
 def forward_body(
@@ -173,13 +198,16 @@
     slope_ref,
     cum_ref,
     cumt_ref,
+    zb_ref,
+    gated_ref,
 ):
     rows, channels = xraw_ref.shape
     pair = bcact_ref.shape[1]
     state = pair // 2
     head_width = channels // heads
+    base = 2 * channels
     slots = recv_ref.shape[0]
-    label = recv_ref[:, channels + pair : channels + pair + LANES].astype(f32)[:, LANES - 1 :]
+    label = recv_ref[:, base + pair : base + pair + LANES].astype(f32)[:, LANES - 1 :]
     place = (label == (lane_ids((slots, rows)) + 1).astype(f32)).astype(bf16)
     pt_ref[...] = place
     raw = dot_tn(place, recv_ref[...])
@@ -189,7 +217,7 @@
     xpre = conv(xraw, cx_ref[...], keeps)
     xpre_ref[...] = xpre
     xact = xpre * jax.nn.sigmoid(xpre)
-    bcraw = raw[:, channels : channels + pair]
+    bcraw = raw[:, base : base + pair]
     share = share_ref.shape[2] // 2
     for s in range(share_ref.shape[0]):
         tile = bcraw[:, (s // 2) * LANES : (s // 2 + 1) * LANES]
@@ -203,7 +231,7 @@
     scores = dot_nt(bcact[:, state:], bcact[:, :state])
     scores_ref[...] = scores
     mask = seen_mask(len_ref, rows)
-    dt = raw[:, channels + pair : channels + pair + LANES] + bias_ref[...]
+    dt = raw[:, base + pair : base + pair + LANES] + bias_ref[...]
     real = lane_ids(dt.shape) < heads
     step = jnp.where(real, jnp.maximum(dt, 0.0) + jnp.log1p(jnp.exp(-jnp.abs(dt))), 0.0)
     step_ref[...] = step
@@ -225,30 +253,17 @@
             part = jnp.where(low if half == 0 else ~low, tile, jnp.zeros_like(tile))
             total = total + dot_nn(weights, part)
         mixed_ref[:, p * LANES : (p + 1) * LANES] = total
-
-
-def gate_body(recv_ref, pt_ref, mixed_ref, zb_ref, gated_ref, sums_ref):
-    z = dot_tn(pt_ref[...], recv_ref[...])
+    z = raw[:, channels:base]
     zb_ref[...] = z.astype(bf16)
-    gated = mixed_ref[...] * (z * jax.nn.sigmoid(z))
-    gated_ref[...] = gated
-    ones = jnp.ones((8, gated.shape[1]), f32)
-    sums_ref[...] = dot_nt(ones, gated * gated, exact)
-
-
-def as_column(parts):
-    total = parts[0][...]
-    for part in parts[1:]:
-        total = total + part[...]
-    return dot_tn(total, jnp.full((8, LANES), 0.125, f32), exact)
-
-
-def norm_body(size, gated_ref, gain_ref, *refs):
-    parts, (normed_ref, inv_ref) = refs[:-2], refs[-2:]
-    inverse = lax.rsqrt(as_column(parts) / size + 1e-05)
-    inv_ref[...] = inverse
-    normed = gated_ref[...] * inverse[:, :1] * gain_ref[...]
-    normed_ref[...] = normed.astype(bf16)
+    gated_ref[...] = mixed_ref[...] * (z * jax.nn.sigmoid(z))
+
+
+def as_column(sums_ref):
+    total = sums_ref[:16]
+    for k in range(1, sums_ref.shape[0] // 16):
+        total = total + sums_ref[16 * k : 16 * (k + 1)]
+    eighth = jnp.full((8, LANES), 0.125, f32)
+    return dot_tn(total[:8], eighth, exact), dot_tn(total[8:], eighth, exact)
 
 
 def rows_of(out_ref, k):
@@ -256,54 +271,80 @@
     return out_ref[:, k].reshape(tensor * panel, columns)
 
 
-def dnormed_body(out_ref, w_ref, *p_refs):
-    w = jnp.concatenate([w_ref[z] for z in range(w_ref.shape[0])], axis=1)
-    for k, p_ref in enumerate(p_refs):
-        p_ref[...] = dot_nt(rows_of(out_ref, k), w).astype(p_ref.dtype)
-
-
-def term_body(scale, out_ref, *refs):
-    normed, term_ref = refs[:-1], refs[-1]
+def dnormed_body(out_ref, *refs):
+    blocks, p_ref = refs[:-1], refs[-1]
+    w = jnp.concatenate([block[...] for block in blocks], axis=1)
+    inner = out_ref.shape[1]
+    rows = p_ref.shape[0] // inner
+    for k in range(inner):
+        p_ref[k * rows : (k + 1) * rows] = dot_nt(rows_of(out_ref, k), w).astype(bf16)
+
+
+def term_body(scale, out_ref, normed_ref, *terms):
+    inner = out_ref.shape[1]
+    rows = normed_ref.shape[0] // inner
     total = None
-    for k, normed_ref in enumerate(normed):
-        part = dot_tn(normed_ref[...], rows_of(out_ref, k))
+    for k in range(inner):
+        part = dot_tn(normed_ref[k * rows : (k + 1) * rows], rows_of(out_ref, k))
         total = part if total is None else total + part
     total = (total * scale).astype(bf16)
-    for z in range(term_ref.shape[0]):
-        term_ref[z] = total[:, z * LANES : (z + 1) * LANES]
-
-
-def cross_body(gated_ref, inv_ref, gain_ref, *refs):
-    parts, (weighted_ref, dgain_ref, sums_ref) = refs[:-3], refs[-3:]
-    dnormed = parts[0][...].astype(f32)
-    for part in parts[1:]:
-        dnormed = dnormed + part[...].astype(f32)
+    for k, term_ref in enumerate(terms):
+        term_ref[...] = total[:, k * LANES : (k + 1) * LANES]
+
+
+def cross_body(gated_ref, gain_ref, parts_ref, dnormed_ref, sums_ref):
     gated = gated_ref[...]
-    product = dnormed * gated
-    dgain_ref[...] = jnp.sum(product * inv_ref[:, :1], axis=0, keepdims=True)
-    weighted = dnormed * gain_ref[...]
-    weighted_ref[...] = weighted
+    rows = gated.shape[0]
+    dnormed = parts_ref[:rows].astype(f32)
+    for k in range(1, parts_ref.shape[0] // rows):
+        dnormed = dnormed + parts_ref[k * rows : (k + 1) * rows].astype(f32)
+    dnormed_ref[...] = dnormed
     ones = jnp.ones((8, gated.shape[1]), f32)
-    sums_ref[...] = dot_nt(ones, product * gain_ref[...], exact)
-
-
-def dz_body(size, weighted_ref, gated_ref, mixed_ref, zb_ref, inv_ref, pt_ref, *refs):
-    parts, (dy_ref, back_ref) = refs[:-2], refs[-2:]
-    inverse = inv_ref[...]
-    factor = (inverse * inverse * inverse * as_column(parts) / size)[:, :1]
-    dgated = inverse[:, :1] * weighted_ref[...] - gated_ref[...] * factor
+    squares = dot_nt(ones, gated * gated, exact)
+    crossing = dot_nt(ones, dnormed * gated * gain_ref[...], exact)
+    for k in range(sums_ref.shape[0] // 16):
+        sums_ref[16 * k : 16 * k + 8] = squares
+        sums_ref[16 * k + 8 : 16 * k + 16] = crossing
+
+
+def dz_body(
+    size,
+    dnormed_ref,
+    gain_ref,
+    gated_ref,
+    mixed_ref,
+    zb_ref,
+    sums_ref,
+    normed_ref,
+    dgain_ref,
+    dy_ref,
+    dz_ref,
+):
+    squares, crossing = as_column(sums_ref)
+    inverse = lax.rsqrt(squares / size + 1e-05)
+    factor = (inverse * inverse * inverse * crossing / size)[:, :1]
+    inverse = inverse[:, :1]
+    gain = gain_ref[...]
+    gated = gated_ref[...]
+    dnormed = dnormed_ref[...]
+    scaled = gated * inverse
+    normed = (scaled * gain).astype(bf16)
+    rows = gated.shape[0]
+    for k in range(normed_ref.shape[0] // rows):
+        normed_ref[k * rows : (k + 1) * rows] = normed
+    dgain_ref[...] = jnp.sum(dnormed * scaled, axis=0, keepdims=True)
+    dgated = inverse * (dnormed * gain) - gated * factor
     z = zb_ref[...].astype(f32)
     sig = jax.nn.sigmoid(z)
     dy_ref[...] = dgated * (z * sig)
     dz = dgated * mixed_ref[...] * sig * (1.0 + z * (1.0 - sig))
-    back_ref[...] = dot_nn(pt_ref[...], dz.astype(bf16)).astype(bf16)
+    dz_ref[...] = dz.astype(bf16)
 
 
 def backward_body(
     width,
     heads,
     len_ref,
-    co_ref,
     dy_ref,
     xpre_ref,
     xraw_ref,
@@ -385,14 +426,14 @@
         dot_tn(dsb, bcact_ref[:, state:]),
         dot_nn(dsb, bcact_ref[:, :state]),
     )
-    share = pieces_ref.shape[2] // 2
-    for s in range(pieces_ref.shape[0]):
+    share = pieces_ref.shape[1] // 2
+    for s in range(pieces_ref.shape[0] // rows):
         low_lane = (s * share) % state
         tile = dbc[s * share // state][:, low_lane // LANES * LANES : (low_lane // LANES + 1) * LANES]
         if low_lane % LANES:
             tile = pltpu.roll(tile, share, 1)
         tile = jnp.where(lane_ids(tile.shape) < share, tile, 0.0)
-        pieces_ref[jnp.bitwise_xor(co_ref[2], s)] = tile.astype(bf16)
+        pieces_ref[s * rows : (s + 1) * rows] = tile.astype(bf16)
 
 
 def share_body(
@@ -402,14 +443,16 @@
     share_ref,
     taps_ref,
     gx_ref,
+    dz_ref,
     ddt_ref,
     pt_ref,
     dcx_ref,
     dgain_ref,
     dheads_ref,
-    *refs,
+    parts_ref,
+    back_ref,
+    small_ref,
 ):
-    parts, back_ref, small_ref = refs[:-2], refs[-2], refs[-1]
     rows = ddt_ref.shape[0]
     channels = gx_ref.shape[1]
     slots = back_ref.shape[0]
@@ -418,15 +461,17 @@
     taps = taps_ref[...]
     pre = conv(raw, taps, keeps)
     sig = jax.nn.sigmoid(pre)
-    dact = parts[0][...].astype(f32)
-    for part in parts[1:]:
-        dact = dact + part[...].astype(f32)
+    dact = parts_ref[:rows].astype(f32)
+    for k in range(1, parts_ref.shape[0] // rows):
+        dact = dact + parts_ref[k * rows : (k + 1) * rows].astype(f32)
     draw, dtaps = conv_back(dact * (sig * (1.0 + pre * (1.0 - sig))), raw, taps, keeps)
     share = LANES // 2
     meta = draw + pltpu.roll(ddt_ref[...], share, 1)
     place = pt_ref[...]
     back_ref[:, :channels] = dot_nn(place, gx_ref[...]).astype(bf16)
-    back_ref[:, channels : channels + LANES] = dot_nn(place, meta.astype(bf16)).astype(bf16)
+    back_ref[:, channels : 2 * channels] = dot_nn(place, dz_ref[...]).astype(bf16)
+    last = 2 * channels + LANES
+    back_ref[:, 2 * channels : last] = dot_nn(place, meta.astype(bf16)).astype(bf16)
     small_ref[...] = jnp.zeros_like(small_ref)
     small_ref[0:width] = dcx_ref[...]
     small_ref[width : width + 1] = dgain_ref[...]
@@ -438,31 +483,38 @@
     half = channels // 2
     block = jnp.concatenate([small_ref[:, :half], small_ref[:, half:]], axis=0).astype(bf16)
     for k in range(slots // PANEL):
-        back_ref[k * PANEL : (k + 1) * PANEL, channels + LANES :] = block
-
-
-def home_z_body(bin_ref, ret_ref, gz_ref):
-    for p in range(bin_ref.shape[0]):
-        at = pl.ds(pl.multiple_of(bin_ref[p] * PANEL, PANEL), PANEL)
-        gz_ref[p * PANEL : (p + 1) * PANEL] = ret_ref[at]
+        back_ref[k * PANEL : (k + 1) * PANEL, last:] = block
 
 
 def home_body(
-    scale, heads, bin_ref, ret_ref, gx_ref, gbc_ref, gdt_ref, dcx_ref, dcbc_ref, dgain_ref, dheads_ref
+    scale,
+    heads,
+    bin_ref,
+    ret_ref,
+    gx_ref,
+    gz_ref,
+    gbc_ref,
+    gdt_ref,
+    dcx_ref,
+    dcbc_ref,
+    dgain_ref,
+    dheads_ref,
 ):
     channels = gx_ref.shape[1]
     width = dcx_ref.shape[0]
     share = gbc_ref.shape[1]
+    last = 2 * channels + LANES
     for p in range(bin_ref.shape[0]):
         rows = slice(p * PANEL, (p + 1) * PANEL)
         at = pl.ds(pl.multiple_of(bin_ref[p] * PANEL, PANEL), PANEL)
         gx_ref[rows] = ret_ref[at, :channels]
-        meta = ret_ref[at, channels : channels + LANES].astype(f32)
+        gz_ref[rows] = ret_ref[at, channels : 2 * channels]
+        meta = ret_ref[at, 2 * channels : last].astype(f32)
         gbc_ref[rows] = meta[:, :share].astype(bf16)
         gdt_ref[rows] = pltpu.roll(meta, LANES - share, 1)[:, :heads].astype(bf16)
     total = None
     for k in range(ret_ref.shape[0] // PANEL):
-        part = ret_ref[k * PANEL : (k + 1) * PANEL, channels + LANES :].astype(f32)
+        part = ret_ref[k * PANEL : (k + 1) * PANEL, last:].astype(f32)
         total = part if total is None else total + part
     total = total * scale
     small = jnp.concatenate([total[:8], total[8:]], axis=1)
@@ -513,47 +565,48 @@
     scale = 1.0 / math.sqrt(rows * dp)
     columns = outer * LANES
 
-    coords = jnp.stack([group, x_index, local]).astype(jnp.int32)
-    over_z = [[z * inner + x for z in range(outer)] for x in range(inner)]
-
-    def along_x(block, shift):
-        route = []
-        for z in range(outer):
-            for x in range(inner):
-                route.append((z * inner + x, z * inner + (x + shift) % inner))
+    z_index = lax.axis_index("dp") // inner
+    coords = jnp.stack([group, x_index, local, z_index]).astype(jnp.int32)
+    over_x = [[z * inner + x for x in range(inner)] for z in range(outer)]
+    in_group = [[g * members + m for m in range(members)] for g in range(GROUPS)]
+
+    def along_z(block, shift):
+        route = [(d, (d + shift * inner) % dp) for d in range(dp)]
         return lax.ppermute(block, "dp", route)
 
-    def partner(block, flip):
-        return lax.ppermute(block, "tensor", [(t, t ^ flip) for t in range(tensor)])
-
-    def in_group(block):
-        return [block] + [partner(block, flip) for flip in range(1, members)]
-
-    d_parts = call(
-        pack_dout_body,
-        [shaped((dout.shape[0], columns), bf16)] * inner,
+    def swap(blocks, axis, groups=None):
+        return lax.all_to_all(
+            blocks, axis, split_axis=0, concat_axis=0, tiled=True, axis_index_groups=groups
+        )
+
+    (d_parts,) = call(
+        functools.partial(pack_dout_body, inner),
+        [shaped((inner * dout.shape[0], columns), bf16)],
         [coords, dout],
         scalars=1,
+        fetch=(1,),
         name="pack_dout",
     )
-    d_own = [d_parts[0]] + [along_x(d_parts[k], k) for k in range(1, inner)]
-    out_rows = lax.all_gather(jnp.concatenate(d_own, axis=0), "tensor", axis=0, tiled=True)
+    d_own = swap(d_parts, "dp", over_x)
+    out_rows = lax.all_gather(d_own, "tensor", axis=0, tiled=True)
     out_rows = out_rows.reshape(tensor, inner, dout.shape[0], columns)
-    w_cols = lax.all_gather(
-        w_out, "dp", axis=0, tiled=True, axis_index_groups=over_z
-    ).reshape(outer, channels, LANES)
-
-    dt_wide = jnp.pad(dt_in.astype(f32), ((0, 0), (0, LANES - heads)))
-    first = channels + pair + LANES
-    send_a, send_z = call(
+
+    (send,) = call(
         pack_body,
-        [shaped((slots, first), bf16), shaped((slots, channels), bf16)],
-        [panel_bin, panel_slot, coords, x_in, z_in, bc_in, dt_wide],
+        [shaped((slots, 2 * channels + pair + LANES), bf16)],
+        [panel_bin, panel_slot, coords, x_in, z_in, bc_in, dt_in],
         scalars=3,
+        fetch=(3, 4, 5, 6),
         name="pack",
     )
-    recv_a = lax.all_to_all(send_a, "dp", split_axis=0, concat_axis=0, tiled=True)
-    recv_z = lax.all_to_all(send_z, "dp", split_axis=0, concat_axis=0, tiled=True)
+    recv = swap(send, "dp")
+
+    ups, downs = [w_out], [w_out]
+    for step in range(1, outer // 2 + 1):
+        ups.append(along_z(ups[-1], 1))
+        if step < outer - outer // 2:
+            downs.append(along_z(downs[-1], -1))
+    w_cols = ups + downs[:0:-1]
 
     bias_row = jnp.pad(dt_bias, (0, LANES - heads))[None, :]
     alog_row = jnp.pad(a_log, (0, LANES - heads))[None, :]
@@ -564,7 +617,21 @@
         ((0, 0), (0, LANES - share)),
     )
 
-    place, xraw, xpre, mixed, raw_share, bcact, scores, step, slope, cum, cumt = call(
+    (
+        place,
+        xraw,
+        xpre,
+        mixed,
+        raw_share,
+        bcact,
+        scores,
+        step,
+        slope,
+        cum,
+        cumt,
+        zb,
+        gated,
+    ) = call(
         functools.partial(forward_body, width, heads),
         [
             shaped((slots, rows), bf16),
@@ -578,73 +645,42 @@
             shaped((rows, LANES), f32),
             shaped((rows, LANES), f32),
             shaped((8, rows), f32),
+            shaped((rows, channels), bf16),
+            shaped((rows, channels), f32),
         ],
-        [lengths, coords, recv_a, conv_x, conv_bc, bias_row, alog_row, skip_row],
+        [lengths, coords, recv, conv_x, conv_bc, bias_row, alog_row, skip_row],
         scalars=2,
+        fetch=(3, 4, 5, 6, 7),
         cost=4000,
         name="forward",
     )
-    zb, gated, squares = call(
-        gate_body,
-        [
-            shaped((rows, channels), bf16),
-            shaped((rows, channels), f32),
-            shaped((8, rows), f32),
-        ],
-        [recv_z, place, mixed],
-        cost=1000,
-        name="gate",
-    )
-    normed, inverse = call(
-        functools.partial(norm_body, size),
-        [shaped((rows, channels), bf16), shaped((rows, LANES), f32)],
-        [gated, gain_row] + in_group(squares),
-        cost=500,
-        name="norm",
-    )
-
-    partial = call(
+
+    (partial,) = call(
         dnormed_body,
-        [shaped((rows, channels), f32)] + [shaped((rows, channels), bf16)] * (inner - 1),
-        [out_rows, w_cols],
+        [shaped((inner * rows, channels), bf16)],
+        [out_rows] + w_cols,
+        fetch=range(outer + 1),
         cost=1200,
         name="dnormed",
     )
-    d_terms = [partial[0]] + [along_x(partial[k], -k) for k in range(1, inner)]
-    weighted, dgain, crossing = call(
+    dnormed, sums = call(
         cross_body,
-        [
-            shaped((rows, channels), f32),
-            shaped((1, channels), f32),
-            shaped((8, rows), f32),
-        ],
-        [gated, inverse, gain_row] + d_terms,
+        [shaped((rows, channels), f32), shaped((members * 16, rows), f32)],
+        [gated, gain_row, swap(partial, "dp", over_x)],
         cost=500,
         name="cross",
     )
-    dy, back_z = call(
+    normed, dgain, dy, dz = call(
         functools.partial(dz_body, size),
-        [shaped((rows, channels), f32), shaped((slots, channels), bf16)],
-        [weighted, gated, mixed, zb, inverse, place] + in_group(crossing),
+        [
+            shaped((inner * rows, channels), bf16),
+            shaped((1, channels), f32),
+            shaped((rows, channels), f32),
+            shaped((rows, channels), bf16),
+        ],
+        [dnormed, gain_row, gated, mixed, zb, swap(sums, "tensor", in_group)],
         cost=1000,
         name="dz",
-    )
-    home_z = lax.all_to_all(back_z, "dp", split_axis=0, concat_axis=0, tiled=True)
-
-    normed_all = [normed] + [along_x(normed, k) for k in range(1, inner)]
-    (term,) = call(
-        functools.partial(term_body, scale),
-        [shaped((outer, channels, LANES), bf16)],
-        [out_rows] + normed_all,
-        cost=1200,
-        name="term",
-    )
-    grad_wout = lax.psum_scatter(
-        term.reshape(outer * channels, LANES),
-        "dp",
-        scatter_dimension=0,
-        axis_index_groups=over_z,
-        tiled=True,
     )
 
     gx, dcx, ddt, dheads, pieces = call(
@@ -654,11 +690,10 @@
             shaped((width, channels), f32),
             shaped((rows, LANES), f32),
             shaped((3, LANES), f32),
-            shaped((members, rows, LANES), bf16),
+            shaped((members * rows, LANES), bf16),
         ],
         [
             lengths,
-            coords,
             dy,
             xpre,
             xraw,
@@ -673,43 +708,62 @@
             alog_row,
             skip_row,
         ],
-        scalars=2,
+        scalars=1,
+        fetch=range(2, 14),
         cost=6000,
         name="backward",
     )
-    parts = [pieces[0]] + [partner(pieces[flip], flip) for flip in range(1, members)]
-    (back_a,) = call(
+
+    terms = call(
+        functools.partial(term_body, scale),
+        [shaped((channels, LANES), bf16)] * outer,
+        [out_rows, swap(normed, "dp", over_x)],
+        fetch=(0,),
+        cost=1200,
+        name="term",
+    )
+    (back,) = call(
         functools.partial(share_body, width),
-        [shaped((slots, channels + LANES + channels // 2), bf16)],
+        [shaped((slots, 2 * channels + LANES + channels // 2), bf16)],
         [
             lengths,
             coords,
             raw_share,
             share_taps,
             gx,
+            dz,
             ddt,
             place,
             dcx,
             dgain,
             dheads,
-        ]
-        + parts,
+            swap(pieces, "tensor", in_group),
+        ],
         scalars=2,
+        fetch=(2, 3, 5, 7, 9),
         cost=1500,
         scratch=[pltpu.VMEM((8, channels), f32)],
         name="share",
     )
-    home_a = lax.all_to_all(back_a, "dp", split_axis=0, concat_axis=0, tiled=True)
-    (grad_z,) = call(
-        home_z_body,
-        [shaped((rows, channels), bf16)],
-        [panel_bin, home_z],
-        scalars=1,
-        name="home_z",
-    )
-    grad_x, grad_bc, grad_dt, grad_cx, grad_cbc, grad_gain, grad_heads = call(
+    home = swap(back, "dp")
+
+    def add(moved, term):
+        return (moved.astype(f32) + term.astype(f32)).astype(bf16)
+
+    far = outer // 2
+    down, up = terms[far], terms[far + 1]
+    for k in range(far - 1, 0, -1):
+        down = add(along_z(down, -1), terms[k])
+    for k in range(far + 2, outer):
+        up = add(along_z(up, 1), terms[k])
+    grad_wout = (
+        along_z(down, -1).astype(f32) + along_z(up, 1).astype(f32) + terms[0].astype(f32)
+    ).astype(bf16)
+
+    grad_x, grad_z, grad_bc, grad_dt, grad_cx, grad_cbc, grad_gain, grad_heads = call(
         functools.partial(home_body, scale, heads),
         [
+            shaped((rows, channels), bf16),
             shaped((rows, channels), bf16),
             shaped((rows, share), bf16),
             shaped((rows, heads), bf16),
@@ -718,7 +772,7 @@
             shaped((1, channels), f32),
             shaped((3, heads), f32),
         ],
-        [panel_bin, home_a],
+        [panel_bin, home],
         scalars=1,
         name="home",
     )

time: 248 us -> 235 us (0.948)
  the two profiles are of different devices: /device:TPU:2 before, /device:TPU:248 now
where the time goes in v3:
time: 235 us; the launch traced here: 234 us
  waiting for transfers between devices  78.3 us (33%)
  starting transfers between devices  74.9 us (32%)
  blocking collectives  24.9 us (11%)
  Pallas kernels  23.3 us (10%)
  local copies, waits for them, and re-layouts  17.3 us (7%)
  between operations  14.6 us (6%)
    ppermute x14, waiting for transfers between devices, along_z(): return lax.ppermute(block, 'dp', route)  63.9 us
    ppermute x14, starting transfers between devices, along_z(): return lax.ppermute(block, 'dp', route)  49.1 us
    all_to_all x4, starting transfers between devices, swap(): lax.all_to_all(blocks, axis, split_axis=0, concat_axis=0, tiled=True, axi...  25.8 us
    all_to_all x3, blocking collectives, swap(): lax.all_to_all(blocks, axis, split_axis=0, concat_axis=0, tiled=True, axi...  24.9 us
    pallas_call x10, Pallas kernels, call(): pl.pallas_call(fetching if fetch else body, out_shape=outs, in_specs=spec...  23.3 us
    unnamed x73, local copies, waits for them, and re-layouts  17.1 us
    all_to_all x4, waiting for transfers between devices, swap(): lax.all_to_all(blocks, axis, split_axis=0, concat_axis=0, tiled=True, axi...  14.3 us
  transfers between devices with their start and end apart: 19, of which 10 were waited for; matrix products, arithmetic and copies ran while one was open for 1% of the time, Pallas kernels for 6%

profile of v3, /device:TPU:248, one launch (start us, length us, event | category | flops | bytes accessed | tf_op | source)
XLA Modules:
  0.0 234.3 jit_solution(14249103670386920816)
XLA Ops:
  9.0 10.2 %all_to_all.78 = bf16[4,16,1024]{2,1,0:T(8,128)(2,1)} all-to-all(bf16[4,16,1024]{2,1,0:T(8,128)(2,1)S(1)} %bitcast.29), channel_id=1, replica_groups={{0,16,32,48},{64,80,96,112},{128,144,160,176},{192,208,224,240},{256,27..., dimensions={0} | all-to-all | bytes 262144 | tf_op jit(solution)/shard_map/all_to_all | solution.py:578
  24.3 2.0 pack.1
  26.3 9.1 %all-to-all-start = ((bf16[32,16,1408]{2,1,0:T(8,128)(2,1)}), bf16[32,16,1408]{2,1,0:T(8,128)(2,1)S(1)}, u32[]{:S(2)}, u32[]{:S(2)}) async-start(bf16[32,16,1408]{2,1,0:T(8,128)(2,1)} %bitcast.4), calls=%async_computation | async-start | bytes 2883584 | tf_op jit(solution)/shard_map/all_to_all | solution.py:578
  35.4 4.6 %collective-permute-start = (bf16[512,128]{1,0:T(8,128)(2,1)S(1)}, bf16[512,128]{1,0:T(8,128)(2,1)S(1)}, u32[]{:S(2)}, u32[]{:S(2)}) collective-permute-start(bf16[512,128]{1,0:T(8,128)(2,1)S(1)} %copy-done.10), channel_id=1, source_target_pairs={{0,64},{16,80},{32,96},{48,112},{64,128},{80,144},{96,160},{112,17... | collective-permute-start | bytes 393224 | tf_op jit(solution)/shard_map/ppermute | solution.py:575
  40.0 1.9 collective-permute-start.4
  41.9 26.5 %collective-permute-done.refs_2_ = bf16[512,128]{1,0:T(8,128)(2,1)S(1)} collective-permute-done((bf16[512,128]{1,0:T(8,128)(2,1)S(1)}, bf16[512,128]{1,0:T(8,128)(2,1)S(1)}, u32[]{:S(2)}, u32[]{:S(2)}) %collective-permute-start) | collective-permute-done | bytes 131104 | tf_op jit(solution)/shard_map/ppermute | solution.py:575
  68.5 4.6 %collective-permute-start.1 = (bf16[512,128]{1,0:T(8,128)(2,1)S(1)}, bf16[512,128]{1,0:T(8,128)(2,1)S(1)}, u32[]{:S(2)}, u32[]{:S(2)}) collective-permute-start(bf16[512,128]{1,0:T(8,128)(2,1)S(1)} %collective-permute-done.refs_2_), channel_id=1, source_target_pairs={{0,64},{16,80},{32,96},{48,112},{64,128},{80,144},{96,160},{112,17... | collective-permute-start | bytes 393224 | tf_op jit(solution)/shard_map/ppermute | solution.py:575
  73.1 1.9 collective-permute-start.5
  75.5 5.6 %collective-permute-start.2 = (bf16[512,128]{1,0:T(8,128)(2,1)S(1)}, bf16[512,128]{1,0:T(8,128)(2,1)S(1)}, u32[]{:S(2)}, u32[]{:S(2)}) collective-permute-start(bf16[512,128]{1,0:T(8,128)(2,1)S(1)} %collective-permute-done.1.refs_3_), channel_id=1, source_target_pairs={{0,64},{16,80},{32,96},{48,112},{64,128},{80,144},{96,160},{112,17... | collective-permute-start | bytes 393224 | tf_op jit(solution)/shard_map/ppermute | solution.py:575
  81.1 1.9 collective-permute-start.6
  83.6 5.6 %collective-permute-start.3 = (bf16[512,128]{1,0:T(8,128)(2,1)S(1)}, bf16[512,128]{1,0:T(8,128)(2,1)S(1)}, u32[]{:S(2)}, u32[]{:S(2)}) collective-permute-start(bf16[512,128]{1,0:T(8,128)(2,1)S(1)} %collective-permute-done.2.refs_4_), channel_id=1, source_target_pairs={{0,64},{16,80},{32,96},{48,112},{64,128},{80,144},{96,160},{112,17... | collective-permute-start | bytes 393224 | tf_op jit(solution)/shard_map/ppermute | solution.py:575
  89.2 2.5 %collective-permute-done.3.refs_5_ = bf16[512,128]{1,0:T(8,128)(2,1)S(1)} collective-permute-done((bf16[512,128]{1,0:T(8,128)(2,1)S(1)}, bf16[512,128]{1,0:T(8,128)(2,1)S(1)}, u32[]{:S(2)}, u32[]{:S(2)}) %collective-permute-start.3) | collective-permute-done | bytes 131104 | tf_op jit(solution)/shard_map/ppermute | solution.py:575
  93.3 3.9 %dnormed.1 = bf16[1024,512]{1,0:T(8,128)(2,1)} custom-call(bf16[16,4,16,1024]{3,2,1,0:T(8,128)(2,1)S(1)} %bitcast.34, bf16[512,128]{1,0:T(8,128)(2,1)S(1)} %copy-done.10, bf16[512,128]{1,0:T(8,128)(2,1)S(1)} %collective-permute-done.refs_2_, bf16[512,128]{1,0:T(8,128)(2,1)S(1)} %collective-permute-done.1.refs_3_, ...), custom_call_target="tpu_custom_call" | custom-call | flops 1200000000 | bytes 4194304 | tf_op jit(solution)/shard_map/dnormed/pallas_call | solution.py:49
  97.2 4.4 %all-to-all-start.2 = ((bf16[4,256,512]{2,1,0:T(8,128)(2,1)}), bf16[4,256,512]{2,1,0:T(8,128)(2,1)S(1)}, u32[]{:S(2)}, u32[]{:S(2)}) async-start(bf16[4,256,512]{2,1,0:T(8,128)(2,1)} %bitcast.12), calls=%async_computation.2 | async-start | bytes 2097152 | tf_op jit(solution)/shard_map/all_to_all | solution.py:578
  101.8 3.3 %forward.1 = (bf16[512,256]{1,0:T(8,128)(2,1)S(1)}, bf16[256,512]{1,0:T(8,128)(2,1)S(1)}, f32[256,512]{1,0:T(8,128)S(1)}, f32[256,512]{1,0:T(8,128)S(1)}, f32[4,...) custom-call(s32[1,6]{1,0:T(1,128)S(1)} %copy-done.13, ...), custom_call_target="tpu_custom_call" | custom-call | flops 4000000000 | bytes 5147688 | tf_op jit(solution)/shard_map/forward/pallas_call | solution.py:49
  114.2 6.0 %all_to_all.79 = f32[4,16,256]{2,1,0:T(8,128)S(1)} all-to-all(f32[4,16,256]{2,1,0:T(8,128)S(1)} %bitcast.33), channel_id=1, replica_groups={{0,1,2,3},{4,5,6,7},{8,9,10,11},{12,13,14,15},{16,17,18,19},{20,21,22,2..., dimensions={0} | all-to-all | bytes 131072 | tf_op jit(solution)/shard_map/all_to_all | solution.py:578
  120.3 1.8 dz.1
  122.1 5.3 %backward.1 = (bf16[256,512]{1,0:T(8,128)(2,1)S(1)}, f32[4,512]{1,0:T(4,128)S(1)}, f32[256,128]{1,0:T(8,128)S(1)}, f32[3,128]{1,0:T(4,128)S(1)}, bf16[1024,128]{1,0:T(8,128)(2,1)S(1)}) custom-call(s32[1,6]{1,0:T(1,128)S(1)} %copy-done.13, f32[256,512]{1,0:T(8,128)S(1)} %get-tuple-element.55.refs_1_, f32[256,512]{1,0:T(8,128)S(1)} %copy-done.21, ...), custom_call_target="tpu_custom_call" | custom-call | flops 6000000000 | bytes 3305496 | tf_op jit(solution)/shard_map/backward/pallas_call | solution.py:49
  127.4 8.7 %all_to_all.80 = bf16[4,256,128]{2,1,0:T(8,128)(2,1)S(1)} all-to-all(bf16[4,256,128]{2,1,0:T(8,128)(2,1)S(1)} %bitcast.31), channel_id=1, replica_groups={{0,1,2,3},{4,5,6,7},{8,9,10,11},{12,13,14,15},{16,17,18,19},{20,21,22,2..., dimensions={0} | all-to-all | bytes 524288 | tf_op jit(solution)/shard_map/all_to_all | solution.py:578
  136.2 3.7 %all-to-all-start.6 = ((bf16[4,256,512]{2,1,0:T(8,128)(2,1)}), bf16[4,256,512]{2,1,0:T(8,128)(2,1)S(1)}, u32[]{:S(2)}, u32[]{:S(2)}) async-start(bf16[4,256,512]{2,1,0:T(8,128)(2,1)} %bitcast.20), calls=%async_computation.6 | async-start | bytes 2097152 | tf_op jit(solution)/shard_map/all_to_all | solution.py:578
  140.0 2.5 %share.1 = bf16[512,1408]{1,0:T(8,128)(2,1)} custom-call(s32[1,6]{1,0:T(1,128)S(1)} %copy-done.13, s32[4]{0:T(128)S(1)} %pad_add_fusion.refs_2_.refs_1_.refs_0_, f32[4,256,128]{2,1,0:T(8,128)S(1)} %copy-done.17, f32[4,128]{1,0:T(4,128)S(1)} %pad.13.refs_3_, bf16[256,512]{1,0:T(8,128)(2,1)S(1)} %get-tuple-element.64.refs_4_, ...), custom_call_target="tpu_custom_call" | custom-call | flops 1500000000 | bytes 3159592 | tf_op jit(solution)/shard_map/share/pallas_call | solution.py:49
  142.5 12.6 %all-to-all-done.6 = bf16[4,256,512]{2,1,0:T(8,128)(2,1)S(1)} async-done(((bf16[4,256,512]{2,1,0:T(8,128)(2,1)}), bf16[4,256,512]{2,1,0:T(8,128)(2,1)S(1)}, u32[]{:S(2)}, u32[]{:S(2)}) %all-to-all-start.6) | async-done | bytes 1048608 | tf_op jit(solution)/shard_map/all_to_all | solution.py:578
  155.1 8.7 %all-to-all-start.5 = ((bf16[32,16,1408]{2,1,0:T(8,128)(2,1)}), bf16[32,16,1408]{2,1,0:T(8,128)(2,1)S(1)}, u32[]{:S(2)}, u32[]{:S(2)}) async-start(bf16[32,16,1408]{2,1,0:T(8,128)(2,1)} %bitcast.18), calls=%async_computation.5 | async-start | bytes 2883584 | tf_op jit(solution)/shard_map/all_to_all | solution.py:578
  166.8 2.5 %collective-permute-start.7 = (bf16[512,128]{1,0:T(8,128)(2,1)S(1)}, bf16[512,128]{1,0:T(8,128)(2,1)S(1)}, u32[]{:S(2)}, u32[]{:S(2)}) collective-permute-start(bf16[512,128]{1,0:T(8,128)(2,1)S(1)} %get-tuple-element.77), channel_id=1, source_target_pairs={{0,448},{16,464},{32,480},{48,496},{64,0},{80,16},{96,32},{112,48}... | collective-permute-start | bytes 393224 | tf_op jit(solution)/shard_map/ppermute | solution.py:575
  169.3 4.6 %collective-permute-start.11 = (bf16[512,128]{1,0:T(8,128)(2,1)S(1)}, bf16[512,128]{1,0:T(8,128)(2,1)S(1)}, u32[]{:S(2)}, u32[]{:S(2)}) collective-permute-start(bf16[512,128]{1,0:T(8,128)(2,1)S(1)} %get-tuple-element.81), channel_id=1, source_target_pairs={{0,64},{16,80},{32,96},{48,112},{64,128},{80,144},{96,160},{112,17... | collective-permute-start | bytes 393224 | tf_op jit(solution)/shard_map/ppermute | solution.py:575
  173.9 25.7 %collective-permute-done.7 = bf16[512,128]{1,0:T(8,128)(2,1)S(1)} collective-permute-done((bf16[512,128]{1,0:T(8,128)(2,1)S(1)}, bf16[512,128]{1,0:T(8,128)(2,1)S(1)}, u32[]{:S(2)}, u32[]{:S(2)}) %collective-permute-start.7) | collective-permute-done | bytes 131104 | tf_op jit(solution)/shard_map/ppermute | solution.py:575
  199.6 1.9 collective-permute-start.8
  201.6 5.1 %collective-permute-start.12 = (bf16[512,128]{1,0:T(8,128)(2,1)S(1)}, bf16[512,128]{1,0:T(8,128)(2,1)S(1)}, u32[]{:S(2)}, u32[]{:S(2)}) collective-permute-start(bf16[512,128]{1,0:T(8,128)(2,1)S(1)} %add_convert_fusion.2), channel_id=1, source_target_pairs={{0,64},{16,80},{32,96},{48,112},{64,128},{80,144},{96,160},{112,17... | collective-permute-start | bytes 393224 | tf_op jit(solution)/shard_map/ppermute | solution.py:575
  207.7 1.9 collective-permute-start.9
  209.7 5.1 %collective-permute-start.13 = (bf16[512,128]{1,0:T(8,128)(2,1)S(1)}, bf16[512,128]{1,0:T(8,128)(2,1)S(1)}, u32[]{:S(2)}, u32[]{:S(2)}) collective-permute-start(bf16[512,128]{1,0:T(8,128)(2,1)S(1)} %add_convert_fusion.1), channel_id=1, source_target_pairs={{0,64},{16,80},{32,96},{48,112},{64,128},{80,144},{96,160},{112,17... | collective-permute-start | bytes 393224 | tf_op jit(solution)/shard_map/ppermute | solution.py:575
  215.8 1.9 collective-permute-start.10
  217.8 6.1 %collective-permute-done.10 = bf16[512,128]{1,0:T(8,128)(2,1)S(1)} collective-permute-done((bf16[512,128]{1,0:T(8,128)(2,1)S(1)}, bf16[512,128]{1,0:T(8,128)(2,1)S(1)}, u32[]{:S(2)}, u32[]{:S(2)}) %collective-permute-start.10) | collective-permute-done | bytes 131104 | tf_op jit(solution)/shard_map/ppermute | solution.py:575
  (105 shorter events, 27.7 us)
Async XLA Ops:
  7.2 84.5 %all-gather.2.cloned.1.call-start = ((), (), s32[]{:S(2)}) async-start(), calls=%async_computation.7 | async-start | bytes 2228224 | tf_op jit(solution)/shard_map/all_gather | solution.py:591
  26.3 9.1 %copy-start.10 = (bf16[512,128]{1,0:T(8,128)(2,1)S(1)}, bf16[512,128]{1,0:T(8,128)(2,1)}, u32[]{:S(2)}) copy-start(bf16[512,128]{1,0:T(8,128)(2,1)} %refs_1_.5) | copy-start | bytes 393220
  26.3 70.9 %all-to-all-start = ((bf16[32,16,1408]{2,1,0:T(8,128)(2,1)}), bf16[32,16,1408]{2,1,0:T(8,128)(2,1)S(1)}, u32[]{:S(2)}, u32[]{:S(2)}) async-start(bf16[32,16,1408]{2,1,0:T(8,128)(2,1)} %bitcast.4), calls=%async_computation | async-start | bytes 2883584 | tf_op jit(solution)/shard_map/all_to_all | solution.py:578
  35.4 33.0 %collective-permute-start = (bf16[512,128]{1,0:T(8,128)(2,1)S(1)}, bf16[512,128]{1,0:T(8,128)(2,1)S(1)}, u32[]{:S(2)}, u32[]{:S(2)}) collective-permute-start(bf16[512,128]{1,0:T(8,128)(2,1)S(1)} %copy-done.10), channel_id=1, source_target_pairs={{0,64},{16,80},{32,96},{48,112},{64,128},{80,144},{96,160},{112,17... | collective-permute-start | bytes 393224 | tf_op jit(solution)/shard_map/ppermute | solution.py:575
  40.0 33.0 %collective-permute-start.4 = (bf16[512,128]{1,0:T(8,128)(2,1)S(1)}, bf16[512,128]{1,0:T(8,128)(2,1)S(1)}, u32[]{:S(2)}, u32[]{:S(2)}) collective-permute-start(bf16[512,128]{1,0:T(8,128)(2,1)S(1)} %copy-done.10), channel_id=1, source_target_pairs={{0,448},{16,464},{32,480},{48,496},{64,0},{80,16},{96,32},{112,48}... | collective-permute-start | bytes 393224 | tf_op jit(solution)/shard_map/ppermute | solution.py:575
  68.5 7.1 %collective-permute-start.1 = (bf16[512,128]{1,0:T(8,128)(2,1)S(1)}, bf16[512,128]{1,0:T(8,128)(2,1)S(1)}, u32[]{:S(2)}, u32[]{:S(2)}) collective-permute-start(bf16[512,128]{1,0:T(8,128)(2,1)S(1)} %collective-permute-done.refs_2_), channel_id=1, source_target_pairs={{0,64},{16,80},{32,96},{48,112},{64,128},{80,144},{96,160},{112,17... | collective-permute-start | bytes 393224 | tf_op jit(solution)/shard_map/ppermute | solution.py:575
  73.1 8.1 %collective-permute-start.5 = (bf16[512,128]{1,0:T(8,128)(2,1)S(1)}, bf16[512,128]{1,0:T(8,128)(2,1)S(1)}, u32[]{:S(2)}, u32[]{:S(2)}) collective-permute-start(bf16[512,128]{1,0:T(8,128)(2,1)S(1)} %collective-permute-done.4.refs_8_), channel_id=1, source_target_pairs={{0,448},{16,464},{32,480},{48,496},{64,0},{80,16},{96,32},{112,48}... | collective-permute-start | bytes 393224 | tf_op jit(solution)/shard_map/ppermute | solution.py:575
  75.5 8.1 %collective-permute-start.2 = (bf16[512,128]{1,0:T(8,128)(2,1)S(1)}, bf16[512,128]{1,0:T(8,128)(2,1)S(1)}, u32[]{:S(2)}, u32[]{:S(2)}) collective-permute-start(bf16[512,128]{1,0:T(8,128)(2,1)S(1)} %collective-permute-done.1.refs_3_), channel_id=1, source_target_pairs={{0,64},{16,80},{32,96},{48,112},{64,128},{80,144},{96,160},{112,17... | collective-permute-start | bytes 393224 | tf_op jit(solution)/shard_map/ppermute | solution.py:575
  81.1 8.1 %collective-permute-start.6 = (bf16[512,128]{1,0:T(8,128)(2,1)S(1)}, bf16[512,128]{1,0:T(8,128)(2,1)S(1)}, u32[]{:S(2)}, u32[]{:S(2)}) collective-permute-start(bf16[512,128]{1,0:T(8,128)(2,1)S(1)} %collective-permute-done.5.refs_7_), channel_id=1, source_target_pairs={{0,448},{16,464},{32,480},{48,496},{64,0},{80,16},{96,32},{112,48}... | collective-permute-start | bytes 393224 | tf_op jit(solution)/shard_map/ppermute | solution.py:575
  83.6 8.1 %collective-permute-start.3 = (bf16[512,128]{1,0:T(8,128)(2,1)S(1)}, bf16[512,128]{1,0:T(8,128)(2,1)S(1)}, u32[]{:S(2)}, u32[]{:S(2)}) collective-permute-start(bf16[512,128]{1,0:T(8,128)(2,1)S(1)} %collective-permute-done.2.refs_4_), channel_id=1, source_target_pairs={{0,64},{16,80},{32,96},{48,112},{64,128},{80,144},{96,160},{112,17... | collective-permute-start | bytes 393224 | tf_op jit(solution)/shard_map/ppermute | solution.py:575
  97.1 4.5 %copy-start.32 = (f32[8]{0:T(128)S(1)}, f32[8]{0:T(128)}, u32[]{:S(2)}) copy-start(f32[8]{0:T(128)} %param.26) | copy-start | bytes 100
  97.1 4.6 %copy-start.33 = (f32[8]{0:T(128)S(1)}, f32[8]{0:T(128)}, u32[]{:S(2)}) copy-start(f32[8]{0:T(128)} %param.25) | copy-start | bytes 100
  97.1 4.6 %copy-start.34 = (f32[8]{0:T(128)S(1)}, f32[8]{0:T(128)}, u32[]{:S(2)}) copy-start(f32[8]{0:T(128)} %param.24) | copy-start | bytes 100
  97.2 4.6 %copy-start.7 = (f32[4,1024]{1,0:T(4,128)S(1)}, f32[4,1024]{1,0:T(4,128)}, u32[]{:S(2)}) copy-start(f32[4,1024]{1,0:T(4,128)} %refs_4_.3) | copy-start | bytes 49156
  97.2 4.6 %copy-start.11 = (f32[4,512]{1,0:T(4,128)S(1)}, f32[4,512]{1,0:T(4,128)}, u32[]{:S(2)}) copy-start(f32[4,512]{1,0:T(4,128)} %refs_11_.1) | copy-start | bytes 24580
  97.2 4.6 %copy-start.13 = (s32[1,6]{1,0:T(1,128)S(1)}, s32[1,6]{1,0:T(1,128)}, u32[]{:S(2)}) copy-start(s32[1,6]{1,0:T(1,128)} %refs_0_.7) | copy-start | bytes 76
  97.2 16.1 %all-to-all-start.2 = ((bf16[4,256,512]{2,1,0:T(8,128)(2,1)}), bf16[4,256,512]{2,1,0:T(8,128)(2,1)S(1)}, u32[]{:S(2)}, u32[]{:S(2)}) async-start(bf16[4,256,512]{2,1,0:T(8,128)(2,1)} %bitcast.12), calls=%async_computation.2 | async-start | bytes 2097152 | tf_op jit(solution)/shard_map/all_to_all | solution.py:578
  101.8 11.5 %copy-start.12 = (f32[512]{0:T(512)S(1)}, f32[512]{0:T(512)}, u32[]{:S(2)}) copy-start(f32[512]{0:T(512)} %param.27) | copy-start | bytes 6148
  113.3 7.0 %copy-start.15 = (f32[256,512]{1,0:T(8,128)S(1)}, f32[256,512]{1,0:T(8,128)}, u32[]{:S(2)}) copy-start(f32[256,512]{1,0:T(8,128)} %copy-done.14) | copy-start | bytes 1572868
  120.3 1.8 copy-start.25
  127.4 12.6 %copy-start.17 = (f32[4,256,128]{2,1,0:T(8,128)S(1)}, f32[4,256,128]{2,1,0:T(8,128)}, u32[]{:S(2)}) copy-start(f32[4,256,128]{2,1,0:T(8,128)} %copy-done.16) | copy-start | bytes 1572868
  127.4 12.6 %copy-start.19 = (bf16[512,256]{1,0:T(8,128)(2,1)S(1)}, bf16[512,256]{1,0:T(8,128)(2,1)}, u32[]{:S(2)}) copy-start(bf16[512,256]{1,0:T(8,128)(2,1)} %copy-done.18) | copy-start | bytes 786436
  136.2 18.9 %all-to-all-start.6 = ((bf16[4,256,512]{2,1,0:T(8,128)(2,1)}), bf16[4,256,512]{2,1,0:T(8,128)(2,1)S(1)}, u32[]{:S(2)}, u32[]{:S(2)}) async-start(bf16[4,256,512]{2,1,0:T(8,128)(2,1)} %bitcast.20), calls=%async_computation.6 | async-start | bytes 2097152 | tf_op jit(solution)/shard_map/all_to_all | solution.py:578
  155.1 69.5 %all-to-all-start.5 = ((bf16[32,16,1408]{2,1,0:T(8,128)(2,1)}), bf16[32,16,1408]{2,1,0:T(8,128)(2,1)S(1)}, u32[]{:S(2)}, u32[]{:S(2)}) async-start(bf16[32,16,1408]{2,1,0:T(8,128)(2,1)} %bitcast.18), calls=%async_computation.5 | async-start | bytes 2883584 | tf_op jit(solution)/shard_map/all_to_all | solution.py:578
  166.8 57.8 %copy-start.5 = (s32[16]{0:T(128)S(1)}, s32[16]{0:T(128)}, u32[]{:S(2)}) copy-start(s32[16]{0:T(128)} %bin_ref.1) | copy-start | bytes 196
  166.8 32.8 %collective-permute-start.7 = (bf16[512,128]{1,0:T(8,128)(2,1)S(1)}, bf16[512,128]{1,0:T(8,128)(2,1)S(1)}, u32[]{:S(2)}, u32[]{:S(2)}) collective-permute-start(bf16[512,128]{1,0:T(8,128)(2,1)S(1)} %get-tuple-element.77), channel_id=1, source_target_pairs={{0,448},{16,464},{32,480},{48,496},{64,0},{80,16},{96,32},{112,48}... | collective-permute-start | bytes 393224 | tf_op jit(solution)/shard_map/ppermute | solution.py:575
  169.3 32.3 %collective-permute-start.11 = (bf16[512,128]{1,0:T(8,128)(2,1)S(1)}, bf16[512,128]{1,0:T(8,128)(2,1)S(1)}, u32[]{:S(2)}, u32[]{:S(2)}) collective-permute-start(bf16[512,128]{1,0:T(8,128)(2,1)S(1)} %get-tuple-element.81), channel_id=1, source_target_pairs={{0,64},{16,80},{32,96},{48,112},{64,128},{80,144},{96,160},{112,17... | collective-permute-start | bytes 393224 | tf_op jit(solution)/shard_map/ppermute | solution.py:575
  199.6 8.1 %collective-permute-start.8 = (bf16[512,128]{1,0:T(8,128)(2,1)S(1)}, bf16[512,128]{1,0:T(8,128)(2,1)S(1)}, u32[]{:S(2)}, u32[]{:S(2)}) collective-permute-start(bf16[512,128]{1,0:T(8,128)(2,1)S(1)} %add_convert_fusion.5), channel_id=1, source_target_pairs={{0,448},{16,464},{32,480},{48,496},{64,0},{80,16},{96,32},{112,48}... | collective-permute-start | bytes 393224 | tf_op jit(solution)/shard_map/ppermute | solution.py:575
  201.6 8.1 %collective-permute-start.12 = (bf16[512,128]{1,0:T(8,128)(2,1)S(1)}, bf16[512,128]{1,0:T(8,128)(2,1)S(1)}, u32[]{:S(2)}, u32[]{:S(2)}) collective-permute-start(bf16[512,128]{1,0:T(8,128)(2,1)S(1)} %add_convert_fusion.2), channel_id=1, source_target_pairs={{0,64},{16,80},{32,96},{48,112},{64,128},{80,144},{96,160},{112,17... | collective-permute-start | bytes 393224 | tf_op jit(solution)/shard_map/ppermute | solution.py:575
  207.7 8.1 %collective-permute-start.9 = (bf16[512,128]{1,0:T(8,128)(2,1)S(1)}, bf16[512,128]{1,0:T(8,128)(2,1)S(1)}, u32[]{:S(2)}, u32[]{:S(2)}) collective-permute-start(bf16[512,128]{1,0:T(8,128)(2,1)S(1)} %add_convert_fusion.4), channel_id=1, source_target_pairs={{0,448},{16,464},{32,480},{48,496},{64,0},{80,16},{96,32},{112,48}... | collective-permute-start | bytes 393224 | tf_op jit(solution)/shard_map/ppermute | solution.py:575
  209.7 8.1 %collective-permute-start.13 = (bf16[512,128]{1,0:T(8,128)(2,1)S(1)}, bf16[512,128]{1,0:T(8,128)(2,1)S(1)}, u32[]{:S(2)}, u32[]{:S(2)}) collective-permute-start(bf16[512,128]{1,0:T(8,128)(2,1)S(1)} %add_convert_fusion.1), channel_id=1, source_target_pairs={{0,64},{16,80},{32,96},{48,112},{64,128},{80,144},{96,160},{112,17... | collective-permute-start | bytes 393224 | tf_op jit(solution)/shard_map/ppermute | solution.py:575
  215.8 8.1 %collective-permute-start.10 = (bf16[512,128]{1,0:T(8,128)(2,1)S(1)}, bf16[512,128]{1,0:T(8,128)(2,1)S(1)}, u32[]{:S(2)}, u32[]{:S(2)}) collective-permute-start(bf16[512,128]{1,0:T(8,128)(2,1)S(1)} %add_convert_fusion.3), channel_id=1, source_target_pairs={{0,448},{16,464},{32,480},{48,496},{64,0},{80,16},{96,32},{112,48}... | collective-permute-start | bytes 393224 | tf_op jit(solution)/shard_map/ppermute | solution.py:575
  (22 other events, 24.0 us)
Sparse Core Ops, SparseCore 0:
  19.3 40.8 all-gather.1

commit v4 on v3

--- a/solution.py
+++ b/solution.py
@@ -10,6 +10,7 @@
 
 GROUPS = 4
 DP_INNER = 4
+CORES = 2
 PANEL = 16
 LANES = 128
 FAR = -1e30
@@ -19,40 +20,46 @@
 bf16 = jnp.bfloat16
 smem = pl.BlockSpec(memory_space=pltpu.SMEM)
 vmem = pl.BlockSpec(memory_space=pltpu.VMEM)
-anywhere = pl.BlockSpec(memory_space=pl.ANY)
-
-
-def call(body, outs, ins, scalars=0, fetch=(), cost=1, scratch=(), name=None):
-    size = sum(math.prod(o.shape) * o.dtype.itemsize for o in outs)
-    size += sum(math.prod(i.shape) * i.dtype.itemsize for i in ins)
-    specs = [smem] * scalars + [vmem] * (len(ins) - scalars)
-    for k in fetch:
-        specs[k] = anywhere
-    kept = len(ins) + len(outs) + len(scratch)
-
-    def fetching(*refs):
-        args, held, sems = list(refs[:kept]), refs[kept:-1], refs[-1]
+vmem = pl.BlockSpec(memory_space=pltpu.VMEM)
+hbm = pl.BlockSpec(memory_space=pltpu.HBM)
+
+
+def call(body, outs, ins, scalars=0, moves=False, cost=1, scratch=(), name=None):
+    count = len(ins)
+    size = sum(math.prod(a.shape) * a.dtype.itemsize for a in list(outs) + list(ins))
+    moved = list(ins[scalars:]) + list(outs) if moves else []
+
+    def moving(*refs):
+        far, rest = refs[scalars : count + len(outs)], refs[count + len(outs) :]
+        held, own, sems = rest[: len(moved)], rest[len(moved) : -1], rest[-1]
         copies = []
-        for n, k in enumerate(fetch):
-            copies.append(pltpu.make_async_copy(args[k], held[n], sems.at[n]))
-            args[k] = held[n]
-        for copy in copies:
+        for n in range(len(moved)):
+            inward = n < count - scalars
+            ends = (far[n], held[n]) if inward else (held[n], far[n])
+            copies.append(pltpu.make_async_copy(*ends, sems.at[n]))
+        inward, outward = copies[: count - scalars], copies[count - scalars :]
+        for copy in inward:
             copy.start()
-        for copy in copies:
+        for copy in inward:
             copy.wait()
-        body(*args)
-
-    extra = []
-    if fetch:
-        extra = [pltpu.VMEM(ins[k].shape, ins[k].dtype) for k in fetch]
-        extra.append(pltpu.SemaphoreType.DMA((len(fetch),)))
+        body(*refs[:scalars], *held, *own)
+        for copy in outward:
+            copy.start()
+        for copy in outward:
+            copy.wait()
+
+    place = hbm if moves else vmem
+    extra = [pltpu.VMEM(a.shape, a.dtype) for a in moved]
+    extra += list(scratch)
+    if moves:
+        extra.append(pltpu.SemaphoreType.DMA((len(moved),)))
     return pl.pallas_call(
-        fetching if fetch else body,
+        moving if moves else body,
         out_shape=outs,
-        in_specs=specs,
-        out_specs=[vmem] * len(outs),
-        scratch_shapes=list(scratch) + extra,
-        compiler_params=pltpu.CompilerParams(vmem_limit_bytes=16 << 20),
+        in_specs=[smem] * scalars + [place] * (count - scalars),
+        out_specs=[place] * len(outs),
+        scratch_shapes=extra,
+        compiler_params=pltpu.CompilerParams(vmem_limit_bytes=(58 if moves else 16) << 20),
         cost_estimate=pl.CostEstimate(
             flops=int(cost * 1e6), bytes_accessed=size, transcendentals=0
         ),
@@ -142,19 +149,15 @@
     return (lane_ids(shape) // head_width == row_ids(shape)).astype(f32)
 
 
-def pack_dout_body(inner, co_ref, dout_ref, d_ref):
+def pack_body(bin_ref, slot_ref, co_ref, x_ref, z_ref, bc_ref, dt_ref, dout_ref, a_ref, d_ref):
     rows = dout_ref.shape[0]
-    outer = dout_ref.shape[1] // (LANES * inner)
-    for z in range(outer):
-        block = lax.rem(co_ref[3] + outer - z, outer) * inner * LANES
-        low = pl.multiple_of(block, LANES)
-        for x in range(inner):
+    inner = d_ref.shape[0] // rows
+    for x in range(inner):
+        for z in range(d_ref.shape[1] // LANES):
+            low = (z * inner + x) * LANES
             d_ref[x * rows : (x + 1) * rows, z * LANES : (z + 1) * LANES] = dout_ref[
-                :, pl.ds(low + x * LANES, LANES)
+                :, low : low + LANES
             ]
-
-
-def pack_body(bin_ref, slot_ref, co_ref, x_ref, z_ref, bc_ref, dt_ref, a_ref):
     npan = bin_ref.shape[0]
     channels = x_ref.shape[1]
     heads = dt_ref.shape[1]
@@ -266,30 +269,47 @@
     return dot_tn(total[:8], eighth, exact), dot_tn(total[8:], eighth, exact)
 
 
-def rows_of(out_ref, k):
-    tensor, _, panel, columns = out_ref.shape
-    return out_ref[:, k].reshape(tensor * panel, columns)
-
-
-def dnormed_body(out_ref, *refs):
-    blocks, p_ref = refs[:-1], refs[-1]
-    w = jnp.concatenate([block[...] for block in blocks], axis=1)
-    inner = out_ref.shape[1]
-    rows = p_ref.shape[0] // inner
+def collect_body(co_ref, *refs):
+    blocks, half_ref = refs[:-1], refs[-1]
+    count = len(blocks)
+    for k, block in enumerate(blocks):
+        half_ref[lax.rem(co_ref[1] + count - k, count)] = block[...]
+
+
+def dnormed_body(co_ref, mine_ref, other_ref, w_ref, p_ref, rows_ref):
+    outer = w_ref.shape[0]
+    inner = rows_ref.shape[0]
+    panel = mine_ref.shape[1] // inner
+    w = jnp.concatenate([w_ref[z] for z in range(outer)], axis=1)
+    first = co_ref[2] == 0
+    count, columns = rows_ref.shape[1:]
     for k in range(inner):
-        p_ref[k * rows : (k + 1) * rows] = dot_nt(rows_of(out_ref, k), w).astype(bf16)
-
-
-def term_body(scale, out_ref, normed_ref, *terms):
-    inner = out_ref.shape[1]
-    rows = normed_ref.shape[0] // inner
+        at = slice(k * panel, (k + 1) * panel)
+        mine, other = mine_ref[:, at], other_ref[:, at]
+        both = jnp.stack([jnp.where(first, mine, other), jnp.where(first, other, mine)], axis=1)
+        rows = both.reshape(count, columns)
+        rows_ref[k] = rows
+        p_ref[k * count : (k + 1) * count] = dot_nt(rows, w).astype(bf16)
+
+
+def term_body(scale, rows_ref, normed_ref, term_ref):
+    inner, count = rows_ref.shape[:2]
     total = None
     for k in range(inner):
-        part = dot_tn(normed_ref[k * rows : (k + 1) * rows], rows_of(out_ref, k))
+        part = dot_tn(normed_ref[k * count : (k + 1) * count], rows_ref[k])
         total = part if total is None else total + part
     total = (total * scale).astype(bf16)
-    for k, term_ref in enumerate(terms):
-        term_ref[...] = total[:, k * LANES : (k + 1) * LANES]
+    channels = total.shape[0]
+    for k in range(term_ref.shape[0] // channels):
+        term_ref[k * channels : (k + 1) * channels] = total[:, k * LANES : (k + 1) * LANES]
+
+
+def gather_body(recv_ref, grad_ref):
+    count = grad_ref.shape[0]
+    total = recv_ref[:count].astype(f32)
+    for k in range(1, recv_ref.shape[0] // count):
+        total = total + recv_ref[k * count : (k + 1) * count].astype(f32)
+    grad_ref[...] = total.astype(bf16)
 
 
 def cross_body(gated_ref, gain_ref, parts_ref, dnormed_ref, sums_ref):
@@ -345,6 +365,7 @@
     width,
     heads,
     len_ref,
+    co_ref,
     dy_ref,
     xpre_ref,
     xraw_ref,
@@ -362,8 +383,9 @@
     dcx_ref,
     ddt_ref,
     dheads_ref,
-    pieces_ref,
+    *refs,
 ):
+    pieces_refs, both_ref = refs[:-1], refs[-1]
     rows, channels = xraw_ref.shape
     pair = bcact_ref.shape[1]
     state = pair // 2
@@ -426,14 +448,16 @@
         dot_tn(dsb, bcact_ref[:, state:]),
         dot_nn(dsb, bcact_ref[:, :state]),
     )
-    share = pieces_ref.shape[1] // 2
-    for s in range(pieces_ref.shape[0] // rows):
+    share = LANES // 2
+    for s in range(len(pieces_refs)):
         low_lane = (s * share) % state
         tile = dbc[s * share // state][:, low_lane // LANES * LANES : (low_lane // LANES + 1) * LANES]
         if low_lane % LANES:
             tile = pltpu.roll(tile, share, 1)
         tile = jnp.where(lane_ids(tile.shape) < share, tile, 0.0)
-        pieces_ref[s * rows : (s + 1) * rows] = tile.astype(bf16)
+        both_ref[jnp.bitwise_xor(co_ref[5], s)] = tile.astype(bf16)
+    for s, piece_ref in enumerate(pieces_refs):
+        piece_ref[...] = both_ref[s]
 
 
 def share_body(
@@ -449,21 +473,20 @@
     dcx_ref,
     dgain_ref,
     dheads_ref,
-    parts_ref,
-    back_ref,
-    small_ref,
+    *refs,
 ):
+    parts, (back_ref, small_ref) = refs[:-2], refs[-2:]
     rows = ddt_ref.shape[0]
     channels = gx_ref.shape[1]
     slots = back_ref.shape[0]
     keeps = keep_masks(len_ref, rows, width)
-    raw = share_ref[co_ref[2]]
+    raw = share_ref[co_ref[5]]
     taps = taps_ref[...]
     pre = conv(raw, taps, keeps)
     sig = jax.nn.sigmoid(pre)
-    dact = parts_ref[:rows].astype(f32)
-    for k in range(1, parts_ref.shape[0] // rows):
-        dact = dact + parts_ref[k * rows : (k + 1) * rows].astype(f32)
+    dact = parts[0][...].astype(f32)
+    for part in parts[1:]:
+        dact = dact + part[...].astype(f32)
     draw, dtaps = conv_back(dact * (sig * (1.0 + pre * (1.0 - sig))), raw, taps, keeps)
     share = LANES // 2
     meta = draw + pltpu.roll(ddt_ref[...], share, 1)
@@ -566,47 +589,63 @@
     columns = outer * LANES
 
     z_index = lax.axis_index("dp") // inner
-    coords = jnp.stack([group, x_index, local, z_index]).astype(jnp.int32)
+    coords = jnp.stack(
+        [group, t_index // CORES, t_index % CORES, z_index, x_index, local]
+    ).astype(jnp.int32)
     over_x = [[z * inner + x for x in range(inner)] for z in range(outer)]
+    over_z = [[z * inner + x for z in range(outer)] for x in range(inner)]
     in_group = [[g * members + m for m in range(members)] for g in range(GROUPS)]
 
     def along_z(block, shift):
         route = [(d, (d + shift * inner) % dp) for d in range(dp)]
         return lax.ppermute(block, "dp", route)
+
+    def along_y(block, shift):
+        route = [(t, (t + shift * CORES) % tensor) for t in range(tensor)]
+        return lax.ppermute(block, "tensor", route)
+
+    def partner(block, flip):
+        return lax.ppermute(block, "tensor", [(t, t ^ flip) for t in range(tensor)])
 
     def swap(blocks, axis, groups=None):
         return lax.all_to_all(
             blocks, axis, split_axis=0, concat_axis=0, tiled=True, axis_index_groups=groups
         )
 
-    (d_parts,) = call(
-        functools.partial(pack_dout_body, inner),
-        [shaped((inner * dout.shape[0], columns), bf16)],
-        [coords, dout],
+    w_cols = lax.all_gather(
+        w_out, "dp", axis=0, tiled=True, axis_index_groups=over_z
+    ).reshape(outer, channels, LANES)
+
+    send, d_parts = call(
+        pack_body,
+        [
+            shaped((slots, 2 * channels + pair + LANES), bf16),
+            shaped((inner * dout.shape[0], columns), bf16),
+        ],
+        [panel_bin, panel_slot, coords, x_in, z_in, bc_in, dt_in, dout],
+        scalars=3,
+        moves=True,
+        name="pack",
+    )
+    d_own = swap(d_parts, "dp", over_x)
+    send, d_own = lax.optimization_barrier((send, d_own))
+    recv = swap(send, "dp")
+    ring_y = tensor // CORES
+    ups, downs = [d_own], [d_own]
+    for step in range(1, ring_y // 2 + 1):
+        ups.append(along_y(ups[-1], 1))
+        if step < ring_y - ring_y // 2:
+            downs.append(along_y(downs[-1], -1))
+    blocks = ups + downs[:0:-1]
+    blocks[1], w_cols = lax.optimization_barrier((blocks[1], w_cols))
+    (mine,) = call(
+        collect_body,
+        [shaped((ring_y,) + d_own.shape, bf16)],
+        [coords] + blocks,
         scalars=1,
-        fetch=(1,),
-        name="pack_dout",
-    )
-    d_own = swap(d_parts, "dp", over_x)
-    out_rows = lax.all_gather(d_own, "tensor", axis=0, tiled=True)
-    out_rows = out_rows.reshape(tensor, inner, dout.shape[0], columns)
-
-    (send,) = call(
-        pack_body,
-        [shaped((slots, 2 * channels + pair + LANES), bf16)],
-        [panel_bin, panel_slot, coords, x_in, z_in, bc_in, dt_in],
-        scalars=3,
-        fetch=(3, 4, 5, 6),
-        name="pack",
-    )
-    recv = swap(send, "dp")
-
-    ups, downs = [w_out], [w_out]
-    for step in range(1, outer // 2 + 1):
-        ups.append(along_z(ups[-1], 1))
-        if step < outer - outer // 2:
-            downs.append(along_z(downs[-1], -1))
-    w_cols = ups + downs[:0:-1]
+        name="collect",
+    )
+    other = partner(mine, 1)
 
     bias_row = jnp.pad(dt_bias, (0, LANES - heads))[None, :]
     alog_row = jnp.pad(a_log, (0, LANES - heads))[None, :]
@@ -650,16 +689,15 @@
         ],
         [lengths, coords, recv, conv_x, conv_bc, bias_row, alog_row, skip_row],
         scalars=2,
-        fetch=(3, 4, 5, 6, 7),
         cost=4000,
         name="forward",
     )
 
-    (partial,) = call(
+    partial, out_rows = call(
         dnormed_body,
-        [shaped((inner * rows, channels), bf16)],
-        [out_rows] + w_cols,
-        fetch=range(outer + 1),
+        [shaped((inner * rows, channels), bf16), shaped((inner, rows, columns), bf16)],
+        [coords, mine, other, w_cols],
+        scalars=1,
         cost=1200,
         name="dnormed",
     )
@@ -683,17 +721,18 @@
         name="dz",
     )
 
-    gx, dcx, ddt, dheads, pieces = call(
+    gx, dcx, ddt, dheads, *pieces = call(
         functools.partial(backward_body, width, heads),
         [
             shaped((rows, channels), bf16),
             shaped((width, channels), f32),
             shaped((rows, LANES), f32),
             shaped((3, LANES), f32),
-            shaped((members * rows, LANES), bf16),
-        ],
+        ]
+        + [shaped((rows, LANES), bf16)] * members,
         [
             lengths,
+            coords,
             dy,
             xpre,
             xraw,
@@ -708,20 +747,21 @@
             alog_row,
             skip_row,
         ],
-        scalars=1,
-        fetch=range(2, 14),
+        scalars=2,
         cost=6000,
+        scratch=[pltpu.VMEM((members, rows, LANES), bf16)],
         name="backward",
     )
 
-    terms = call(
+    normed_all, gx = lax.optimization_barrier((swap(normed, "dp", over_x), gx))
+    (term,) = call(
         functools.partial(term_body, scale),
-        [shaped((channels, LANES), bf16)] * outer,
-        [out_rows, swap(normed, "dp", over_x)],
-        fetch=(0,),
+        [shaped((outer * channels, LANES), bf16)],
+        [out_rows, normed_all],
         cost=1200,
         name="term",
     )
+    terms = swap(term, "dp", over_z)
     (back,) = call(
         functools.partial(share_body, width),
         [shaped((slots, 2 * channels + LANES + channels // 2), bf16)],
@@ -737,28 +777,19 @@
             dcx,
             dgain,
             dheads,
-            swap(pieces, "tensor", in_group),
-        ],
+            pieces[0],
+        ]
+        + [partner(pieces[flip], flip) for flip in range(1, members)],
         scalars=2,
-        fetch=(2, 3, 5, 7, 9),
         cost=1500,
         scratch=[pltpu.VMEM((8, channels), f32)],
         name="share",
     )
+    back, terms = lax.optimization_barrier((back, terms))
     home = swap(back, "dp")
-
-    def add(moved, term):
-        return (moved.astype(f32) + term.astype(f32)).astype(bf16)
-
-    far = outer // 2
-    down, up = terms[far], terms[far + 1]
-    for k in range(far - 1, 0, -1):
-        down = add(along_z(down, -1), terms[k])
-    for k in range(far + 2, outer):
-        up = add(along_z(up, 1), terms[k])
-    grad_wout = (
-        along_z(down, -1).astype(f32) + along_z(up, 1).astype(f32) + terms[0].astype(f32)
-    ).astype(bf16)
+    (grad_wout,) = call(
+        gather_body, [shaped((channels, LANES), bf16)], [terms], name="gather"
+    )
 
     grad_x, grad_z, grad_bc, grad_dt, grad_cx, grad_cbc, grad_gain, grad_heads = call(
         functools.partial(home_body, scale, heads),

time: 235 us -> 216 us (0.919)
  the two profiles are of different devices: /device:TPU:248 before, /device:TPU:2 now
where the time goes in v4:
time: 216 us; the launch traced here: 214 us
  waiting for transfers between devices  74.8 us (35%)
  starting transfers between devices  63.2 us (29%)
  Pallas kernels  22.6 us (10%)
  blocking collectives  20.4 us (9%)
  local copies, waits for them, and re-layouts  19 us (9%)
  between operations  14.4 us (7%)
    all_to_all x5, waiting for transfers between devices, swap(): lax.all_to_all(blocks, axis, split_axis=0, concat_axis=0, tiled=True, axi...  60 us
    all_to_all x5, starting transfers between devices, swap(): lax.all_to_all(blocks, axis, split_axis=0, concat_axis=0, tiled=True, axi...  30.1 us
    ppermute x7, starting transfers between devices, along_y(): return lax.ppermute(block, 'tensor', route)  23.3 us
    pallas_call x11, Pallas kernels, call(): pl.pallas_call(moving if moves else body, out_shape=outs, in_specs=[smem]...  22.6 us
    all_to_all x2, blocking collectives, swap(): lax.all_to_all(blocks, axis, split_axis=0, concat_axis=0, tiled=True, axi...  20.4 us
    unnamed x71, local copies, waits for them, and re-layouts  18.1 us
    ppermute x4, starting transfers between devices, partner(): return lax.ppermute(block, 'tensor', [(t, t ^ flip) for t in range(tensor)])  9.77 us
    all_gather x1, waiting for transfers between devices, per_device(): lax.all_gather(w_out, 'dp', axis=0, tiled=True, axis_index_groups=over_z)  5.45 us
  transfers between devices with their start and end apart: 17, of which 11 were waited for; matrix products, arithmetic and copies ran while one was open for 1% of the time, Pallas kernels for 8%

profile of v4, /device:TPU:2, one launch (start us, length us, event | category | flops | bytes accessed | tf_op | source)
XLA Modules:
  0.0 214.3 jit_solution(327973053618081242)
XLA Ops:
  10.0 3.3 %pack.1 = (bf16[512,1408]{1,0:T(8,128)(2,1)}, bf16[64,1024]{1,0:T(8,128)(2,1)}) custom-call(s32[16]{0:T(128)} %bin_ref.1, s32[16]{0:T(128)} %refs_1_.1, s32[6]{0:T(128)} %stack.27.refs_2_.co_ref, bf16[256,512]{1,0:T(8,128)(2,1)} %refs_3_.1, bf16[256,512]{1,0:T(8,128)(2,1)} %refs_4_.1, bf16[256,1024]{1,0:T(8,128)(2,1)} %refs_5_.1, ...), custom_call_target="tpu_custom_call" | custom-call | flops 1000000 | bytes 2756760 | tf_op jit(solution)/shard_map/pack/pallas_call | solution.py:56
  13.3 13.7 %all_to_all.80 = bf16[4,16,1024]{2,1,0:T(8,128)(2,1)S(1)} all-to-all(bf16[4,16,1024]{2,1,0:T(8,128)(2,1)} %bitcast.42), channel_id=1, replica_groups={{0,16,32,48},{64,80,96,112},{128,144,160,176},{192,208,224,240},{256,27..., dimensions={0} | all-to-all | bytes 262144 | tf_op jit(solution)/shard_map/all_to_all | solution.py:611
  27.0 8.3 %all-to-all-start.1 = ((bf16[32,16,1408]{2,1,0:T(8,128)(2,1)}), bf16[32,16,1408]{2,1,0:T(8,128)(2,1)S(1)}, u32[]{:S(2)}, u32[]{:S(2)}) async-start(bf16[32,16,1408]{2,1,0:T(8,128)(2,1)} %bitcast.41), calls=%async_computation.1 | async-start | bytes 2883584 | tf_op jit(solution)/shard_map/all_to_all | solution.py:611
  35.3 3.5 %collective-permute-start = (bf16[64,1024]{1,0:T(8,128)(2,1)S(1)}, bf16[64,1024]{1,0:T(8,128)(2,1)S(1)}, u32[]{:S(2)}, u32[]{:S(2)}) collective-permute-start(bf16[64,1024]{1,0:T(8,128)(2,1)S(1)} %bitcast.33), channel_id=1, source_target_pairs={{0,2},{1,3},{2,4},{3,5},{4,6},{5,7},{6,8},{7,9},{8,10},{9,11},{10,... | collective-permute-start | bytes 393224 | tf_op jit(solution)/shard_map/ppermute | solution.py:605
  38.8 3.8 %collective-permute-start.4 = (bf16[64,1024]{1,0:T(8,128)(2,1)S(1)}, bf16[64,1024]{1,0:T(8,128)(2,1)S(1)}, u32[]{:S(2)}, u32[]{:S(2)}) collective-permute-start(bf16[64,1024]{1,0:T(8,128)(2,1)S(1)} %bitcast.34), channel_id=1, source_target_pairs={{0,14},{1,15},{2,0},{3,1},{4,2},{5,3},{6,4},{7,5},{8,6},{9,7},{10,... | collective-permute-start | bytes 393224 | tf_op jit(solution)/shard_map/ppermute | solution.py:605
  43.6 2.0 collective-permute-start.1
  45.7 5.0 %collective-permute-start.5 = (bf16[64,1024]{1,0:T(8,128)(2,1)S(1)}, bf16[64,1024]{1,0:T(8,128)(2,1)S(1)}, u32[]{:S(2)}, u32[]{:S(2)}) collective-permute-start(bf16[64,1024]{1,0:T(8,128)(2,1)S(1)} %collective-permute-done.4.refs_7_), channel_id=1, source_target_pairs={{0,14},{1,15},{2,0},{3,1},{4,2},{5,3},{6,4},{7,5},{8,6},{9,7},{10,... | collective-permute-start | bytes 393224 | tf_op jit(solution)/shard_map/ppermute | solution.py:605
  51.7 1.9 collective-permute-start.2
  53.6 5.1 %collective-permute-start.6 = (bf16[64,1024]{1,0:T(8,128)(2,1)S(1)}, bf16[64,1024]{1,0:T(8,128)(2,1)S(1)}, u32[]{:S(2)}, u32[]{:S(2)}) collective-permute-start(bf16[64,1024]{1,0:T(8,128)(2,1)S(1)} %collective-permute-done.5.refs_6_), channel_id=1, source_target_pairs={{0,14},{1,15},{2,0},{3,1},{4,2},{5,3},{6,4},{7,5},{8,6},{9,7},{10,... | collective-permute-start | bytes 393224 | tf_op jit(solution)/shard_map/ppermute | solution.py:605
  59.8 1.9 collective-permute-start.3
  61.7 5.5 %all-gather.2.cloned.1.call-done = bf16[4096,128]{1,0:T(8,128)(2,1)} async-done(((bf16[512,128]{1,0:T(8,128)(2,1)}), bf16[4096,128]{1,0:T(8,128)(2,1)}) %all-gather.2.cloned.1.call-update) | async-done | bytes 1048592 | tf_op jit(solution)/shard_map/all_gather | solution.py:615
  68.4 1.9 collective-permute-start.7
  70.4 2.6 %collective-permute-done.7.other_ref = bf16[8,64,1024]{2,1,0:T(8,128)(2,1)S(1)} collective-permute-done((bf16[8,64,1024]{2,1,0:T(8,128)(2,1)S(1)}, bf16[8,64,1024]{2,1,0:T(8,128)(2,1)S(1)}, u32[]{:S(2)}, u32[]{:S(2)}) %collective-permute-start.7) | collective-permute-done | bytes 1048608 | tf_op jit(solution)/shard_map/ppermute | solution.py:608
  73.0 2.8 %dnormed.1 = (bf16[1024,512]{1,0:T(8,128)(2,1)}, bf16[4,256,1024]{2,1,0:T(8,128)(2,1)S(1)}) custom-call(s32[6]{0:T(128)S(1)} %copy-done.1, bf16[8,64,1024]{2,1,0:T(8,128)(2,1)S(1)} %collect.1.mine_ref, bf16[8,64,1024]{2,1,0:T(8,128)(2,1)S(1)} %collective-permute-done.7.other_ref, bf16[8,512,128]{2,1,0:T(8,128)(2,1)S(1)} %bitcast.38), custom_call_target="tpu_custom_call" | custom-call | flops 1200000000 | bytes 6291480 | tf_op jit(solution)/shard_map/dnormed/pallas_call | solution.py:56
  77.2 5.2 %all-to-all-start.2 = ((bf16[4,256,512]{2,1,0:T(8,128)(2,1)}), bf16[4,256,512]{2,1,0:T(8,128)(2,1)S(1)}, u32[]{:S(2)}, u32[]{:S(2)}) async-start(bf16[4,256,512]{2,1,0:T(8,128)(2,1)} %bitcast.14), calls=%async_computation.2 | async-start | bytes 2097152 | tf_op jit(solution)/shard_map/all_to_all | solution.py:611
  82.6 3.1 %forward.1 = (bf16[512,256]{1,0:T(8,128)(2,1)S(1)}, bf16[256,512]{1,0:T(8,128)(2,1)S(1)}, f32[256,512]{1,0:T(8,128)S(1)}, f32[256,512]{1,0:T(8,128)S(1)}, f32[4,...) custom-call(s32[1,6]{1,0:T(1,128)S(1)} %copy-done.7, ...), custom_call_target="tpu_custom_call" | custom-call | flops 4000000000 | bytes 5147696 | tf_op jit(solution)/shard_map/forward/pallas_call | solution.py:56
  92.3 4.0 %all-to-all-done.2 = bf16[4,256,512]{2,1,0:T(8,128)(2,1)S(1)} async-done(((bf16[4,256,512]{2,1,0:T(8,128)(2,1)}), bf16[4,256,512]{2,1,0:T(8,128)(2,1)S(1)}, u32[]{:S(2)}, u32[]{:S(2)}) %all-to-all-start.2) | async-done | bytes 1048608 | tf_op jit(solution)/shard_map/all_to_all | solution.py:611
  97.4 6.7 %all_to_all.81 = f32[4,16,256]{2,1,0:T(8,128)S(1)} all-to-all(f32[4,16,256]{2,1,0:T(8,128)S(1)} %bitcast.37), channel_id=1, replica_groups={{0,1,2,3},{4,5,6,7},{8,9,10,11},{12,13,14,15},{16,17,18,19},{20,21,22,2..., dimensions={0} | all-to-all | bytes 131072 | tf_op jit(solution)/shard_map/all_to_all | solution.py:611
  104.0 1.8 dz.1
  105.8 5.1 %all-to-all-start.4 = ((bf16[4,256,512]{2,1,0:T(8,128)(2,1)}), bf16[4,256,512]{2,1,0:T(8,128)(2,1)S(1)}, u32[]{:S(2)}, u32[]{:S(2)}) async-start(bf16[4,256,512]{2,1,0:T(8,128)(2,1)} %bitcast.18), calls=%async_computation.4 | async-start | bytes 2097152 | tf_op jit(solution)/shard_map/all_to_all | solution.py:611
  115.6 4.3 %backward.1 = (bf16[256,512]{1,0:T(8,128)(2,1)S(1)}, f32[4,512]{1,0:T(4,128)S(1)}, f32[256,128]{1,0:T(8,128)S(1)}, f32[3,128]{1,0:T(4,128)S(1)}, bf16[256,128]{1...) custom-call(s32[1,6]{1,0:T(1,128)S(1)} %copy-done.7, ...), custom_call_target="tpu_custom_call" | custom-call | flops 6000000000 | bytes 3305520 | tf_op jit(solution)/shard_map/backward/pallas_call | solution.py:56
  119.8 4.8 %all-to-all-done.4 = bf16[4,256,512]{2,1,0:T(8,128)(2,1)S(1)} async-done(((bf16[4,256,512]{2,1,0:T(8,128)(2,1)}), bf16[4,256,512]{2,1,0:T(8,128)(2,1)S(1)}, u32[]{:S(2)}, u32[]{:S(2)}) %all-to-all-start.4) | async-done | bytes 1048608 | tf_op jit(solution)/shard_map/all_to_all | solution.py:611
  124.6 1.6 copy-done.9
  126.2 2.3 %term.1 = bf16[4096,128]{1,0:T(8,128)(2,1)} custom-call(bf16[4,256,1024]{2,1,0:T(8,128)(2,1)S(1)} %copy-done.9, bf16[1024,512]{1,0:T(8,128)(2,1)S(1)} %bitcast.32), custom_call_target="tpu_custom_call" | custom-call | flops 1200000000 | bytes 4194304 | tf_op jit(solution)/shard_map/term/pallas_call | solution.py:56
  128.5 6.3 %all-to-all-start.5 = ((bf16[8,512,128]{2,1,0:T(8,128)(2,1)}), bf16[8,512,128]{2,1,0:T(8,128)(2,1)S(1)}, u32[]{:S(2)}, u32[]{:S(2)}) async-start(bf16[8,512,128]{2,1,0:T(8,128)(2,1)} %bitcast.20), calls=%async_computation.5 | async-start | bytes 2097152 | tf_op jit(solution)/shard_map/all_to_all | solution.py:611
  134.8 1.9 collective-permute-start.10
  136.7 2.2 %collective-permute-start.8 = (bf16[256,128]{1,0:T(8,128)(2,1)S(1)}, bf16[256,128]{1,0:T(8,128)(2,1)S(1)}, u32[]{:S(2)}, u32[]{:S(2)}) collective-permute-start(bf16[256,128]{1,0:T(8,128)(2,1)S(1)} %get-tuple-element.88), channel_id=1, source_target_pairs={{0,1},{1,0},{2,3},{3,2},{4,5},{5,4},{6,7},{7,6},{8,9},{9,8},{10,11... | collective-permute-start | bytes 196616 | tf_op jit(solution)/shard_map/ppermute | solution.py:608
  138.9 3.8 %collective-permute-start.9 = (bf16[256,128]{1,0:T(8,128)(2,1)S(1)}, bf16[256,128]{1,0:T(8,128)(2,1)S(1)}, u32[]{:S(2)}, u32[]{:S(2)}) collective-permute-start(bf16[256,128]{1,0:T(8,128)(2,1)S(1)} %get-tuple-element.89), channel_id=1, source_target_pairs={{0,2},{1,3},{2,0},{3,1},{4,6},{5,7},{6,4},{7,5},{8,10},{9,11},{10,... | collective-permute-start | bytes 196616 | tf_op jit(solution)/shard_map/ppermute | solution.py:608
  142.8 2.3 %collective-permute-done.9.refs_2_ = bf16[256,128]{1,0:T(8,128)(2,1)S(1)} collective-permute-done((bf16[256,128]{1,0:T(8,128)(2,1)S(1)}, bf16[256,128]{1,0:T(8,128)(2,1)S(1)}, u32[]{:S(2)}, u32[]{:S(2)}) %collective-permute-start.9) | collective-permute-done | bytes 65568 | tf_op jit(solution)/shard_map/ppermute | solution.py:608
  147.5 15.0 %all-to-all-done.5 = bf16[8,512,128]{2,1,0:T(8,128)(2,1)S(1)} async-done(((bf16[8,512,128]{2,1,0:T(8,128)(2,1)}), bf16[8,512,128]{2,1,0:T(8,128)(2,1)S(1)}, u32[]{:S(2)}, u32[]{:S(2)}) %all-to-all-start.5) | async-done | bytes 1048608 | tf_op jit(solution)/shard_map/all_to_all | solution.py:611
  162.5 5.2 %all-to-all-start.6 = ((bf16[32,16,1408]{2,1,0:T(8,128)(2,1)}), bf16[32,16,1408]{2,1,0:T(8,128)(2,1)S(1)}, u32[]{:S(2)}, u32[]{:S(2)}) async-start(bf16[32,16,1408]{2,1,0:T(8,128)(2,1)} %bitcast.30), calls=%async_computation.6 | async-start | bytes 2883584 | tf_op jit(solution)/shard_map/all_to_all | solution.py:611
  168.5 36.2 %all-to-all-done.6 = bf16[32,16,1408]{2,1,0:T(8,128)(2,1)S(1)} async-done(((bf16[32,16,1408]{2,1,0:T(8,128)(2,1)}), bf16[32,16,1408]{2,1,0:T(8,128)(2,1)S(1)}, u32[]{:S(2)}, u32[]{:S(2)}) %all-to-all-start.6) | async-done | bytes 1441824 | tf_op jit(solution)/shard_map/all_to_all | solution.py:611
  (93 shorter events, 26.8 us)
Async XLA Ops:
  7.2 60.0 %all-gather.2.cloned.1.call-start = ((), (), s32[]{:S(2)}) async-start(), calls=%async_computation.7 | async-start | bytes 1179648 | tf_op jit(solution)/shard_map/all_gather | solution.py:615
  27.0 40.8 %copy-start.1 = (s32[6]{0:T(128)S(1)}, s32[6]{0:T(128)}, u32[]{:S(2)}) copy-start(s32[6]{0:T(128)} %stack.27.refs_2_.co_ref) | copy-start | bytes 76
  27.0 50.2 %all-to-all-start.1 = ((bf16[32,16,1408]{2,1,0:T(8,128)(2,1)}), bf16[32,16,1408]{2,1,0:T(8,128)(2,1)S(1)}, u32[]{:S(2)}, u32[]{:S(2)}) async-start(bf16[32,16,1408]{2,1,0:T(8,128)(2,1)} %bitcast.41), calls=%async_computation.1 | async-start | bytes 2883584 | tf_op jit(solution)/shard_map/all_to_all | solution.py:611
  35.3 8.3 %collective-permute-start = (bf16[64,1024]{1,0:T(8,128)(2,1)S(1)}, bf16[64,1024]{1,0:T(8,128)(2,1)S(1)}, u32[]{:S(2)}, u32[]{:S(2)}) collective-permute-start(bf16[64,1024]{1,0:T(8,128)(2,1)S(1)} %bitcast.33), channel_id=1, source_target_pairs={{0,2},{1,3},{2,4},{3,5},{4,6},{5,7},{6,8},{7,9},{8,10},{9,11},{10,... | collective-permute-start | bytes 393224 | tf_op jit(solution)/shard_map/ppermute | solution.py:605
  38.8 6.9 %collective-permute-start.4 = (bf16[64,1024]{1,0:T(8,128)(2,1)S(1)}, bf16[64,1024]{1,0:T(8,128)(2,1)S(1)}, u32[]{:S(2)}, u32[]{:S(2)}) collective-permute-start(bf16[64,1024]{1,0:T(8,128)(2,1)S(1)} %bitcast.34), channel_id=1, source_target_pairs={{0,14},{1,15},{2,0},{3,1},{4,2},{5,3},{6,4},{7,5},{8,6},{9,7},{10,... | collective-permute-start | bytes 393224 | tf_op jit(solution)/shard_map/ppermute | solution.py:605
  43.6 8.1 %collective-permute-start.1 = (bf16[64,1024]{1,0:T(8,128)(2,1)S(1)}, bf16[64,1024]{1,0:T(8,128)(2,1)S(1)}, u32[]{:S(2)}, u32[]{:S(2)}) collective-permute-start(bf16[64,1024]{1,0:T(8,128)(2,1)S(1)} %collective-permute-done.refs_1_), channel_id=1, source_target_pairs={{0,2},{1,3},{2,4},{3,5},{4,6},{5,7},{6,8},{7,9},{8,10},{9,11},{10,... | collective-permute-start | bytes 393224 | tf_op jit(solution)/shard_map/ppermute | solution.py:605
  45.7 7.9 %collective-permute-start.5 = (bf16[64,1024]{1,0:T(8,128)(2,1)S(1)}, bf16[64,1024]{1,0:T(8,128)(2,1)S(1)}, u32[]{:S(2)}, u32[]{:S(2)}) collective-permute-start(bf16[64,1024]{1,0:T(8,128)(2,1)S(1)} %collective-permute-done.4.refs_7_), channel_id=1, source_target_pairs={{0,14},{1,15},{2,0},{3,1},{4,2},{5,3},{6,4},{7,5},{8,6},{9,7},{10,... | collective-permute-start | bytes 393224 | tf_op jit(solution)/shard_map/ppermute | solution.py:605
  51.7 8.1 %collective-permute-start.2 = (bf16[64,1024]{1,0:T(8,128)(2,1)S(1)}, bf16[64,1024]{1,0:T(8,128)(2,1)S(1)}, u32[]{:S(2)}, u32[]{:S(2)}) collective-permute-start(bf16[64,1024]{1,0:T(8,128)(2,1)S(1)} %collective-permute-done.1.refs_2_), channel_id=1, source_target_pairs={{0,2},{1,3},{2,4},{3,5},{4,6},{5,7},{6,8},{7,9},{8,10},{9,11},{10,... | collective-permute-start | bytes 393224 | tf_op jit(solution)/shard_map/ppermute | solution.py:605
  53.6 13.5 %collective-permute-start.6 = (bf16[64,1024]{1,0:T(8,128)(2,1)S(1)}, bf16[64,1024]{1,0:T(8,128)(2,1)S(1)}, u32[]{:S(2)}, u32[]{:S(2)}) collective-permute-start(bf16[64,1024]{1,0:T(8,128)(2,1)S(1)} %collective-permute-done.5.refs_6_), channel_id=1, source_target_pairs={{0,14},{1,15},{2,0},{3,1},{4,2},{5,3},{6,4},{7,5},{8,6},{9,7},{10,... | collective-permute-start | bytes 393224 | tf_op jit(solution)/shard_map/ppermute | solution.py:605
  59.8 8.1 %collective-permute-start.3 = (bf16[64,1024]{1,0:T(8,128)(2,1)S(1)}, bf16[64,1024]{1,0:T(8,128)(2,1)S(1)}, u32[]{:S(2)}, u32[]{:S(2)}) collective-permute-start(bf16[64,1024]{1,0:T(8,128)(2,1)S(1)} %collective-permute-done.2.refs_3_), channel_id=1, source_target_pairs={{0,2},{1,3},{2,4},{3,5},{4,6},{5,7},{6,8},{7,9},{8,10},{9,11},{10,... | collective-permute-start | bytes 393224 | tf_op jit(solution)/shard_map/ppermute | solution.py:605
  67.1 5.9 %copy-start.4 = (bf16[4096,128]{1,0:T(8,128)(2,1)S(1)}, bf16[4096,128]{1,0:T(8,128)(2,1)}, u32[]{:S(2)}) copy-start(bf16[4096,128]{1,0:T(8,128)(2,1)} %all-gather.2.cloned.1.call-done) | copy-start | bytes 3145732
  68.4 4.6 %collective-permute-start.7 = (bf16[8,64,1024]{2,1,0:T(8,128)(2,1)S(1)}, bf16[8,64,1024]{2,1,0:T(8,128)(2,1)S(1)}, u32[]{:S(2)}, u32[]{:S(2)}) collective-permute-start(bf16[8,64,1024]{2,1,0:T(8,128)(2,1)S(1)} %collect.1.mine_ref), channel_id=1, source_target_pairs={{0,1},{1,0},{2,3},{3,2},{4,5},{5,4},{6,7},{7,6},{8,9},{9,8},{10,11... | collective-permute-start | bytes 3145736 | tf_op jit(solution)/shard_map/ppermute | solution.py:608
  77.2 5.3 %copy-start.31 = (f32[8]{0:T(128)S(1)}, f32[8]{0:T(128)}, u32[]{:S(2)}) copy-start(f32[8]{0:T(128)} %param.26) | copy-start | bytes 100
  77.2 5.4 %copy-start.32 = (f32[8]{0:T(128)S(1)}, f32[8]{0:T(128)}, u32[]{:S(2)}) copy-start(f32[8]{0:T(128)} %param.25) | copy-start | bytes 100
  77.2 5.4 %copy-start.33 = (f32[8]{0:T(128)S(1)}, f32[8]{0:T(128)}, u32[]{:S(2)}) copy-start(f32[8]{0:T(128)} %param.24) | copy-start | bytes 100
  77.2 5.4 %copy-start.3 = (f32[4,1024]{1,0:T(4,128)S(1)}, f32[4,1024]{1,0:T(4,128)}, u32[]{:S(2)}) copy-start(f32[4,1024]{1,0:T(4,128)} %cbc_ref.1) | copy-start | bytes 49156
  77.2 5.4 %copy-start.5 = (f32[4,512]{1,0:T(4,128)S(1)}, f32[4,512]{1,0:T(4,128)}, u32[]{:S(2)}) copy-start(f32[4,512]{1,0:T(4,128)} %cx_ref.3) | copy-start | bytes 24580
  77.2 5.4 %copy-start.7 = (s32[1,6]{1,0:T(1,128)S(1)}, s32[1,6]{1,0:T(1,128)}, u32[]{:S(2)}) copy-start(s32[1,6]{1,0:T(1,128)} %len_ref.5) | copy-start | bytes 76
  77.2 19.2 %all-to-all-start.2 = ((bf16[4,256,512]{2,1,0:T(8,128)(2,1)}), bf16[4,256,512]{2,1,0:T(8,128)(2,1)S(1)}, u32[]{:S(2)}, u32[]{:S(2)}) async-start(bf16[4,256,512]{2,1,0:T(8,128)(2,1)} %bitcast.14), calls=%async_computation.2 | async-start | bytes 2097152 | tf_op jit(solution)/shard_map/all_to_all | solution.py:611
  82.6 13.8 %copy-start.6 = (f32[512]{0:T(512)S(1)}, f32[512]{0:T(512)}, u32[]{:S(2)}) copy-start(f32[512]{0:T(512)} %param.27) | copy-start | bytes 6148
  92.3 11.7 %copy-start.29 = (f32[256,128]{1,0:T(8,128)}, f32[256,128]{1,0:T(8,128)S(1)}, u32[]{:S(2)}) copy-start(f32[256,128]{1,0:T(8,128)S(1)} %get-tuple-element.75.cum_ref) | copy-start | bytes 393220
  96.4 7.6 %copy-start.11 = (f32[256,512]{1,0:T(8,128)S(1)}, f32[256,512]{1,0:T(8,128)}, u32[]{:S(2)}) copy-start(f32[256,512]{1,0:T(8,128)} %copy-done.10) | copy-start | bytes 1572868
  96.4 7.6 %copy-start.16 = (bf16[256,512]{1,0:T(8,128)(2,1)S(1)}, bf16[256,512]{1,0:T(8,128)(2,1)}, u32[]{:S(2)}) copy-start(bf16[256,512]{1,0:T(8,128)(2,1)} %copy-done.15) | copy-start | bytes 786436
  105.8 18.8 %all-to-all-start.4 = ((bf16[4,256,512]{2,1,0:T(8,128)(2,1)}), bf16[4,256,512]{2,1,0:T(8,128)(2,1)S(1)}, u32[]{:S(2)}, u32[]{:S(2)}) async-start(bf16[4,256,512]{2,1,0:T(8,128)(2,1)} %bitcast.18), calls=%async_computation.4 | async-start | bytes 2097152 | tf_op jit(solution)/shard_map/all_to_all | solution.py:611
  128.5 16.6 %copy-start.14 = (f32[4,256,128]{2,1,0:T(8,128)S(1)}, f32[4,256,128]{2,1,0:T(8,128)}, u32[]{:S(2)}) copy-start(f32[4,256,128]{2,1,0:T(8,128)} %copy-done.13) | copy-start | bytes 1572868
  128.5 16.6 %copy-start.18 = (bf16[512,256]{1,0:T(8,128)(2,1)S(1)}, bf16[512,256]{1,0:T(8,128)(2,1)}, u32[]{:S(2)}) copy-start(bf16[512,256]{1,0:T(8,128)(2,1)} %copy-done.17) | copy-start | bytes 786436
  128.5 34.0 %all-to-all-start.5 = ((bf16[8,512,128]{2,1,0:T(8,128)(2,1)}), bf16[8,512,128]{2,1,0:T(8,128)(2,1)S(1)}, u32[]{:S(2)}, u32[]{:S(2)}) async-start(bf16[8,512,128]{2,1,0:T(8,128)(2,1)} %bitcast.20), calls=%async_computation.5 | async-start | bytes 2097152 | tf_op jit(solution)/shard_map/all_to_all | solution.py:611
  134.8 8.0 %collective-permute-start.10 = (bf16[256,128]{1,0:T(8,128)(2,1)S(1)}, bf16[256,128]{1,0:T(8,128)(2,1)S(1)}, u32[]{:S(2)}, u32[]{:S(2)}) collective-permute-start(bf16[256,128]{1,0:T(8,128)(2,1)S(1)} %get-tuple-element.90), channel_id=1, source_target_pairs={{0,3},{1,2},{2,1},{3,0},{4,7},{5,6},{6,5},{7,4},{8,11},{9,10},{10,... | collective-permute-start | bytes 196616 | tf_op jit(solution)/shard_map/ppermute | solution.py:608
  136.7 6.1 %collective-permute-start.8 = (bf16[256,128]{1,0:T(8,128)(2,1)S(1)}, bf16[256,128]{1,0:T(8,128)(2,1)S(1)}, u32[]{:S(2)}, u32[]{:S(2)}) collective-permute-start(bf16[256,128]{1,0:T(8,128)(2,1)S(1)} %get-tuple-element.88), channel_id=1, source_target_pairs={{0,1},{1,0},{2,3},{3,2},{4,5},{5,4},{6,7},{7,6},{8,9},{9,8},{10,11... | collective-permute-start | bytes 196616 | tf_op jit(solution)/shard_map/ppermute | solution.py:608
  138.9 6.2 %collective-permute-start.9 = (bf16[256,128]{1,0:T(8,128)(2,1)S(1)}, bf16[256,128]{1,0:T(8,128)(2,1)S(1)}, u32[]{:S(2)}, u32[]{:S(2)}) collective-permute-start(bf16[256,128]{1,0:T(8,128)(2,1)S(1)} %get-tuple-element.89), channel_id=1, source_target_pairs={{0,2},{1,3},{2,0},{3,1},{4,6},{5,7},{6,4},{7,5},{8,10},{9,11},{10,... | collective-permute-start | bytes 196616 | tf_op jit(solution)/shard_map/ppermute | solution.py:608
  162.5 42.2 %copy-start.2 = (s32[16]{0:T(128)S(1)}, s32[16]{0:T(128)}, u32[]{:S(2)}) copy-start(s32[16]{0:T(128)} %bin_ref.1) | copy-start | bytes 196
  162.5 42.2 %all-to-all-start.6 = ((bf16[32,16,1408]{2,1,0:T(8,128)(2,1)}), bf16[32,16,1408]{2,1,0:T(8,128)(2,1)S(1)}, u32[]{:S(2)}, u32[]{:S(2)}) async-start(bf16[32,16,1408]{2,1,0:T(8,128)(2,1)} %bitcast.30), calls=%async_computation.6 | async-start | bytes 2883584 | tf_op jit(solution)/shard_map/all_to_all | solution.py:611
  (19 other events, 25.5 us)
Sparse Core Ops, SparseCore 0:
  10.1 56.9 all-gather.1

commit v5 on v4

--- a/solution.py
+++ b/solution.py
@@ -292,11 +292,12 @@
         p_ref[k * count : (k + 1) * count] = dot_nt(rows, w).astype(bf16)
 
 
-def term_body(scale, rows_ref, normed_ref, term_ref):
-    inner, count = rows_ref.shape[:2]
+def term_body(scale, co_ref, rows_ref, *refs):
+    inner = rows_ref.shape[0]
+    normed, term_ref = refs[:-1], refs[-1]
     total = None
     for k in range(inner):
-        part = dot_tn(normed_ref[k * count : (k + 1) * count], rows_ref[k])
+        part = dot_tn(normed[k][...], rows_ref[lax.rem(co_ref[4] + inner - k, inner)])
         total = part if total is None else total + part
     total = (total * scale).astype(bf16)
     channels = total.shape[0]
@@ -335,10 +336,11 @@
     mixed_ref,
     zb_ref,
     sums_ref,
+    pt_ref,
     normed_ref,
     dgain_ref,
     dy_ref,
-    dz_ref,
+    back_ref,
 ):
     squares, crossing = as_column(sums_ref)
     inverse = lax.rsqrt(squares / size + 1e-05)
@@ -348,17 +350,14 @@
     gated = gated_ref[...]
     dnormed = dnormed_ref[...]
     scaled = gated * inverse
-    normed = (scaled * gain).astype(bf16)
-    rows = gated.shape[0]
-    for k in range(normed_ref.shape[0] // rows):
-        normed_ref[k * rows : (k + 1) * rows] = normed
+    normed_ref[...] = (scaled * gain).astype(bf16)
     dgain_ref[...] = jnp.sum(dnormed * scaled, axis=0, keepdims=True)
     dgated = inverse * (dnormed * gain) - gated * factor
     z = zb_ref[...].astype(f32)
     sig = jax.nn.sigmoid(z)
     dy_ref[...] = dgated * (z * sig)
     dz = dgated * mixed_ref[...] * sig * (1.0 + z * (1.0 - sig))
-    dz_ref[...] = dz.astype(bf16)
+    back_ref[...] = dot_nn(pt_ref[...], dz.astype(bf16)).astype(bf16)
 
 
 def backward_body(
@@ -467,7 +466,6 @@
     share_ref,
     taps_ref,
     gx_ref,
-    dz_ref,
     ddt_ref,
     pt_ref,
     dcx_ref,
@@ -492,9 +490,8 @@
     meta = draw + pltpu.roll(ddt_ref[...], share, 1)
     place = pt_ref[...]
     back_ref[:, :channels] = dot_nn(place, gx_ref[...]).astype(bf16)
-    back_ref[:, channels : 2 * channels] = dot_nn(place, dz_ref[...]).astype(bf16)
-    last = 2 * channels + LANES
-    back_ref[:, 2 * channels : last] = dot_nn(place, meta.astype(bf16)).astype(bf16)
+    last = channels + LANES
+    back_ref[:, channels : last] = dot_nn(place, meta.astype(bf16)).astype(bf16)
     small_ref[...] = jnp.zeros_like(small_ref)
     small_ref[0:width] = dcx_ref[...]
     small_ref[width : width + 1] = dgain_ref[...]
@@ -509,13 +506,18 @@
         back_ref[k * PANEL : (k + 1) * PANEL, last:] = block
 
 
+def home_z_body(bin_ref, ret_ref, gz_ref):
+    for p in range(bin_ref.shape[0]):
+        at = pl.ds(pl.multiple_of(bin_ref[p] * PANEL, PANEL), PANEL)
+        gz_ref[p * PANEL : (p + 1) * PANEL] = ret_ref[at]
+
+
 def home_body(
     scale,
     heads,
     bin_ref,
     ret_ref,
     gx_ref,
-    gz_ref,
     gbc_ref,
     gdt_ref,
     dcx_ref,
@@ -526,13 +528,12 @@
     channels = gx_ref.shape[1]
     width = dcx_ref.shape[0]
     share = gbc_ref.shape[1]
-    last = 2 * channels + LANES
+    last = channels + LANES
     for p in range(bin_ref.shape[0]):
         rows = slice(p * PANEL, (p + 1) * PANEL)
         at = pl.ds(pl.multiple_of(bin_ref[p] * PANEL, PANEL), PANEL)
         gx_ref[rows] = ret_ref[at, :channels]
-        gz_ref[rows] = ret_ref[at, channels : 2 * channels]
-        meta = ret_ref[at, 2 * channels : last].astype(f32)
+        meta = ret_ref[at, channels:last].astype(f32)
         gbc_ref[rows] = meta[:, :share].astype(bf16)
         gdt_ref[rows] = pltpu.roll(meta, LANES - share, 1)[:, :heads].astype(bf16)
     total = None
@@ -600,6 +601,13 @@
         route = [(d, (d + shift * inner) % dp) for d in range(dp)]
         return lax.ppermute(block, "dp", route)
 
+    def along_x(block, shift):
+        route = []
+        for z in range(outer):
+            for x in range(inner):
+                route.append((z * inner + x, z * inner + (x + shift) % inner))
+        return lax.ppermute(block, "dp", route)
+
     def along_y(block, shift):
         route = [(t, (t + shift * CORES) % tensor) for t in range(tensor)]
         return lax.ppermute(block, "tensor", route)
@@ -708,19 +716,21 @@
         cost=500,
         name="cross",
     )
-    normed, dgain, dy, dz = call(
+    normed, dgain, dy, back_z = call(
         functools.partial(dz_body, size),
         [
-            shaped((inner * rows, channels), bf16),
+            shaped((rows, channels), bf16),
             shaped((1, channels), f32),
             shaped((rows, channels), f32),
-            shaped((rows, channels), bf16),
+            shaped((slots, channels), bf16),
         ],
-        [dnormed, gain_row, gated, mixed, zb, swap(sums, "tensor", in_group)],
+        [dnormed, gain_row, gated, mixed, zb, swap(sums, "tensor", in_group), place],
         cost=1000,
         name="dz",
     )
 
+    home_z = swap(back_z, "dp")
+    normed_all = [normed] + [along_x(normed, k) for k in range(1, inner)]
     gx, dcx, ddt, dheads, *pieces = call(
         functools.partial(backward_body, width, heads),
         [
@@ -753,25 +763,26 @@
         name="backward",
     )
 
-    normed_all, gx = lax.optimization_barrier((swap(normed, "dp", over_x), gx))
+    normed_all, gx = lax.optimization_barrier((normed_all, gx))
     (term,) = call(
         functools.partial(term_body, scale),
         [shaped((outer * channels, LANES), bf16)],
-        [out_rows, normed_all],
+        [coords, out_rows] + normed_all,
+        scalars=1,
         cost=1200,
         name="term",
     )
+    term, home_z = lax.optimization_barrier((term, home_z))
     terms = swap(term, "dp", over_z)
     (back,) = call(
         functools.partial(share_body, width),
-        [shaped((slots, 2 * channels + LANES + channels // 2), bf16)],
+        [shaped((slots, channels + LANES + channels // 2), bf16)],
         [
             lengths,
             coords,
             raw_share,
             share_taps,
             gx,
-            dz,
             ddt,
             place,
             dcx,
@@ -791,10 +802,16 @@
         gather_body, [shaped((channels, LANES), bf16)], [terms], name="gather"
     )
 
-    grad_x, grad_z, grad_bc, grad_dt, grad_cx, grad_cbc, grad_gain, grad_heads = call(
+    (grad_z,) = call(
+        home_z_body,
+        [shaped((rows, channels), bf16)],
+        [panel_bin, home_z],
+        scalars=1,
+        name="home_z",
+    )
+    grad_x, grad_bc, grad_dt, grad_cx, grad_cbc, grad_gain, grad_heads = call(
         functools.partial(home_body, scale, heads),
         [
-            shaped((rows, channels), bf16),
             shaped((rows, channels), bf16),
             shaped((rows, share), bf16),
             shaped((rows, heads), bf16),

time: 216 us -> 214 us (level)
  waiting for transfers between devices: 74.8 us -> 56.4 us
  starting transfers between devices: 63.2 us -> 76.6 us
  Pallas kernels: 22.6 us -> 25.5 us
    all_to_all x5, waiting for transfers between devices: 60 us -> 41.8 us  [swap(): lax.all_to_all(blocks, axis, split_axis=0, concat_axis=0, tiled=True, axi...]
    ppermute x0 -> x3, starting transfers between devices: none -> 11.2 us  [along_x(): return lax.ppermute(block, 'dp', route)]
    pallas_call x11 -> x12, Pallas kernels: 22.6 us -> 25.5 us  [call(): pl.pallas_call(moving if moves else body, out_shape=outs, in_specs=[smem]...]
    all_to_all x5, starting transfers between devices: 30.1 us -> 32.6 us  [swap(): lax.all_to_all(blocks, axis, split_axis=0, concat_axis=0, tiled=True, axi...]
    unnamed x71 -> x73, local copies, waits for them, and re-layouts: 18.1 us -> 18.9 us
  transfers between devices with their start and end apart: 17 -> 20, of which waited for: 11 -> 11; matrix products, arithmetic and copies ran while one was open for 1% -> 1% of each run, Pallas kernels for 8% -> 10%
where the time goes in v5:
time: 214 us; the launch traced here: 213 us
  starting transfers between devices  76.6 us (36%)
  waiting for transfers between devices  56.4 us (26%)
  Pallas kernels  25.5 us (12%)
  blocking collectives  20.5 us (10%)
  local copies, waits for them, and re-layouts  19.7 us (9%)
  between operations  14.4 us (7%)
    all_to_all x5, waiting for transfers between devices, swap(): lax.all_to_all(blocks, axis, split_axis=0, concat_axis=0, tiled=True, axi...  41.8 us
    all_to_all x5, starting transfers between devices, swap(): lax.all_to_all(blocks, axis, split_axis=0, concat_axis=0, tiled=True, axi...  32.6 us
    pallas_call x12, Pallas kernels, call(): pl.pallas_call(moving if moves else body, out_shape=outs, in_specs=[smem]...  25.5 us
    ppermute x7, starting transfers between devices, along_y(): return lax.ppermute(block, 'tensor', route)  23.3 us
    all_to_all x2, blocking collectives, swap(): lax.all_to_all(blocks, axis, split_axis=0, concat_axis=0, tiled=True, axi...  20.5 us
    unnamed x73, local copies, waits for them, and re-layouts  18.9 us
    ppermute x3, starting transfers between devices, along_x(): return lax.ppermute(block, 'dp', route)  11.2 us
    ppermute x4, starting transfers between devices, partner(): return lax.ppermute(block, 'tensor', [(t, t ^ flip) for t in range(tensor)])  9.49 us
  transfers between devices with their start and end apart: 20, of which 11 were waited for; matrix products, arithmetic and copies ran while one was open for 1% of the time, Pallas kernels for 10%

profile of v5, /device:TPU:2, one launch (start us, length us, event | category | flops | bytes accessed | tf_op | source)
XLA Modules:
  0.0 213.1 jit_solution(8999068612538567773)
XLA Ops:
  10.0 3.3 %pack.1 = (bf16[512,1408]{1,0:T(8,128)(2,1)}, bf16[64,1024]{1,0:T(8,128)(2,1)}) custom-call(s32[16]{0:T(128)} %bin_ref.3, s32[16]{0:T(128)} %refs_1_.1, s32[6]{0:T(128)} %stack.27.refs_2_.co_ref, bf16[256,512]{1,0:T(8,128)(2,1)} %refs_3_.1, bf16[256,512]{1,0:T(8,128)(2,1)} %refs_4_.1, bf16[256,1024]{1,0:T(8,128)(2,1)} %refs_5_.1, ...), custom_call_target="tpu_custom_call" | custom-call | flops 1000000 | bytes 2756760 | tf_op jit(solution)/shard_map/pack/pallas_call | solution.py:56
  13.3 13.7 %all_to_all.80 = bf16[4,16,1024]{2,1,0:T(8,128)(2,1)S(1)} all-to-all(bf16[4,16,1024]{2,1,0:T(8,128)(2,1)} %bitcast.41), channel_id=1, replica_groups={{0,16,32,48},{64,80,96,112},{128,144,160,176},{192,208,224,240},{256,27..., dimensions={0} | all-to-all | bytes 262144 | tf_op jit(solution)/shard_map/all_to_all | solution.py:619
  27.0 8.3 %all-to-all-start.1 = ((bf16[32,16,1408]{2,1,0:T(8,128)(2,1)}), bf16[32,16,1408]{2,1,0:T(8,128)(2,1)S(1)}, u32[]{:S(2)}, u32[]{:S(2)}) async-start(bf16[32,16,1408]{2,1,0:T(8,128)(2,1)} %bitcast.40), calls=%async_computation.1 | async-start | bytes 2883584 | tf_op jit(solution)/shard_map/all_to_all | solution.py:619
  35.3 3.5 %collective-permute-start = (bf16[64,1024]{1,0:T(8,128)(2,1)S(1)}, bf16[64,1024]{1,0:T(8,128)(2,1)S(1)}, u32[]{:S(2)}, u32[]{:S(2)}) collective-permute-start(bf16[64,1024]{1,0:T(8,128)(2,1)S(1)} %bitcast.32), channel_id=1, source_target_pairs={{0,2},{1,3},{2,4},{3,5},{4,6},{5,7},{6,8},{7,9},{8,10},{9,11},{10,... | collective-permute-start | bytes 393224 | tf_op jit(solution)/shard_map/ppermute | solution.py:613
  38.8 3.8 %collective-permute-start.4 = (bf16[64,1024]{1,0:T(8,128)(2,1)S(1)}, bf16[64,1024]{1,0:T(8,128)(2,1)S(1)}, u32[]{:S(2)}, u32[]{:S(2)}) collective-permute-start(bf16[64,1024]{1,0:T(8,128)(2,1)S(1)} %bitcast.33), channel_id=1, source_target_pairs={{0,14},{1,15},{2,0},{3,1},{4,2},{5,3},{6,4},{7,5},{8,6},{9,7},{10,... | collective-permute-start | bytes 393224 | tf_op jit(solution)/shard_map/ppermute | solution.py:613
  43.6 2.0 collective-permute-start.1
  45.7 5.0 %collective-permute-start.5 = (bf16[64,1024]{1,0:T(8,128)(2,1)S(1)}, bf16[64,1024]{1,0:T(8,128)(2,1)S(1)}, u32[]{:S(2)}, u32[]{:S(2)}) collective-permute-start(bf16[64,1024]{1,0:T(8,128)(2,1)S(1)} %collective-permute-done.4.refs_7_), channel_id=1, source_target_pairs={{0,14},{1,15},{2,0},{3,1},{4,2},{5,3},{6,4},{7,5},{8,6},{9,7},{10,... | collective-permute-start | bytes 393224 | tf_op jit(solution)/shard_map/ppermute | solution.py:613
  51.7 1.9 collective-permute-start.2
  53.6 5.1 %collective-permute-start.6 = (bf16[64,1024]{1,0:T(8,128)(2,1)S(1)}, bf16[64,1024]{1,0:T(8,128)(2,1)S(1)}, u32[]{:S(2)}, u32[]{:S(2)}) collective-permute-start(bf16[64,1024]{1,0:T(8,128)(2,1)S(1)} %collective-permute-done.5.refs_6_), channel_id=1, source_target_pairs={{0,14},{1,15},{2,0},{3,1},{4,2},{5,3},{6,4},{7,5},{8,6},{9,7},{10,... | collective-permute-start | bytes 393224 | tf_op jit(solution)/shard_map/ppermute | solution.py:613
  59.8 1.9 collective-permute-start.3
  61.7 4.8 %all-gather.2.cloned.1.call-done = bf16[4096,128]{1,0:T(8,128)(2,1)} async-done(((bf16[512,128]{1,0:T(8,128)(2,1)}), bf16[4096,128]{1,0:T(8,128)(2,1)}) %all-gather.2.cloned.1.call-update) | async-done | bytes 1048592 | tf_op jit(solution)/shard_map/all_gather | solution.py:623
  68.4 1.9 collective-permute-start.7
  70.4 2.6 %collective-permute-done.7.other_ref = bf16[8,64,1024]{2,1,0:T(8,128)(2,1)S(1)} collective-permute-done((bf16[8,64,1024]{2,1,0:T(8,128)(2,1)S(1)}, bf16[8,64,1024]{2,1,0:T(8,128)(2,1)S(1)}, u32[]{:S(2)}, u32[]{:S(2)}) %collective-permute-start.7) | collective-permute-done | bytes 1048608 | tf_op jit(solution)/shard_map/ppermute | solution.py:616
  73.0 2.8 %dnormed.1 = (bf16[1024,512]{1,0:T(8,128)(2,1)}, bf16[4,256,1024]{2,1,0:T(8,128)(2,1)S(1)}) custom-call(s32[6]{0:T(128)S(1)} %copy-done, bf16[8,64,1024]{2,1,0:T(8,128)(2,1)S(1)} %collect.1.mine_ref, bf16[8,64,1024]{2,1,0:T(8,128)(2,1)S(1)} %collective-permute-done.7.other_ref, bf16[8,512,128]{2,1,0:T(8,128)(2,1)S(1)} %bitcast.37), custom_call_target="tpu_custom_call" | custom-call | flops 1200000000 | bytes 6291480 | tf_op jit(solution)/shard_map/dnormed/pallas_call | solution.py:56
  77.2 5.2 %all-to-all-start.2 = ((bf16[4,256,512]{2,1,0:T(8,128)(2,1)}), bf16[4,256,512]{2,1,0:T(8,128)(2,1)S(1)}, u32[]{:S(2)}, u32[]{:S(2)}) async-start(bf16[4,256,512]{2,1,0:T(8,128)(2,1)} %bitcast.14), calls=%async_computation.2 | async-start | bytes 2097152 | tf_op jit(solution)/shard_map/all_to_all | solution.py:619
  82.6 3.2 %forward.1 = (bf16[512,256]{1,0:T(8,128)(2,1)S(1)}, bf16[256,512]{1,0:T(8,128)(2,1)S(1)}, f32[256,512]{1,0:T(8,128)S(1)}, f32[256,512]{1,0:T(8,128)S(1)}, f32[4,...) custom-call(s32[1,6]{1,0:T(1,128)S(1)} %copy-done.6, ...), custom_call_target="tpu_custom_call" | custom-call | flops 4000000000 | bytes 5147696 | tf_op jit(solution)/shard_map/forward/pallas_call | solution.py:56
  92.2 4.1 %all-to-all-done.2 = bf16[4,256,512]{2,1,0:T(8,128)(2,1)S(1)} async-done(((bf16[4,256,512]{2,1,0:T(8,128)(2,1)}), bf16[4,256,512]{2,1,0:T(8,128)(2,1)S(1)}, u32[]{:S(2)}, u32[]{:S(2)}) %all-to-all-start.2) | async-done | bytes 1048608 | tf_op jit(solution)/shard_map/all_to_all | solution.py:619
  97.3 6.7 %all_to_all.81 = f32[4,16,256]{2,1,0:T(8,128)S(1)} all-to-all(f32[4,16,256]{2,1,0:T(8,128)S(1)} %bitcast.36), channel_id=1, replica_groups={{0,1,2,3},{4,5,6,7},{8,9,10,11},{12,13,14,15},{16,17,18,19},{20,21,22,2..., dimensions={0} | all-to-all | bytes 131072 | tf_op jit(solution)/shard_map/all_to_all | solution.py:619
  106.8 8.4 %all-to-all-start.4 = ((bf16[32,16,512]{2,1,0:T(8,128)(2,1)}), bf16[32,16,512]{2,1,0:T(8,128)(2,1)S(1)}, u32[]{:S(2)}, u32[]{:S(2)}) async-start(bf16[32,16,512]{2,1,0:T(8,128)(2,1)} %bitcast.18), calls=%async_computation.4 | async-start | bytes 1048576 | tf_op jit(solution)/shard_map/all_to_all | solution.py:619
  115.2 2.1 %collective-permute-start.10 = (bf16[256,512]{1,0:T(8,128)(2,1)S(1)}, bf16[256,512]{1,0:T(8,128)(2,1)S(1)}, u32[]{:S(2)}, u32[]{:S(2)}) collective-permute-start(bf16[256,512]{1,0:T(8,128)(2,1)S(1)} %get-tuple-element.95.refs_0_), channel_id=1, source_target_pairs={{0,48},{16,0},{32,16},{48,32},{64,112},{80,64},{96,80},{112,96},{1... | collective-permute-start | bytes 786440 | tf_op jit(solution)/shard_map/ppermute | solution.py:609
  117.3 3.7 %collective-permute-start.8 = (bf16[256,512]{1,0:T(8,128)(2,1)S(1)}, bf16[256,512]{1,0:T(8,128)(2,1)S(1)}, u32[]{:S(2)}, u32[]{:S(2)}) collective-permute-start(bf16[256,512]{1,0:T(8,128)(2,1)S(1)} %get-tuple-element.95.refs_0_), channel_id=1, source_target_pairs={{0,16},{16,32},{32,48},{48,0},{64,80},{80,96},{96,112},{112,64},{1... | collective-permute-start | bytes 786440 | tf_op jit(solution)/shard_map/ppermute | solution.py:609
  121.0 5.4 %collective-permute-start.9 = (bf16[256,512]{1,0:T(8,128)(2,1)S(1)}, bf16[256,512]{1,0:T(8,128)(2,1)S(1)}, u32[]{:S(2)}, u32[]{:S(2)}) collective-permute-start(bf16[256,512]{1,0:T(8,128)(2,1)S(1)} %get-tuple-element.95.refs_0_), channel_id=1, source_target_pairs={{0,32},{16,48},{32,0},{48,16},{64,96},{80,112},{96,64},{112,80},{1... | collective-permute-start | bytes 786440 | tf_op jit(solution)/shard_map/ppermute | solution.py:609
  133.1 4.4 %backward.1 = (bf16[256,512]{1,0:T(8,128)(2,1)S(1)}, f32[4,512]{1,0:T(4,128)S(1)}, f32[256,128]{1,0:T(8,128)S(1)}, f32[3,128]{1,0:T(4,128)S(1)}, bf16[256,128]{1...) custom-call(s32[1,6]{1,0:T(1,128)S(1)} %copy-done.6, ...), custom_call_target="tpu_custom_call" | custom-call | flops 6000000000 | bytes 3305520 | tf_op jit(solution)/shard_map/backward/pallas_call | solution.py:56
  138.2 2.9 %term.1 = bf16[4096,128]{1,0:T(8,128)(2,1)} custom-call(s32[6]{0:T(128)S(1)} %copy-done, bf16[4,256,1024]{2,1,0:T(8,128)(2,1)S(1)} %copy-done.8, bf16[256,512]{1,0:T(8,128)(2,1)S(1)} %get-tuple-element.95.refs_0_, bf16[256,512]{1,0:T(8,128)(2,1)S(1)} %collective-permute-done.8.refs_1_, bf16[256,512]{1,0:T(8,128)(2,1)S(1)} %collective-permute-done.9.refs_2_, ...), custom_call_target="tpu_custom_call" | custom-call | flops 1200000000 | bytes 4194328 | tf_op jit(solution)/shard_map/term/pallas_call | solution.py:56
  141.1 6.8 %all-to-all-start.5 = ((bf16[8,512,128]{2,1,0:T(8,128)(2,1)}), bf16[8,512,128]{2,1,0:T(8,128)(2,1)S(1)}, u32[]{:S(2)}, u32[]{:S(2)}) async-start(bf16[8,512,128]{2,1,0:T(8,128)(2,1)} %bitcast.20), calls=%async_computation.5 | async-start | bytes 2097152 | tf_op jit(solution)/shard_map/all_to_all | solution.py:619
  147.9 1.9 collective-permute-start.11
  149.8 2.1 collective-permute-start.12
  151.9 3.6 %collective-permute-start.13 = (bf16[256,128]{1,0:T(8,128)(2,1)S(1)}, bf16[256,128]{1,0:T(8,128)(2,1)S(1)}, u32[]{:S(2)}, u32[]{:S(2)}) collective-permute-start(bf16[256,128]{1,0:T(8,128)(2,1)S(1)} %get-tuple-element.93), channel_id=1, source_target_pairs={{0,3},{1,2},{2,1},{3,0},{4,7},{5,6},{6,5},{7,4},{8,11},{9,10},{10,... | collective-permute-start | bytes 196616 | tf_op jit(solution)/shard_map/ppermute | solution.py:616
  157.7 2.1 share.1
  159.8 15.2 %all-to-all-done.5 = bf16[8,512,128]{2,1,0:T(8,128)(2,1)S(1)} async-done(((bf16[8,512,128]{2,1,0:T(8,128)(2,1)}), bf16[8,512,128]{2,1,0:T(8,128)(2,1)S(1)}, u32[]{:S(2)}, u32[]{:S(2)}) %all-to-all-start.5) | async-done | bytes 1048608 | tf_op jit(solution)/shard_map/all_to_all | solution.py:619
  175.0 3.9 %all-to-all-start.6 = ((bf16[32,16,896]{2,1,0:T(8,128)(2,1)}), bf16[32,16,896]{2,1,0:T(8,128)(2,1)S(1)}, u32[]{:S(2)}, u32[]{:S(2)}) async-start(bf16[32,16,896]{2,1,0:T(8,128)(2,1)} %bitcast.22), calls=%async_computation.6 | async-start | bytes 1835008 | tf_op jit(solution)/shard_map/all_to_all | solution.py:619
  181.0 22.5 %all-to-all-done.6 = bf16[32,16,896]{2,1,0:T(8,128)(2,1)S(1)} async-done(((bf16[32,16,896]{2,1,0:T(8,128)(2,1)}), bf16[32,16,896]{2,1,0:T(8,128)(2,1)S(1)}, u32[]{:S(2)}, u32[]{:S(2)}) %all-to-all-start.6) | async-done | bytes 917536 | tf_op jit(solution)/shard_map/all_to_all | solution.py:619
  (102 shorter events, 33.8 us)
Async XLA Ops:
  7.2 59.3 %all-gather.2.cloned.1.call-start = ((), (), s32[]{:S(2)}) async-start(), calls=%async_computation.7 | async-start | bytes 1179648 | tf_op jit(solution)/shard_map/all_gather | solution.py:623
  27.0 40.8 %copy-start = (s32[6]{0:T(128)S(1)}, s32[6]{0:T(128)}, u32[]{:S(2)}) copy-start(s32[6]{0:T(128)} %stack.27.refs_2_.co_ref) | copy-start | bytes 76
  27.0 50.2 %all-to-all-start.1 = ((bf16[32,16,1408]{2,1,0:T(8,128)(2,1)}), bf16[32,16,1408]{2,1,0:T(8,128)(2,1)S(1)}, u32[]{:S(2)}, u32[]{:S(2)}) async-start(bf16[32,16,1408]{2,1,0:T(8,128)(2,1)} %bitcast.40), calls=%async_computation.1 | async-start | bytes 2883584 | tf_op jit(solution)/shard_map/all_to_all | solution.py:619
  35.3 8.3 %collective-permute-start = (bf16[64,1024]{1,0:T(8,128)(2,1)S(1)}, bf16[64,1024]{1,0:T(8,128)(2,1)S(1)}, u32[]{:S(2)}, u32[]{:S(2)}) collective-permute-start(bf16[64,1024]{1,0:T(8,128)(2,1)S(1)} %bitcast.32), channel_id=1, source_target_pairs={{0,2},{1,3},{2,4},{3,5},{4,6},{5,7},{6,8},{7,9},{8,10},{9,11},{10,... | collective-permute-start | bytes 393224 | tf_op jit(solution)/shard_map/ppermute | solution.py:613
  38.8 6.9 %collective-permute-start.4 = (bf16[64,1024]{1,0:T(8,128)(2,1)S(1)}, bf16[64,1024]{1,0:T(8,128)(2,1)S(1)}, u32[]{:S(2)}, u32[]{:S(2)}) collective-permute-start(bf16[64,1024]{1,0:T(8,128)(2,1)S(1)} %bitcast.33), channel_id=1, source_target_pairs={{0,14},{1,15},{2,0},{3,1},{4,2},{5,3},{6,4},{7,5},{8,6},{9,7},{10,... | collective-permute-start | bytes 393224 | tf_op jit(solution)/shard_map/ppermute | solution.py:613
  43.6 8.1 %collective-permute-start.1 = (bf16[64,1024]{1,0:T(8,128)(2,1)S(1)}, bf16[64,1024]{1,0:T(8,128)(2,1)S(1)}, u32[]{:S(2)}, u32[]{:S(2)}) collective-permute-start(bf16[64,1024]{1,0:T(8,128)(2,1)S(1)} %collective-permute-done.refs_1_), channel_id=1, source_target_pairs={{0,2},{1,3},{2,4},{3,5},{4,6},{5,7},{6,8},{7,9},{8,10},{9,11},{10,... | collective-permute-start | bytes 393224 | tf_op jit(solution)/shard_map/ppermute | solution.py:613
  45.7 7.9 %collective-permute-start.5 = (bf16[64,1024]{1,0:T(8,128)(2,1)S(1)}, bf16[64,1024]{1,0:T(8,128)(2,1)S(1)}, u32[]{:S(2)}, u32[]{:S(2)}) collective-permute-start(bf16[64,1024]{1,0:T(8,128)(2,1)S(1)} %collective-permute-done.4.refs_7_), channel_id=1, source_target_pairs={{0,14},{1,15},{2,0},{3,1},{4,2},{5,3},{6,4},{7,5},{8,6},{9,7},{10,... | collective-permute-start | bytes 393224 | tf_op jit(solution)/shard_map/ppermute | solution.py:613
  51.7 8.1 %collective-permute-start.2 = (bf16[64,1024]{1,0:T(8,128)(2,1)S(1)}, bf16[64,1024]{1,0:T(8,128)(2,1)S(1)}, u32[]{:S(2)}, u32[]{:S(2)}) collective-permute-start(bf16[64,1024]{1,0:T(8,128)(2,1)S(1)} %collective-permute-done.1.refs_2_), channel_id=1, source_target_pairs={{0,2},{1,3},{2,4},{3,5},{4,6},{5,7},{6,8},{7,9},{8,10},{9,11},{10,... | collective-permute-start | bytes 393224 | tf_op jit(solution)/shard_map/ppermute | solution.py:613
  53.6 12.8 %collective-permute-start.6 = (bf16[64,1024]{1,0:T(8,128)(2,1)S(1)}, bf16[64,1024]{1,0:T(8,128)(2,1)S(1)}, u32[]{:S(2)}, u32[]{:S(2)}) collective-permute-start(bf16[64,1024]{1,0:T(8,128)(2,1)S(1)} %collective-permute-done.5.refs_6_), channel_id=1, source_target_pairs={{0,14},{1,15},{2,0},{3,1},{4,2},{5,3},{6,4},{7,5},{8,6},{9,7},{10,... | collective-permute-start | bytes 393224 | tf_op jit(solution)/shard_map/ppermute | solution.py:613
  59.8 8.1 %collective-permute-start.3 = (bf16[64,1024]{1,0:T(8,128)(2,1)S(1)}, bf16[64,1024]{1,0:T(8,128)(2,1)S(1)}, u32[]{:S(2)}, u32[]{:S(2)}) collective-permute-start(bf16[64,1024]{1,0:T(8,128)(2,1)S(1)} %collective-permute-done.2.refs_3_), channel_id=1, source_target_pairs={{0,2},{1,3},{2,4},{3,5},{4,6},{5,7},{6,8},{7,9},{8,10},{9,11},{10,... | collective-permute-start | bytes 393224 | tf_op jit(solution)/shard_map/ppermute | solution.py:613
  66.4 6.6 %copy-start.3 = (bf16[4096,128]{1,0:T(8,128)(2,1)S(1)}, bf16[4096,128]{1,0:T(8,128)(2,1)}, u32[]{:S(2)}) copy-start(bf16[4096,128]{1,0:T(8,128)(2,1)} %all-gather.2.cloned.1.call-done) | copy-start | bytes 3145732
  68.4 4.6 %collective-permute-start.7 = (bf16[8,64,1024]{2,1,0:T(8,128)(2,1)S(1)}, bf16[8,64,1024]{2,1,0:T(8,128)(2,1)S(1)}, u32[]{:S(2)}, u32[]{:S(2)}) collective-permute-start(bf16[8,64,1024]{2,1,0:T(8,128)(2,1)S(1)} %collect.1.mine_ref), channel_id=1, source_target_pairs={{0,1},{1,0},{2,3},{3,2},{4,5},{5,4},{6,7},{7,6},{8,9},{9,8},{10,11... | collective-permute-start | bytes 3145736 | tf_op jit(solution)/shard_map/ppermute | solution.py:616
  77.2 5.4 %copy-start.2 = (f32[4,1024]{1,0:T(4,128)S(1)}, f32[4,1024]{1,0:T(4,128)}, u32[]{:S(2)}) copy-start(f32[4,1024]{1,0:T(4,128)} %cbc_ref.1) | copy-start | bytes 49156
  77.2 5.4 %copy-start.4 = (f32[4,512]{1,0:T(4,128)S(1)}, f32[4,512]{1,0:T(4,128)}, u32[]{:S(2)}) copy-start(f32[4,512]{1,0:T(4,128)} %cx_ref.3) | copy-start | bytes 24580
  77.2 5.4 %copy-start.6 = (s32[1,6]{1,0:T(1,128)S(1)}, s32[1,6]{1,0:T(1,128)}, u32[]{:S(2)}) copy-start(s32[1,6]{1,0:T(1,128)} %len_ref.5) | copy-start | bytes 76
  77.2 19.1 %all-to-all-start.2 = ((bf16[4,256,512]{2,1,0:T(8,128)(2,1)}), bf16[4,256,512]{2,1,0:T(8,128)(2,1)S(1)}, u32[]{:S(2)}, u32[]{:S(2)}) async-start(bf16[4,256,512]{2,1,0:T(8,128)(2,1)} %bitcast.14), calls=%async_computation.2 | async-start | bytes 2097152 | tf_op jit(solution)/shard_map/all_to_all | solution.py:619
  82.6 13.8 %copy-start.5 = (f32[512]{0:T(512)S(1)}, f32[512]{0:T(512)}, u32[]{:S(2)}) copy-start(f32[512]{0:T(512)} %param.27) | copy-start | bytes 6148
  96.3 7.7 %copy-start.10 = (f32[256,512]{1,0:T(8,128)S(1)}, f32[256,512]{1,0:T(8,128)}, u32[]{:S(2)}) copy-start(f32[256,512]{1,0:T(8,128)} %copy-done.9) | copy-start | bytes 1572868
  96.3 7.7 %copy-start.15 = (bf16[256,512]{1,0:T(8,128)(2,1)S(1)}, bf16[256,512]{1,0:T(8,128)(2,1)}, u32[]{:S(2)}) copy-start(bf16[256,512]{1,0:T(8,128)(2,1)} %copy-done.14) | copy-start | bytes 786436
  104.0 22.4 %copy-start.11 = (f32[256,512]{1,0:T(8,128)S(1)}, f32[256,512]{1,0:T(8,128)}, u32[]{:S(2)}) copy-start(f32[256,512]{1,0:T(8,128)} %copy-done.9) | copy-start | bytes 1572868
  106.8 34.3 %all-to-all-start.4 = ((bf16[32,16,512]{2,1,0:T(8,128)(2,1)}), bf16[32,16,512]{2,1,0:T(8,128)(2,1)S(1)}, u32[]{:S(2)}, u32[]{:S(2)}) async-start(bf16[32,16,512]{2,1,0:T(8,128)(2,1)} %bitcast.18), calls=%async_computation.4 | async-start | bytes 1048576 | tf_op jit(solution)/shard_map/all_to_all | solution.py:619
  115.2 23.0 %collective-permute-start.10 = (bf16[256,512]{1,0:T(8,128)(2,1)S(1)}, bf16[256,512]{1,0:T(8,128)(2,1)S(1)}, u32[]{:S(2)}, u32[]{:S(2)}) collective-permute-start(bf16[256,512]{1,0:T(8,128)(2,1)S(1)} %get-tuple-element.95.refs_0_), channel_id=1, source_target_pairs={{0,48},{16,0},{32,16},{48,32},{64,112},{80,64},{96,80},{112,96},{1... | collective-permute-start | bytes 786440 | tf_op jit(solution)/shard_map/ppermute | solution.py:609
  117.3 20.9 %collective-permute-start.8 = (bf16[256,512]{1,0:T(8,128)(2,1)S(1)}, bf16[256,512]{1,0:T(8,128)(2,1)S(1)}, u32[]{:S(2)}, u32[]{:S(2)}) collective-permute-start(bf16[256,512]{1,0:T(8,128)(2,1)S(1)} %get-tuple-element.95.refs_0_), channel_id=1, source_target_pairs={{0,16},{16,32},{32,48},{48,0},{64,80},{80,96},{96,112},{112,64},{1... | collective-permute-start | bytes 786440 | tf_op jit(solution)/shard_map/ppermute | solution.py:609
  121.0 17.2 %collective-permute-start.9 = (bf16[256,512]{1,0:T(8,128)(2,1)S(1)}, bf16[256,512]{1,0:T(8,128)(2,1)S(1)}, u32[]{:S(2)}, u32[]{:S(2)}) collective-permute-start(bf16[256,512]{1,0:T(8,128)(2,1)S(1)} %get-tuple-element.95.refs_0_), channel_id=1, source_target_pairs={{0,32},{16,48},{32,0},{48,16},{64,96},{80,112},{96,64},{112,80},{1... | collective-permute-start | bytes 786440 | tf_op jit(solution)/shard_map/ppermute | solution.py:609
  141.1 16.6 %copy-start.17 = (f32[4,256,128]{2,1,0:T(8,128)S(1)}, f32[4,256,128]{2,1,0:T(8,128)}, u32[]{:S(2)}) copy-start(f32[4,256,128]{2,1,0:T(8,128)} %copy-done.16) | copy-start | bytes 1572868
  141.1 16.6 %copy-start.19 = (bf16[256,512]{1,0:T(8,128)(2,1)S(1)}, bf16[256,512]{1,0:T(8,128)(2,1)}, u32[]{:S(2)}) copy-start(bf16[256,512]{1,0:T(8,128)(2,1)} %copy-done.18) | copy-start | bytes 786436
  141.1 33.9 %all-to-all-start.5 = ((bf16[8,512,128]{2,1,0:T(8,128)(2,1)}), bf16[8,512,128]{2,1,0:T(8,128)(2,1)S(1)}, u32[]{:S(2)}, u32[]{:S(2)}) async-start(bf16[8,512,128]{2,1,0:T(8,128)(2,1)} %bitcast.20), calls=%async_computation.5 | async-start | bytes 2097152 | tf_op jit(solution)/shard_map/all_to_all | solution.py:619
  147.9 7.7 %collective-permute-start.11 = (bf16[256,128]{1,0:T(8,128)(2,1)S(1)}, bf16[256,128]{1,0:T(8,128)(2,1)S(1)}, u32[]{:S(2)}, u32[]{:S(2)}) collective-permute-start(bf16[256,128]{1,0:T(8,128)(2,1)S(1)} %get-tuple-element.91), channel_id=1, source_target_pairs={{0,1},{1,0},{2,3},{3,2},{4,5},{5,4},{6,7},{7,6},{8,9},{9,8},{10,11... | collective-permute-start | bytes 196616 | tf_op jit(solution)/shard_map/ppermute | solution.py:616
  149.8 6.4 %collective-permute-start.12 = (bf16[256,128]{1,0:T(8,128)(2,1)S(1)}, bf16[256,128]{1,0:T(8,128)(2,1)S(1)}, u32[]{:S(2)}, u32[]{:S(2)}) collective-permute-start(bf16[256,128]{1,0:T(8,128)(2,1)S(1)} %get-tuple-element.92), channel_id=1, source_target_pairs={{0,2},{1,3},{2,0},{3,1},{4,6},{5,7},{6,4},{7,5},{8,10},{9,11},{10,... | collective-permute-start | bytes 196616 | tf_op jit(solution)/shard_map/ppermute | solution.py:616
  151.9 5.8 %collective-permute-start.13 = (bf16[256,128]{1,0:T(8,128)(2,1)S(1)}, bf16[256,128]{1,0:T(8,128)(2,1)S(1)}, u32[]{:S(2)}, u32[]{:S(2)}) collective-permute-start(bf16[256,128]{1,0:T(8,128)(2,1)S(1)} %get-tuple-element.93), channel_id=1, source_target_pairs={{0,3},{1,2},{2,1},{3,0},{4,7},{5,6},{6,5},{7,4},{8,11},{9,10},{10,... | collective-permute-start | bytes 196616 | tf_op jit(solution)/shard_map/ppermute | solution.py:616
  159.8 19.1 %copy-start.1 = (s32[16]{0:T(128)S(1)}, s32[16]{0:T(128)}, u32[]{:S(2)}) copy-start(s32[16]{0:T(128)} %bin_ref.3) | copy-start | bytes 196
  175.0 28.5 %all-to-all-start.6 = ((bf16[32,16,896]{2,1,0:T(8,128)(2,1)}), bf16[32,16,896]{2,1,0:T(8,128)(2,1)S(1)}, u32[]{:S(2)}, u32[]{:S(2)}) async-start(bf16[32,16,896]{2,1,0:T(8,128)(2,1)} %bitcast.22), calls=%async_computation.6 | async-start | bytes 1835008 | tf_op jit(solution)/shard_map/all_to_all | solution.py:619
  (23 other events, 37.0 us)
Sparse Core Ops, SparseCore 0:
  10.1 56.3 all-gather.1
